TPU v7x, 32 devices: a whole 2x2x4 slice. The times are simulated.
32 devices in a mesh: chan: 4 (over x, core), row: 8 (over z, y).
Axes of the slice: x: 2, y: 2, z: 4, core: 2. Of those that a mesh axis runs over, the one named last changes fastest.
Arguments:
- samples: bfloat16 [8, 128, 65536], P(None, 'chan', 'row'), may hold values from -6 to 6
- history: bfloat16 [8, 128, 7168], P(None, 'chan'), may hold values from -6 to 6
- antenna_flags: int32 [1024], replicated, may hold values 0 or 1
- beam_delays: int32 [256, 1024], replicated, may hold values from 0 to 1023
Outputs:
- visibilities: bfloat16 [512, 2, 1024, 1024], P('chan', None, 'row')
- beam_series: float32 [256, 64, 1024], P(('chan', 'row'))
All inputs are finite; a program needn't handle non-finite values.
Results may differ from a plain program's by a relative error of at most 0.0075.
Values may be sent and summed in bfloat16 or wider, within the bound.
No kernel may reach another device: no remote copies, remote signals or barrier semaphores. Data moves between devices by JAX's collectives and lax.ppermute only.
A program may use at most 320 MiB of HBM per device.

v0:
```python
import math

import jax
import jax.numpy as jnp
from jax import lax
from jax.sharding import PartitionSpec as P

A = 1024
FOURIER_LENGTH = 1024
NCH = 512
FILTER_TAPS = 8
BEAMS = 256


def from_behind(block, axis, distance):
    devices = range(lax.axis_size(axis))
    route = [(i - distance, i) for i in devices if i - distance in devices]
    return lax.ppermute(block, axis, route)


def tap_table():
    position = jnp.arange(FILTER_TAPS * FOURIER_LENGTH, dtype=jnp.int32).astype(jnp.float32) + 0.5
    centred = position / FOURIER_LENGTH - FILTER_TAPS / 2.0
    window = 0.5 - 0.5 * jnp.cos(2.0 * math.pi * position / (FILTER_TAPS * FOURIER_LENGTH))
    return (jnp.sinc(centred) * window).reshape(FILTER_TAPS, FOURIER_LENGTH)


def dft_table():
    sample_ids = jnp.arange(FOURIER_LENGTH, dtype=jnp.int32)
    chan_ids = jnp.arange(NCH, dtype=jnp.int32)
    phase_angle = (sample_ids[:, None] * chan_ids[None, :] % FOURIER_LENGTH).astype(jnp.float32) * (
        2.0 * math.pi / FOURIER_LENGTH
    )
    scale = 1.0 / math.sqrt(FOURIER_LENGTH)
    return jnp.stack([jnp.cos(phase_angle) * scale, -jnp.sin(phase_angle) * scale], axis=1).astype(
        jnp.bfloat16
    )


def synth_table():
    chan_ids = jnp.arange(NCH, dtype=jnp.int32)
    sample_ids = jnp.arange(FOURIER_LENGTH, dtype=jnp.int32)
    phase_angle = (chan_ids[:, None] * sample_ids[None, :] % FOURIER_LENGTH).astype(jnp.float32) * (
        2.0 * math.pi / FOURIER_LENGTH
    )
    scale = 1.0 / math.sqrt(NCH)
    return jnp.stack([jnp.cos(phase_angle) * scale, -jnp.sin(phase_angle) * scale], axis=0).astype(
        jnp.bfloat16
    )


def steering(delay_rows, chan_ids):
    delay_index = delay_rows[None, :, :] * chan_ids[:, None, None] % FOURIER_LENGTH
    phase_angle = delay_index.astype(jnp.float32) * (2.0 * math.pi / FOURIER_LENGTH)
    scale = 1.0 / math.sqrt(A)
    return (
        (jnp.cos(phase_angle) * scale).astype(jnp.bfloat16),
        (-jnp.sin(phase_angle) * scale).astype(jnp.bfloat16),
    )


def beam_terms(delay_rows, spectra, chan_ids, frames):
    w_real, w_imag = steering(delay_rows, chan_ids)
    x_real = spectra[:, :, :frames]
    x_imag = spectra[:, :, frames:]
    beam_real = jnp.einsum(
        "cba,caf->bcf", w_real, x_real, preferred_element_type=jnp.float32
    ) - jnp.einsum("cba,caf->bcf", w_imag, x_imag, preferred_element_type=jnp.float32)
    beam_imag = jnp.einsum(
        "cba,caf->bcf", w_real, x_imag, preferred_element_type=jnp.float32
    ) + jnp.einsum("cba,caf->bcf", w_imag, x_real, preferred_element_type=jnp.float32)
    return jnp.stack([beam_real, beam_imag], axis=1)


def gram_block(own_rows, swapped, all_columns, frames):
    real_part = jnp.einsum(
        "cam,cbm->cab", own_rows, all_columns, preferred_element_type=jnp.float32
    )
    imag_part = jnp.einsum("cam,cbm->cab", swapped, all_columns, preferred_element_type=jnp.float32)
    return (jnp.stack([real_part, imag_part], axis=1) / frames).astype(jnp.bfloat16)


def body(samples, history, antenna_flags, beam_delays):
    channel_number = lax.axis_size("chan")
    n_row = lax.axis_size("row")
    chan_id = lax.axis_index("chan")
    row_id = lax.axis_index("row")
    block_list, antennas_per_shard, shard_length = samples.shape
    frames_per_shard = shard_length // FOURIER_LENGTH
    frames = frames_per_shard * n_row
    channel_total = NCH // channel_number
    row_count = A // n_row
    beam_count = BEAMS // (channel_number * n_row)
    chan_ids = chan_id * channel_total + jnp.arange(channel_total, dtype=jnp.int32)
    tail = samples[:, :, shard_length - (FILTER_TAPS - 1) * FOURIER_LENGTH :]
    before = from_behind(tail, "row", 1)
    before = jnp.where(row_id == 0, history, before)
    extended = jnp.concatenate([before, samples], axis=2).reshape(
        block_list, antennas_per_shard, frames_per_shard + FILTER_TAPS - 1, FOURIER_LENGTH
    )
    tap_weights = tap_table()
    filter_output = jnp.zeros(
        (block_list, antennas_per_shard, frames_per_shard, FOURIER_LENGTH), jnp.float32
    )
    for tap in range(FILTER_TAPS):
        filter_output = (
            filter_output
            + extended[:, :, tap : tap + frames_per_shard, :].astype(jnp.float32) * tap_weights[tap]
        )
    filter_output = filter_output.astype(jnp.bfloat16)
    spectra = jnp.dot(
        filter_output.reshape(block_list * antennas_per_shard * frames_per_shard, FOURIER_LENGTH),
        dft_table().reshape(FOURIER_LENGTH, 2 * NCH),
        preferred_element_type=jnp.float32,
    )
    spectra = spectra.astype(jnp.bfloat16).reshape(
        block_list, antennas_per_shard, frames_per_shard, 2, channel_number, channel_total
    )
    departing_blocks = spectra.transpose(4, 0, 5, 1, 3, 2)
    received_blocks = lax.all_to_all(
        departing_blocks.reshape(
            channel_number * block_list, channel_total, antennas_per_shard, 2, frames_per_shard
        ),
        ("chan", "row"),
        split_axis=0,
        concat_axis=0,
        tiled=True,
    )
    received_blocks = received_blocks.reshape(
        channel_number, block_list, channel_total, antennas_per_shard, 2, frames_per_shard
    )
    own_rows = received_blocks.transpose(2, 0, 3, 4, 1, 5).reshape(
        channel_total, row_count, 2 * frames
    )
    row_flags = lax.dynamic_slice_in_dim(antenna_flags, row_id * row_count, row_count)
    own_rows = own_rows * row_flags.astype(jnp.bfloat16)[None, :, None]
    swapped = jnp.concatenate([own_rows[:, :, frames:], -own_rows[:, :, :frames]], axis=2)
    visibilities = gram_block(
        own_rows, swapped, lax.all_gather(own_rows, "row", axis=1, tiled=True), frames
    )
    row_delays = lax.dynamic_slice_in_dim(beam_delays, row_id * row_count, row_count, 1)
    partial_value = beam_terms(row_delays, own_rows, chan_ids, frames)
    arrived_beams = lax.all_to_all(
        partial_value, ("chan", "row"), split_axis=0, concat_axis=2, tiled=True
    )
    beam_spectra = arrived_beams.reshape(
        beam_count, 2, channel_number, n_row, channel_total, frames
    )
    beam_spectra = jnp.sum(beam_spectra, axis=3).reshape(beam_count, 2, NCH, frames)
    beam_spectra = beam_spectra.astype(jnp.bfloat16)
    beam_series = jnp.einsum(
        "bekf,ekn->bfn", beam_spectra, synth_table(), preferred_element_type=jnp.float32
    )
    return (visibilities, beam_series)


def solution(mesh):
    in_specs = (P(None, "chan", "row"), P(None, "chan", None), P(), P())
    out_specs = (P("chan", None, "row", None), P(("chan", "row"), None, None))
    return jax.shard_map(body, mesh=mesh, in_specs=in_specs, out_specs=out_specs, check_vma=False)
```

profile of v0, /device:TPU:0, one launch (start us, length us, event | category | flops | bytes accessed | tf_op | source)
XLA Modules:
  0.0 1294.5 jit_solution(1672229826883309400)
XLA Ops:
  7.2 4.2 slice.67
  11.4 6.7 collective-permute-start
  18.2 8.6 multiply_convert_fusion.12
  27.0 68.1 %collective-permute-done = bf16[8,32,7168]{2,1,0:T(8,128)(2,1)} collective-permute-done((bf16[8,32,7168]{2,1,0:T(8,128)(2,1)}, bf16[8,32,7168]{2,1,0:T(8,128)(2,1)}, u32[]{:S(2)}, u32[]{:S(2)}) %collective-permute-start) | collective-permute-done | bytes 3670048 | tf_op jit(solution)/shard_map/ppermute | solution.py:18
  95.1 2.2 broadcast_select_fusion
  97.4 6.9 pad_maximum_fusion.1
  104.2 12.6 reshape.220
  116.8 25.0 %add_convert_fusion = bf16[8,32,8,1024]{3,2,1,0:T(8,128)(2,1)S(1)} fusion(bf16[8,32,15,1024]{3,2,1,0:T(8,128)(2,1)} %reshape.220, f32[1024]{0:T(1024)S(1)} %get-tuple-element.21, f32[1024]{0:T(1024)S(1)} %get-tuple-element.22, f32[1024]{0:T(1024)S(1)} %get-tuple-element.23, f32[1024]{0:T(1024)S(1)} %get-tuple-element.24, f32[1024]{0:T(1024)S(1)} %get-tuple-element.25, ...), kind=kLoop, calls=%fused_computation.21 | loop fusion | flops 50331648 | bytes 37781504 | tf_op jit(solution)/shard_map/convert_element_type | solution.py:110
  141.8 5.0 convolution_convert_fusion
  146.8 3.2 copy.75
  150.0 9.0 all-to-all-start
  159.3 0.8 dynamic-slice_convert_fusion
  160.0 94.9 %all-to-all-done = bf16[32,128,32,2,8]{1,4,3,2,0:T(8,128)(2,1)} async-done(((bf16[32,128,32,2,8]{1,4,3,2,0:T(8,128)(2,1)}), bf16[32,128,32,2,8]{1,4,3,2,0:T(8,128)(2,1)}, u32[]{:S(2)}, u32[]{:S(2)}) %all-to-all-start) | async-done | bytes 4194336 | tf_op jit(solution)/shard_map/all_to_all | solution.py:120
  254.9 5.4 copy.76
  260.3 6.6 copy.77
  267.0 4.5 broadcast_multiply_fusion
  271.5 64.4 %fusion.4 = f32[128,64,256]{2,1,0:T(8,128)S(1)} fusion(s32[128]{0:T(128)S(1)} %iota_add_fusion, s32[256,128]{1,0:T(8,128)S(1)} %constant_dynamic-slice_fusion, bf16[128,128,128]{2,1,0:T(8,128)(2,1)} %broadcast_multiply_fusion), kind=kOutput, calls=%fused_computation.17 | convolution fusion | flops 603979776 | bytes 12714496 | tf_op jit(solution)/shard_map/cba,caf->bcf/dot_general | solution.py:69
  336.0 73.6 %fusion.5 = f32[128,64,256]{2,1,0:T(8,128)S(1)} fusion(s32[128]{0:T(128)S(1)} %iota_add_fusion, s32[256,128]{1,0:T(8,128)S(1)} %constant_dynamic-slice_fusion, bf16[128,128,128]{2,1,0:T(8,128)(2,1)S(1)} %copy-done.2), kind=kOutput, calls=%fused_computation.18 | convolution fusion | flops 603979776 | bytes 12714496 | tf_op jit(solution)/shard_map/cba,caf->bcf/dot_general | solution.py:66
  409.6 63.3 %add_bitcast_fusion = f32[256,1,128,64]{0,3,2,1:T(8,128)S(1)} fusion(f32[128,64,256]{2,1,0:T(8,128)S(1)} %fusion.4, s32[128]{0:T(128)S(1)} %iota_add_fusion, s32[256,128]{1,0:T(8,128)S(1)} %constant_dynamic-slice_fusion, bf16[128,128,128]{2,1,0:T(8,128)(2,1)S(1)} %copy-done.2), kind=kOutput, calls=%fused_computation.15 | convolution fusion | flops 610271232 | bytes 21103104 | tf_op jit(solution)/shard_map/cba,caf->bcf/dot_general | solution.py:71
  473.0 63.7 %subtract_bitcast_fusion = f32[256,1,128,64]{0,3,2,1:T(8,128)S(1)} fusion(f32[128,64,256]{2,1,0:T(8,128)S(1)} %fusion.5, s32[128]{0:T(128)S(1)} %iota_add_fusion, s32[256,128]{1,0:T(8,128)S(1)} %constant_dynamic-slice_fusion, bf16[128,128,128]{2,1,0:T(8,128)(2,1)S(1)} %copy-done.2), kind=kOutput, calls=%fused_computation.16 | convolution fusion | flops 610271232 | bytes 21103104 | tf_op jit(solution)/shard_map/cba,caf->bcf/dot_general | solution.py:68
  536.7 6.2 pad_maximum_fusion
  542.9 16.8 %copy.82 = f32[256,2,128,64]{2,3,1,0:T(8,128)} copy(f32[256,2,128,64]{0,3,2,1:T(8,128)} %pad_maximum_fusion) | data formatting | bytes 33554432 | tf_op jit(solution)/shard_map/stack | solution.py:72
  559.7 3.9 all-to-all-start.1
  563.7 8.6 multiply_convert_fusion.10
  572.2 7.3 fusion.70
  579.5 515.8 %all-to-all-done.1 = f32[256,2,128,64]{2,3,1,0:T(8,128)} async-done(((f32[256,2,128,64]{2,3,1,0:T(8,128)}), f32[256,2,128,64]{2,3,1,0:T(8,128)}, u32[]{:S(2)}, u32[]{:S(2)}) %all-to-all-start.1) | async-done | bytes 16777248 | tf_op jit(solution)/shard_map/all_to_all | solution.py:143
  1095.4 7.9 reduce_sum.9
  1103.3 2.6 fusion.30
  1105.9 36.2 %convolution_bitcast_fusion.1 = f32[128,1,128,1024]{3,2,0,1:T(8,128)} fusion(bf16[128,128,128]{2,1,0:T(8,128)(2,1)} %broadcast_multiply_fusion, bf16[128,1024,128]{2,1,0:T(8,128)(2,1)} %all-gather.2.cloned.1.call-done), kind=kOutput, calls=%fused_computation.6 | convolution fusion | flops 4294967296 | bytes 104857600 | tf_op jit(solution)/shard_map/cam,cbm->cab/dot_general | solution.py:76
  1142.1 37.7 %convolution_bitcast_fusion = f32[128,1,128,1024]{3,2,0,1:T(8,128)} fusion(bf16[128,1024,128]{2,1,0:T(8,128)(2,1)} %all-gather.2.cloned.1.call-done, bf16[128,128,64]{2,1,0:T(8,128)(2,1)} %get-tuple-element.19, bf16[128,128,64]{2,1,0:T(8,128)(2,1)} %get-tuple-element.18), kind=kOutput, calls=%fused_computation.5 | convolution fusion | flops 4303355904 | bytes 104857600 | tf_op jit(solution)/shard_map/cam,cbm->cab/dot_general | solution.py:79
  1179.8 64.1 %fusion = bf16[128,2,128,1024]{3,2,0,1:T(8,128)(2,1)} fusion(f32[128,1,128,1024]{3,2,0,1:T(8,128)} %convolution_bitcast_fusion, f32[128,1,128,1024]{3,2,0,1:T(8,128)} %convolution_bitcast_fusion.1), kind=kLoop, calls=%fused_computation.1 | loop fusion | flops 100663296 | bytes 201326592 | tf_op jit(solution)/shard_map/convert_element_type | solution.py:80
  1243.9 43.5 %copy.84 = bf16[128,2,128,1024]{3,2,1,0:T(8,128)(2,1)} copy(bf16[128,2,128,1024]{3,2,0,1:T(8,128)(2,1)} %fusion) | data formatting | bytes 134217728
  (16 shorter events, 0.7 us)
Async XLA Ops:
  7.2 264.3 %copy-start = (s32[256,1024]{1,0:T(8,128)S(1)}, s32[256,1024]{1,0:T(8,128)}, u32[]{:S(2)}) copy-start(s32[256,1024]{1,0:T(8,128)} %param.7) | copy-start | bytes 3145732
  11.4 83.8 %collective-permute-start = (bf16[8,32,7168]{2,1,0:T(8,128)(2,1)}, bf16[8,32,7168]{2,1,0:T(8,128)(2,1)}, u32[]{:S(2)}, u32[]{:S(2)}) collective-permute-start(bf16[8,32,7168]{2,1,0:T(8,128)(2,1)} %slice.67), channel_id=1, source_target_pairs={{0,1},{1,2},{2,3},{3,4},{4,5},{5,6},{6,7},{8,9},{9,10},{10,11},{11... | collective-permute-start | bytes 11010056 | tf_op jit(solution)/shard_map/ppermute | solution.py:18
  18.1 77.1 %copy-start.3 = (bf16[8,32,7168]{2,1,0:T(8,128)(2,1)S(1)}, bf16[8,32,7168]{2,1,0:T(8,128)(2,1)}, u32[]{:S(2)}) copy-start(bf16[8,32,7168]{2,1,0:T(8,128)(2,1)} %param.5) | copy-start | bytes 11010052
  150.0 105.0 %all-to-all-start = ((bf16[32,128,32,2,8]{1,4,3,2,0:T(8,128)(2,1)}), bf16[32,128,32,2,8]{1,4,3,2,0:T(8,128)(2,1)}, u32[]{:S(2)}, u32[]{:S(2)}) async-start(bf16[32,128,32,2,8]{1,4,3,2,0:T(8,128)(2,1)} %bitcast.53), calls=%async_computation | async-start | bytes 8388608 | tf_op jit(solution)/shard_map/all_to_all | solution.py:120
  159.0 946.9 %all-gather.2.cloned.1.call-start = ((), (), s32[]{:S(2)}) async-start(), calls=%async_computation.2 | async-start | bytes 37748736 | tf_op jit(solution)/shard_map/all_gather | solution.py:139
  271.5 64.5 %copy-start.2 = (bf16[128,128,128]{2,1,0:T(8,128)(2,1)S(1)}, bf16[128,128,128]{2,1,0:T(8,128)(2,1)}, u32[]{:S(2)}) copy-start(bf16[128,128,128]{2,1,0:T(8,128)(2,1)} %broadcast_multiply_fusion) | copy-start | bytes 12582916
  559.7 535.6 %all-to-all-start.1 = ((f32[256,2,128,64]{2,3,1,0:T(8,128)}), f32[256,2,128,64]{2,3,1,0:T(8,128)}, u32[]{:S(2)}, u32[]{:S(2)}) async-start(f32[256,2,128,64]{2,3,1,0:T(8,128)} %copy.82), calls=%async_computation.1 | async-start | bytes 33554432 | tf_op jit(solution)/shard_map/all_to_all | solution.py:143
  1243.8 43.5 %copy-start.1 = (s32[256,1024]{1,0:T(8,128)S(1)}, s32[256,1024]{1,0:T(8,128)}, u32[]{:S(2)}) copy-start(s32[256,1024]{1,0:T(8,128)} %param.7) | copy-start | bytes 3145732
Sparse Core Ops, SparseCore 0:
  271.6 803.6 all-gather.1
where the time goes:
time: 1310 us; the launch traced here: 1290 us
  waiting for transfers between devices  679 us (52%)
  matrix products  347 us (26%)
  other arithmetic  142 us (11%)
  local copies, waits for them, and re-layouts  92.4 us (7%)
  starting transfers between devices  19.8 us (2%)
  between operations  14.6 us (1%)
    all_to_all x1, waiting for transfers between devices, body(): lax.all_to_all(partial_value, ('chan', 'row'), split_axis=0, concat_axis=...  516 us
    all_to_all x1, waiting for transfers between devices, body(): lax.all_to_all(departing_blocks.reshape(channel_number * block_list, chan...  94.9 us
    dot_general x1, matrix products, beam_terms(): jnp.einsum('cba,caf->bcf', w_real, x_real, preferred_element_type=jnp.flo...  73.6 us
    ppermute x1, waiting for transfers between devices, from_behind(): return lax.ppermute(block, axis, route)  68.1 us
    dot_general x1, matrix products, beam_terms(): jnp.einsum('cba,caf->bcf', w_real, x_imag, preferred_element_type=jnp.flo...  64.4 us
    convert_element_type x1, other arithmetic, gram_block(): (jnp.stack([real_part, imag_part], axis=1) / frames).astype(jnp.bfloat16)  64.1 us
    dot_general x1, matrix products, beam_terms(): jnp.einsum('cba,caf->bcf', w_imag, x_imag, preferred_element_type=jnp.flo...  63.7 us
    dot_general x1, matrix products, beam_terms(): jnp.einsum('cba,caf->bcf', w_imag, x_real, preferred_element_type=jnp.flo...  63.3 us
  transfers between devices with their start and end apart: 4, of which 3 were waited for; matrix products, arithmetic and copies ran while one was open for 25% of the time, Pallas kernels for 0%

commit v1 on v0

v1 whole, which is shorter than its diff:
```python
import functools
import math

import jax
import jax.numpy as jnp
from jax import lax
from jax.experimental import pallas as pl
from jax.experimental.pallas import tpu as pltpu
from jax.sharding import PartitionSpec as P

A = 1024
FOURIER_LENGTH = 1024
NCH = 512
FILTER_TAPS = 8
BEAMS = 256
LANES = 128
CHUNKS = 8
VMEM = pl.BlockSpec(memory_space=pltpu.VMEM)
ANY = pl.BlockSpec(memory_space=pl.ANY)


def params(mib):
    return pltpu.CompilerParams(vmem_limit_bytes=mib * 2**20)


def cost(flops, bytes_accessed):
    return pl.CostEstimate(flops=int(flops), bytes_accessed=int(bytes_accessed), transcendentals=0)


def from_behind(block, axis, distance):
    devices = range(lax.axis_size(axis))
    route = [(i - distance, i) for i in devices if i - distance in devices]
    return lax.ppermute(block, axis, route)


def tap_table():
    position = jnp.arange(FILTER_TAPS * FOURIER_LENGTH, dtype=jnp.int32).astype(jnp.float32) + 0.5
    centred = position / FOURIER_LENGTH - FILTER_TAPS / 2.0
    window = 0.5 - 0.5 * jnp.cos(2.0 * math.pi * position / (FILTER_TAPS * FOURIER_LENGTH))
    return (jnp.sinc(centred) * window).reshape(FILTER_TAPS, FOURIER_LENGTH)


def dft_rows(channel_number):
    chan_ids = jnp.arange(NCH, dtype=jnp.int32).reshape(channel_number, 1, -1, 1)
    sample_ids = jnp.arange(FOURIER_LENGTH, dtype=jnp.int32)
    phase_angle = (chan_ids * sample_ids % FOURIER_LENGTH).astype(jnp.float32) * (
        2.0 * math.pi / FOURIER_LENGTH
    )
    scale = 1.0 / math.sqrt(FOURIER_LENGTH)
    table = jnp.concatenate([jnp.cos(phase_angle) * scale, -jnp.sin(phase_angle) * scale], axis=1)
    return table.astype(jnp.bfloat16).reshape(channel_number, -1, FOURIER_LENGTH)


def synth_table():
    chan_ids = jnp.arange(NCH, dtype=jnp.int32)
    sample_ids = jnp.arange(FOURIER_LENGTH, dtype=jnp.int32)
    phase_angle = (chan_ids[:, None] * sample_ids[None, :] % FOURIER_LENGTH).astype(jnp.float32) * (
        2.0 * math.pi / FOURIER_LENGTH
    )
    scale = 1.0 / math.sqrt(NCH)
    return jnp.stack([jnp.cos(phase_angle) * scale, -jnp.sin(phase_angle) * scale], axis=0).astype(
        jnp.bfloat16
    )


def phasor(delays, chan_ids, scale):
    angle = (delays * chan_ids % FOURIER_LENGTH).astype(jnp.float32) * (
        2.0 * math.pi / FOURIER_LENGTH
    )
    return jnp.cos(angle) * scale, -jnp.sin(angle) * scale


def front_kernel(rows, steps, parcels, place, samples, before, history, taps, table, *refs):
    outs, (filtered, wide) = refs[:-2], refs[-2:]
    step = pl.program_id(0)
    frames = samples.shape[1] // FOURIER_LENGTH
    past = FILTER_TAPS - 1
    group = min(16, rows)

    @pl.when(step < steps)
    def _():
        first = place[1] == 0

        def columns(i, carry):
            at = pl.multiple_of(i * LANES, LANES)
            weights = [
                jnp.broadcast_to(taps[t : t + 1, pl.ds(at, LANES)], (group, LANES))
                for t in range(FILTER_TAPS)
            ]
            for g in range(rows // group):
                here = slice(g * group, (g + 1) * group)
                values = []
                for frame in range(past):
                    lanes = pl.ds(at + frame * FOURIER_LENGTH, LANES)
                    values.append(
                        jnp.where(
                            first,
                            history[here, lanes].astype(jnp.float32),
                            before[here, lanes].astype(jnp.float32),
                        )
                    )
                for frame in range(frames):
                    lanes = pl.ds(at + frame * FOURIER_LENGTH, LANES)
                    values.append(samples[here, lanes].astype(jnp.float32))
                for frame in range(frames):
                    total = values[frame] * weights[0]
                    for t in range(1, FILTER_TAPS):
                        total = total + values[frame + t] * weights[t]
                    filtered[
                        frame, pl.ds(step * rows + g * group, group), pl.ds(at, LANES)
                    ] = total.astype(jnp.bfloat16)
            return carry

        lax.fori_loop(0, FOURIER_LENGTH // LANES, columns, 0)

    count = table.shape[0] // 2
    antennas = filtered.shape[1]
    width = wide.shape[2]
    parts = antennas // width
    for m in range(len(outs) // len(parcels)):

        @pl.when(step == steps + m)
        def _(m=m):
            for frame in range(frames):
                got = lax.dot_general(
                    table[...],
                    filtered[frame],
                    (((1,), (1,)), ((), ())),
                    preferred_element_type=jnp.float32,
                )
                for part in range(parts):
                    lanes = slice(part * width, (part + 1) * width)
                    wide[part, pl.ds(frame, count, stride=2 * frames), :] = got[:count, lanes]
                    wide[part, pl.ds(frames + frame, count, stride=2 * frames), :] = got[
                        count:, lanes
                    ]
            start = 0
            for p, size in enumerate(parcels):
                out = outs[m * len(parcels) + p]
                for part in range(parts):
                    lanes = slice(part * width, (part + 1) * width)
                    out[:, lanes] = wide[
                        part, start * 2 * frames : (start + size) * 2 * frames, :
                    ].astype(jnp.bfloat16)
                start += size


def front(samples, before, history, place, channel_number, parcels):
    antennas, length = samples.shape
    frames = length // FOURIER_LENGTH
    channel_total = NCH // channel_number
    rows = min(32, antennas)
    steps = antennas // rows
    width = min(LANES, antennas)
    past = (FILTER_TAPS - 1) * FOURIER_LENGTH
    grid_spec = pltpu.PrefetchScalarGridSpec(
        num_scalar_prefetch=1,
        grid=(steps + channel_number,),
        in_specs=[
            pl.BlockSpec((rows, length), lambda i, s: (jnp.minimum(i, steps - 1), 0)),
            pl.BlockSpec((rows, past), lambda i, s: (jnp.minimum(i, steps - 1), 0)),
            pl.BlockSpec((rows, past), lambda i, s: (jnp.minimum(i, steps - 1), 0)),
            VMEM,
            pl.BlockSpec(
                (None, 2 * channel_total, FOURIER_LENGTH),
                lambda i, s: (lax.rem(s[0] + jnp.maximum(i - steps, 0), channel_number), 0, 0),
            ),
        ],
        out_specs=[VMEM] * (channel_number * len(parcels)),
        scratch_shapes=[
            pltpu.VMEM((frames, antennas, FOURIER_LENGTH), jnp.bfloat16),
            pltpu.VMEM((antennas // width, channel_total * 2 * frames, width), jnp.float32),
        ],
    )
    return pl.pallas_call(
        functools.partial(front_kernel, rows, steps, parcels),
        grid_spec=grid_spec,
        out_shape=[
            jax.ShapeDtypeStruct((size * 2 * frames, antennas), jnp.bfloat16)
            for _ in range(channel_number)
            for size in parcels
        ],
        compiler_params=params(48),
        cost_estimate=cost(2 * antennas * frames * FOURIER_LENGTH * 2 * NCH * 2, 16 * 2**20),
        name="front",
    )(place, samples, before, history, tap_table(), dft_rows(channel_number))


def order_kernel(number, *refs):
    pieces, spread, outs = refs[:number], refs[number], refs[number + 1 :]
    rows = outs[0].shape[0]
    tile = math.gcd(rows, 256)
    for j, out in enumerate(outs):

        def part(i, carry, out=out, j=j):
            at = pl.multiple_of(i * tile, tile)
            total = None
            for m, piece in enumerate(pieces):
                got = jnp.dot(
                    piece[pl.ds(j * rows + at, tile), :],
                    spread[m],
                    preferred_element_type=jnp.float32,
                )
                total = got if total is None else total + got
            out[pl.ds(at, tile), :] = total.astype(jnp.bfloat16)
            return carry

        lax.fori_loop(0, rows // tile, part, 0)


def into_order(pieces, spread, chunks, rows):
    return pl.pallas_call(
        functools.partial(order_kernel, len(pieces)),
        in_specs=[VMEM] * (len(pieces) + 1),
        out_specs=[VMEM] * chunks,
        out_shape=[jax.ShapeDtypeStruct((rows, A), jnp.bfloat16)] * chunks,
        compiler_params=params(40),
        cost_estimate=cost(2 * chunks * rows * A * A * 2, chunks * rows * A * 4),
        name="into_order",
    )(*pieces, spread)


def spread_table(antenna_flags, chan_id, channel_number, block_list):
    per_shard = A // (channel_number * block_list)
    block = (chan_id - jnp.arange(channel_number, dtype=jnp.int32)) % channel_number
    own = jnp.arange(block_list * per_shard, dtype=jnp.int32)
    target = (
        (own // per_shard) * (A // block_list) + block[:, None] * per_shard + own % per_shard
    )
    hit = target[:, :, None] == jnp.arange(A, dtype=jnp.int32)
    return jnp.where(hit, antenna_flags, 0).astype(jnp.bfloat16)


def visibility_kernel(number, frames, aliased, place, *refs):
    pieces, out = refs[:number], refs[-1]
    half = pieces[0].shape[1] // 2
    row_count = out.shape[2]
    own_lanes = pl.ds(pl.multiple_of(place[1] * row_count, row_count), row_count)
    for i in range(pieces[0].shape[0]):
        everything = jnp.concatenate([piece[i] for piece in pieces], axis=0)
        own = jnp.concatenate([piece[i, :, own_lanes] for piece in pieces], axis=0)
        wide = own.astype(jnp.float32)
        swapped = jnp.concatenate(
            [
                part
                for s in range(number)
                for part in (
                    wide[(2 * s + 1) * half : (2 * s + 2) * half],
                    -wide[2 * s * half : (2 * s + 1) * half],
                )
            ],
            axis=0,
        )
        for e, left in enumerate((wide, swapped)):
            got = jnp.dot(
                left.T.astype(jnp.bfloat16), everything, preferred_element_type=jnp.float32
            )
            out[i, e] = (got * (1.0 / frames)).astype(jnp.bfloat16)


def visibilities_of(pieces, place, target, first, channel_total, row_count, frames):
    count = pieces[0].shape[0]
    block = math.gcd(count, 4)
    offset = first // block
    aliased = target is not None
    in_specs = [
        pl.BlockSpec((block,) + pieces[0].shape[1:], lambda i, s: (i, 0, 0)) for _ in pieces
    ]
    return pl.pallas_call(
        functools.partial(visibility_kernel, len(pieces), frames, aliased),
        grid_spec=pltpu.PrefetchScalarGridSpec(
            num_scalar_prefetch=1,
            grid=(count // block,),
            in_specs=in_specs + [ANY] * aliased,
            out_specs=pl.BlockSpec(
                (block, 2, row_count, A), lambda i, s: (i + offset, 0, 0, 0)
            ),
        ),
        out_shape=jax.ShapeDtypeStruct((channel_total, 2, row_count, A), jnp.bfloat16),
        input_output_aliases={1 + len(pieces): 0} if aliased else {},
        compiler_params=params(40),
        cost_estimate=cost(8 * count * row_count * A * 256, count * row_count * A * 4),
        name="visibilities",
    )(place, *pieces, *([target] if aliased else []))


def beam_kernel(number, *refs):
    pieces = refs[:number]
    base_re, base_im, step_re, step_im, out, state_re, state_im = refs[number:]
    half = pieces[0].shape[1] // 2
    beams = base_re.shape[0]

    @pl.when(pl.program_id(0) == 0)
    def _():
        state_re[...] = base_re[...]
        state_im[...] = base_im[...]

    for i in range(pieces[0].shape[0]):
        now_re, now_im = state_re[...], state_im[...]
        weights = jnp.concatenate([now_re, now_im], axis=0).astype(jnp.bfloat16)
        state_re[...] = now_re * step_re[...] - now_im * step_im[...]
        state_im[...] = now_re * step_im[...] + now_im * step_re[...]
        everything = jnp.concatenate([piece[i] for piece in pieces], axis=0)
        got = lax.dot_general(
            weights, everything, (((1,), (1,)), ((), ())), preferred_element_type=jnp.float32
        )
        direct, crossed = got[:beams], got[beams:]
        width = got.shape[1]
        lane = lax.broadcasted_iota(jnp.int32, crossed.shape, 1)
        real_lane = lax.rem(lane, 2 * half) < half
        crossed = jnp.where(
            real_lane,
            -pltpu.roll(crossed, width - half, 1),
            pltpu.roll(crossed, half, 1),
        )
        out[i] = (direct + crossed).astype(jnp.bfloat16)


def beams_of(pieces, base_re, base_im, step_re, step_im):
    count, rows, _ = pieces[0].shape
    number = len(pieces)
    beams = step_re.shape[0]
    block = math.gcd(count, 4)
    whole = pl.BlockSpec((beams, A), lambda i: (0, 0))
    return pl.pallas_call(
        functools.partial(beam_kernel, number),
        grid=(count // block,),
        in_specs=[pl.BlockSpec((block, rows, A), lambda i: (i, 0, 0)) for _ in pieces]
        + [whole] * 4,
        out_specs=pl.BlockSpec((block, beams, number * rows), lambda i: (i, 0, 0)),
        out_shape=jax.ShapeDtypeStruct((count, beams, number * rows), jnp.bfloat16),
        scratch_shapes=[pltpu.VMEM((beams, A), jnp.float32)] * 2,
        compiler_params=params(40),
        cost_estimate=cost(8 * count * beams * A * 256, count * number * rows * A * 2),
        name="beams",
    )(*pieces, base_re, base_im, step_re, step_im)


def synthesis_kernel(number, half, owners, spectra, table, out):
    got = [
        lax.dot_general(
            spectra[...], table[e], (((0,), (0,)), ((), ())), preferred_element_type=jnp.float32
        )
        for e in range(2)
    ]
    for s in range(number):
        real, imag = 2 * s * half, (2 * s + 1) * half
        at = pl.multiple_of(owners[s] * half, half)
        out[pl.ds(at, half), :] = got[0][real : real + half] + got[1][imag : imag + half]


def synthesis(spectra, owners, frames):
    beam_count, channels, width = spectra.shape
    number = owners.shape[0]
    return pl.pallas_call(
        functools.partial(synthesis_kernel, number, frames // number),
        grid_spec=pltpu.PrefetchScalarGridSpec(
            num_scalar_prefetch=1,
            grid=(beam_count,),
            in_specs=[pl.BlockSpec((None, channels, width), lambda i, s: (i, 0, 0)), VMEM],
            out_specs=pl.BlockSpec((None, frames, FOURIER_LENGTH), lambda i, s: (i, 0, 0)),
        ),
        out_shape=jax.ShapeDtypeStruct((beam_count, frames, FOURIER_LENGTH), jnp.float32),
        compiler_params=params(40),
        cost_estimate=cost(4 * beam_count * channels * width * FOURIER_LENGTH, 8 * 2**20),
        name="synthesis",
    )(owners, spectra, synth_table())


def body(samples, history, antenna_flags, beam_delays):
    channel_number = lax.axis_size("chan")
    n_row = lax.axis_size("row")
    chan_id = lax.axis_index("chan")
    row_id = lax.axis_index("row")
    block_list, antennas_per_shard, shard_length = samples.shape
    frames_per_shard = shard_length // FOURIER_LENGTH
    frames = frames_per_shard * n_row
    channel_total = NCH // channel_number
    row_count = A // n_row
    beam_count = BEAMS // (channel_number * n_row)
    antennas = block_list * antennas_per_shard
    chunk = channel_total // CHUNKS
    chunk_rows = chunk * 2 * frames_per_shard
    place = jnp.stack([chan_id, row_id]).astype(jnp.int32)

    cycle = [i for i in range(n_row) if i % 2 == 0] + [i for i in reversed(range(n_row)) if i % 2]
    onward = [(cycle[i], cycle[(i + 1) % n_row]) for i in range(n_row)]
    backward = [(b, a) for a, b in onward]
    position = jnp.array([cycle.index(i) for i in range(n_row)], jnp.int32)[row_id]
    owners = jnp.array(cycle, jnp.int32)[
        (position - jnp.arange(n_row, dtype=jnp.int32)) % n_row
    ]

    tail = samples[:, :, shard_length - (FILTER_TAPS - 1) * FOURIER_LENGTH :]
    before = from_behind(tail, "row", 1)

    parcels = [2, CHUNKS - 2]
    sent = front(
        samples.reshape(antennas, -1),
        before.reshape(antennas, -1),
        history.reshape(antennas, -1),
        place,
        channel_number,
        [p * chunk for p in parcels],
    )
    spread = spread_table(antenna_flags, chan_id, channel_number, block_list)
    chunks = []
    for p, size in enumerate(parcels):
        pieces = []
        for m in range(channel_number):
            piece = sent[m * len(parcels) + p]
            if m:
                route = [(i, (i + m) % channel_number) for i in range(channel_number)]
                piece = lax.ppermute(piece, "chan", route)
            pieces.append(piece)
        chunks += into_order(pieces, spread, size, chunk_rows)

    delays = lax.dynamic_index_in_dim(
        beam_delays.reshape(channel_number, n_row, beam_count, A), row_id, 1, keepdims=False
    ).reshape(channel_number * beam_count, A)
    starts = chan_id * channel_total + chunk * jnp.arange(CHUNKS, dtype=jnp.int32)
    base_re, base_im = phasor(delays[None], starts[:, None, None], 1.0 / math.sqrt(A))
    step_re, step_im = phasor(delays, 1, 1.0)

    visibilities = None
    beams = []
    for j in range(CHUNKS):
        piece = chunks[j].reshape(chunk, 2 * frames_per_shard, A)
        held = [piece]
        for _ in range(n_row - 1):
            piece = lax.ppermute(piece, "row", backward if j % 2 else onward)
            held.append(piece)
        if j % 2:
            held = held[:1] + held[:0:-1]
        beams.append(beams_of(held, base_re[j], base_im[j], step_re, step_im))
        visibilities = visibilities_of(
            held, place, visibilities, j * chunk, channel_total, row_count, frames
        )

    def to_owners(parts):
        value = jnp.concatenate(parts, axis=0)
        value = value.reshape(-1, channel_number, beam_count, 2 * frames).transpose(1, 2, 0, 3)
        return lax.all_to_all(value, "chan", split_axis=0, concat_axis=0, tiled=True)

    arrived = [to_owners(beams[: CHUNKS - 2]), to_owners(beams[CHUNKS - 2 :])]
    spectra = jnp.concatenate(arrived, axis=2).transpose(1, 0, 2, 3)
    beam_series = synthesis(
        spectra.reshape(beam_count, NCH, 2 * frames), owners, frames
    )
    return (visibilities, beam_series)


def solution(mesh):
    in_specs = (P(None, "chan", "row"), P(None, "chan", None), P(), P())
    out_specs = (P("chan", None, "row", None), P(("chan", "row"), None, None))
    return jax.shard_map(body, mesh=mesh, in_specs=in_specs, out_specs=out_specs, check_vma=False)
```

time: 1310 us -> 532 us (0.41); the launches traced: 1290 us -> 530 us
  waiting for transfers between devices: 679 us -> 250 us
  matrix products: 347 us -> 0 us
  Pallas kernels: 0 us -> 119 us
  other arithmetic: 142 us -> 31.5 us
  starting transfers between devices: 19.8 us -> 88.7 us
  local copies, waits for them, and re-layouts: 92.4 us -> 39.3 us
  between operations: 14.6 us -> 1.5 us
    all_to_all x2, waiting for transfers between devices: 611 us -> 0.01 us  [to_owners(): lax.all_to_all(value, 'chan', split_axis=0, concat_axis=0, tiled=True)]
    dot_general x8 -> x0, matrix products: 347 us -> none  [the longest x1 73.6 us: beam_terms(): jnp.einsum('cba,caf->bcf', w_real, x_real, preferred_element_type=jnp.flo...]
    ppermute x0 -> x62, waiting for transfers between devices: none -> 184 us  [the longest x56 162 us: body(): piece = lax.ppermute(piece, 'row', backward if j % 2 else onward)]
    pallas_call x0 -> x20, Pallas kernels: none -> 119 us  [the longest x8 57.4 us: visibilities_of(): pl.pallas_call(functools.partial(visibility_kernel, len(pieces), frames,...]
    convert_element_type x3 -> x1, other arithmetic: 89.8 us -> 0.4 us  [spread_table(): return jnp.where(hit, antenna_flags, 0).astype(jnp.bfloat16)]
    ppermute x0 -> x62, starting transfers between devices: none -> 73.8 us  [the longest x56 70.2 us: body(): piece = lax.ppermute(piece, 'row', backward if j % 2 else onward)]
    reshape x3 -> x2, local copies, waits for them, and re-layouts: 22.4 us -> 2.01 us  [to_owners(): value.reshape(-1, channel_number, beam_count, 2 * frames)]
    another operation x1 -> x0, local copies, waits for them, and re-layouts: 16.8 us -> none  [beam_terms(): return jnp.stack([beam_real, beam_imag], axis=1)]
  transfers between devices with their start and end apart: 4 -> 65, of which waited for: 3 -> 29; matrix products, arithmetic and copies ran while one was open for 25% -> 7% of each run, Pallas kernels for 0% -> 18%
where the time goes in v1:
time: 532 us; the launch traced here: 530 us
  waiting for transfers between devices  250 us (47%)
  Pallas kernels  119 us (22%)
  starting transfers between devices  88.7 us (17%)
  local copies, waits for them, and re-layouts  39.3 us (7%)
  other arithmetic  31.5 us (6%)
    ppermute x56, waiting for transfers between devices, body(): piece = lax.ppermute(piece, 'row', backward if j % 2 else onward)  162 us
    ppermute x56, starting transfers between devices, body(): piece = lax.ppermute(piece, 'row', backward if j % 2 else onward)  70.2 us
    ppermute x1, waiting for transfers between devices, from_behind(): return lax.ppermute(block, axis, route)  66.1 us
    pallas_call x8, Pallas kernels, visibilities_of(): pl.pallas_call(functools.partial(visibility_kernel, len(pieces), frames,...  57.4 us
    pallas_call x8, Pallas kernels, beams_of(): pl.pallas_call(functools.partial(beam_kernel, number), grid=(count // blo...  32.9 us
    unnamed x171, local copies, waits for them, and re-layouts  29 us
    ppermute x6, waiting for transfers between devices, body(): piece = lax.ppermute(piece, 'chan', route)  22.7 us
    another operation x2, other arithmetic  18.4 us
  transfers between devices with their start and end apart: 65, of which 29 were waited for; matrix products, arithmetic and copies ran while one was open for 7% of the time, Pallas kernels for 18%

profile of v1, /device:TPU:0, one launch (start us, length us, event | category | flops | bytes accessed | tf_op | source)
XLA Modules:
  0.0 530.2 jit_solution(13955153151919547270)
XLA Ops:
  4.7 6.7 %collective-permute-start = (bf16[8,32,7168]{2,1,0:T(8,128)(2,1)}, bf16[8,32,7168]{2,1,0:T(8,128)(2,1)}, u32[]{:S(2)}, u32[]{:S(2)}) collective-permute-start(bf16[8,32,7168]{2,1,0:T(8,128)(2,1)} %slice.51), channel_id=1, source_target_pairs={{0,1},{1,2},{2,3},{3,4},{4,5},{5,6},{6,7},{8,9},{9,10},{10,11},{11... | collective-permute-start | bytes 11010056 | tf_op jit(solution)/shard_map/ppermute | solution.py:33
  11.7 9.1 %multiply_convert_fusion.3 = (bf16[4,1,128,1024]{3,2,1,0:T(8,128)(2,1)S(1)}, bf16[4,1,128,1024]{3,2,1,0:T(8,128)(2,1)S(1)}) fusion(s32[4,128]{1,0:T(4,128)S(1)} %multiply_add_fusion.1), kind=kLoop, calls=%fused_computation.22 | loop fusion | flops 9961472 | bytes 2099200 | tf_op jit(solution)/shard_map/convert.2
  22.4 66.1 %collective-permute-done = bf16[8,32,7168]{2,1,0:T(8,128)(2,1)} collective-permute-done((bf16[8,32,7168]{2,1,0:T(8,128)(2,1)}, bf16[8,32,7168]{2,1,0:T(8,128)(2,1)}, u32[]{:S(2)}, u32[]{:S(2)}) %collective-permute-start) | collective-permute-done | bytes 3670048 | tf_op jit(solution)/shard_map/ppermute | solution.py:33
  88.5 18.2 %front.1 = (bf16[512,256]{1,0:T(8,128)(2,1)S(1)}, bf16[1536,256]{1,0:T(8,128)(2,1)S(1)}, bf16[512,256]{1,0:T(8,128)(2,1)S(1)}, bf16[1536,256]{1,0:T(8,128)(2,1)S...) custom-call(s32[2]{0:T(128)S(1)} %pad_add_fusion.place, ...), custom_call_target="tpu_custom_call" | custom-call | flops 8589934592 | bytes 16777216 | tf_op jit(solution)/shard_map/front/pallas_call | solution.py:175
  127.0 10.6 %collective-permute-done.56.refs_1_ = bf16[16,16,1024]{2,1,0:T(8,128)(2,1)S(1)} collective-permute-done((bf16[16,16,1024]{2,1,0:T(8,128)(2,1)S(1)}, bf16[16,16,1024]{2,1,0:T(8,128)(2,1)S(1)}, u32[]{:S(2)}, u32[]{:S(2)}) %collective-permute-start.56) | collective-permute-done | bytes 524320 | tf_op jit(solution)/shard_map/ppermute | solution.py:431
  140.8 12.8 %collective-permute-done.3.refs_3_ = bf16[1536,256]{1,0:T(8,128)(2,1)S(1)} collective-permute-done((bf16[1536,256]{1,0:T(8,128)(2,1)S(1)}, bf16[1536,256]{1,0:T(8,128)(2,1)S(1)}, u32[]{:S(2)}, u32[]{:S(2)}) %collective-permute-start.3) | collective-permute-done | bytes 786464 | tf_op jit(solution)/shard_map/ppermute | solution.py:414
  165.3 7.6 %collective-permute-done.11.refs_1_ = bf16[16,16,1024]{2,1,0:T(8,128)(2,1)S(1)} collective-permute-done((bf16[16,16,1024]{2,1,0:T(8,128)(2,1)S(1)}, bf16[16,16,1024]{2,1,0:T(8,128)(2,1)S(1)}, u32[]{:S(2)}, u32[]{:S(2)}) %collective-permute-start.11) | collective-permute-done | bytes 524320 | tf_op jit(solution)/shard_map/ppermute | solution.py:431
  178.6 8.0 %collective-permute-done.18.refs_7_ = bf16[16,16,1024]{2,1,0:T(8,128)(2,1)S(1)} collective-permute-done((bf16[16,16,1024]{2,1,0:T(8,128)(2,1)S(1)}, bf16[16,16,1024]{2,1,0:T(8,128)(2,1)S(1)}, u32[]{:S(2)}, u32[]{:S(2)}) %collective-permute-start.18) | collective-permute-done | bytes 524320 | tf_op jit(solution)/shard_map/ppermute | solution.py:431
  189.4 8.4 %collective-permute-done.32.refs_7_ = bf16[16,16,1024]{2,1,0:T(8,128)(2,1)S(1)} collective-permute-done((bf16[16,16,1024]{2,1,0:T(8,128)(2,1)S(1)}, bf16[16,16,1024]{2,1,0:T(8,128)(2,1)S(1)}, u32[]{:S(2)}, u32[]{:S(2)}) %collective-permute-start.32) | collective-permute-done | bytes 524320 | tf_op jit(solution)/shard_map/ppermute | solution.py:431
  199.7 7.0 %collective-permute-done.58.refs_3_ = bf16[16,16,1024]{2,1,0:T(8,128)(2,1)S(1)} collective-permute-done((bf16[16,16,1024]{2,1,0:T(8,128)(2,1)S(1)}, bf16[16,16,1024]{2,1,0:T(8,128)(2,1)S(1)}, u32[]{:S(2)}, u32[]{:S(2)}) %collective-permute-start.58) | collective-permute-done | bytes 524320 | tf_op jit(solution)/shard_map/ppermute | solution.py:431
  210.7 7.1 %collective-permute-done.12.refs_2_ = bf16[16,16,1024]{2,1,0:T(8,128)(2,1)S(1)} collective-permute-done((bf16[16,16,1024]{2,1,0:T(8,128)(2,1)S(1)}, bf16[16,16,1024]{2,1,0:T(8,128)(2,1)S(1)}, u32[]{:S(2)}, u32[]{:S(2)}) %collective-permute-start.12) | collective-permute-done | bytes 524320 | tf_op jit(solution)/shard_map/ppermute | solution.py:431
  223.5 8.0 %collective-permute-done.19.refs_6_ = bf16[16,16,1024]{2,1,0:T(8,128)(2,1)S(1)} collective-permute-done((bf16[16,16,1024]{2,1,0:T(8,128)(2,1)S(1)}, bf16[16,16,1024]{2,1,0:T(8,128)(2,1)S(1)}, u32[]{:S(2)}, u32[]{:S(2)}) %collective-permute-start.19) | collective-permute-done | bytes 524320 | tf_op jit(solution)/shard_map/ppermute | solution.py:431
  235.2 7.6 %collective-permute-done.33.refs_6_ = bf16[16,16,1024]{2,1,0:T(8,128)(2,1)S(1)} collective-permute-done((bf16[16,16,1024]{2,1,0:T(8,128)(2,1)S(1)}, bf16[16,16,1024]{2,1,0:T(8,128)(2,1)S(1)}, u32[]{:S(2)}, u32[]{:S(2)}) %collective-permute-start.33) | collective-permute-done | bytes 524320 | tf_op jit(solution)/shard_map/ppermute | solution.py:431
  244.7 6.9 %collective-permute-done.59.refs_4_ = bf16[16,16,1024]{2,1,0:T(8,128)(2,1)S(1)} collective-permute-done((bf16[16,16,1024]{2,1,0:T(8,128)(2,1)S(1)}, bf16[16,16,1024]{2,1,0:T(8,128)(2,1)S(1)}, u32[]{:S(2)}, u32[]{:S(2)}) %collective-permute-start.59) | collective-permute-done | bytes 524320 | tf_op jit(solution)/shard_map/ppermute | solution.py:431
  255.7 7.1 %collective-permute-done.13.refs_3_ = bf16[16,16,1024]{2,1,0:T(8,128)(2,1)} collective-permute-done((bf16[16,16,1024]{2,1,0:T(8,128)(2,1)S(1)}, bf16[16,16,1024]{2,1,0:T(8,128)(2,1)}, u32[]{:S(2)}, u32[]{:S(2)}) %collective-permute-start.13) | collective-permute-done | bytes 524320 | tf_op jit(solution)/shard_map/ppermute | solution.py:431
  268.6 7.9 %collective-permute-done.20.refs_5_ = bf16[16,16,1024]{2,1,0:T(8,128)(2,1)} collective-permute-done((bf16[16,16,1024]{2,1,0:T(8,128)(2,1)S(1)}, bf16[16,16,1024]{2,1,0:T(8,128)(2,1)}, u32[]{:S(2)}, u32[]{:S(2)}) %collective-permute-start.20) | collective-permute-done | bytes 524320 | tf_op jit(solution)/shard_map/ppermute | solution.py:431
  278.6 9.1 %collective-permute-done.34.refs_5_ = bf16[16,16,1024]{2,1,0:T(8,128)(2,1)S(1)} collective-permute-done((bf16[16,16,1024]{2,1,0:T(8,128)(2,1)S(1)}, bf16[16,16,1024]{2,1,0:T(8,128)(2,1)S(1)}, u32[]{:S(2)}, u32[]{:S(2)}) %collective-permute-start.34) | collective-permute-done | bytes 524320 | tf_op jit(solution)/shard_map/ppermute | solution.py:431
  289.3 7.2 %collective-permute-done.60.refs_5_ = bf16[16,16,1024]{2,1,0:T(8,128)(2,1)S(1)} collective-permute-done((bf16[16,16,1024]{2,1,0:T(8,128)(2,1)S(1)}, bf16[16,16,1024]{2,1,0:T(8,128)(2,1)S(1)}, u32[]{:S(2)}, u32[]{:S(2)}) %collective-permute-start.60) | collective-permute-done | bytes 524320 | tf_op jit(solution)/shard_map/ppermute | solution.py:431
  301.3 6.6 %collective-permute-done.14.refs_4_ = bf16[16,16,1024]{2,1,0:T(8,128)(2,1)} collective-permute-done((bf16[16,16,1024]{2,1,0:T(8,128)(2,1)}, bf16[16,16,1024]{2,1,0:T(8,128)(2,1)}, u32[]{:S(2)}, u32[]{:S(2)}) %collective-permute-start.14) | collective-permute-done | bytes 524320 | tf_op jit(solution)/shard_map/ppermute | solution.py:431
  311.9 9.6 %collective-permute-done.21.refs_4_ = bf16[16,16,1024]{2,1,0:T(8,128)(2,1)} collective-permute-done((bf16[16,16,1024]{2,1,0:T(8,128)(2,1)}, bf16[16,16,1024]{2,1,0:T(8,128)(2,1)}, u32[]{:S(2)}, u32[]{:S(2)}) %collective-permute-start.21) | collective-permute-done | bytes 524320 | tf_op jit(solution)/shard_map/ppermute | solution.py:431
  328.8 9.3 %multiply_convert_fusion = (bf16[1,512,1024]{2,1,0:T(8,128)(2,1)}, bf16[1,512,1024]{2,1,0:T(8,128)(2,1)}) fusion(), kind=kLoop, calls=%fused_computation.17 | loop fusion | flops 9961472 | bytes 2097152 | tf_op jit(solution)/shard_map/convert.1
  346.7 6.1 %collective-permute-done.15.refs_5_ = bf16[16,16,1024]{2,1,0:T(8,128)(2,1)} collective-permute-done((bf16[16,16,1024]{2,1,0:T(8,128)(2,1)}, bf16[16,16,1024]{2,1,0:T(8,128)(2,1)}, u32[]{:S(2)}, u32[]{:S(2)}) %collective-permute-start.15) | collective-permute-done | bytes 524320 | tf_op jit(solution)/shard_map/ppermute | solution.py:431
  368.5 9.2 %collective-permute-done.36.refs_3_ = bf16[16,16,1024]{2,1,0:T(8,128)(2,1)} collective-permute-done((bf16[16,16,1024]{2,1,0:T(8,128)(2,1)}, bf16[16,16,1024]{2,1,0:T(8,128)(2,1)}, u32[]{:S(2)}, u32[]{:S(2)}) %collective-permute-start.36) | collective-permute-done | bytes 524320 | tf_op jit(solution)/shard_map/ppermute | solution.py:431
  380.4 6.9 %visibilities.8.refs_8_ = bf16[128,2,128,1024]{3,2,1,0:T(8,128)(2,1)} custom-call(s32[2]{0:T(128)S(1)} %pad_add_fusion.place, bf16[16,16,1024]{2,1,0:T(8,128)(2,1)S(1)} %bitcast.89, bf16[16,16,1024]{2,1,0:T(8,128)(2,1)S(1)} %copy-done.31, bf16[16,16,1024]{2,1,0:T(8,128)(2,1)S(1)} %copy-done.33, bf16[16,16,1024]{2,1,0:T(8,128)(2,1)S(1)} %copy-done.43, ...), custom_call_target="tpu_custom_call" | custom-call | flops 4294967296 | bytes 8388608 | tf_op jit(solution)/shard_map/visibilities/pallas_call | solution.py:269
  389.4 8.4 %collective-permute-done.16.refs_6_ = bf16[16,16,1024]{2,1,0:T(8,128)(2,1)S(1)} collective-permute-done((bf16[16,16,1024]{2,1,0:T(8,128)(2,1)}, bf16[16,16,1024]{2,1,0:T(8,128)(2,1)S(1)}, u32[]{:S(2)}, u32[]{:S(2)}) %collective-permute-start.16) | collective-permute-done | bytes 524320 | tf_op jit(solution)/shard_map/ppermute | solution.py:431
  401.7 6.9 %visibilities.9.refs_8_ = bf16[128,2,128,1024]{3,2,1,0:T(8,128)(2,1)} custom-call(s32[2]{0:T(128)S(1)} %pad_add_fusion.place, bf16[16,16,1024]{2,1,0:T(8,128)(2,1)S(1)} %bitcast.86, bf16[16,16,1024]{2,1,0:T(8,128)(2,1)S(1)} %collective-permute-done.55.refs_1_, bf16[16,16,1024]{2,1,0:T(8,128)(2,1)S(1)} %copy-done.60, ...), custom_call_target="tpu_custom_call", output_to_operand_aliasing={{}: (9, {})} | custom-call | flops 4294967296 | bytes 8388608 | tf_op jit(solution)/shard_map/visibilities/pallas_call | solution.py:269
  458.4 7.0 %visibilities.10.refs_8_ = bf16[128,2,128,1024]{3,2,1,0:T(8,128)(2,1)} custom-call(s32[2]{0:T(128)S(1)} %pad_add_fusion.place, bf16[16,16,1024]{2,1,0:T(8,128)(2,1)S(1)} %bitcast.84, bf16[16,16,1024]{2,1,0:T(8,128)(2,1)S(1)} %copy-done.25, bf16[16,16,1024]{2,1,0:T(8,128)(2,1)S(1)} %copy-done.37, ...), custom_call_target="tpu_custom_call", output_to_operand_aliasing={{}: (9, {})} | custom-call | flops 4294967296 | bytes 8388608 | tf_op jit(solution)/shard_map/visibilities/pallas_call | solution.py:269
  469.7 7.3 %visibilities.11.refs_8_ = bf16[128,2,128,1024]{3,2,1,0:T(8,128)(2,1)} custom-call(s32[2]{0:T(128)S(1)} %pad_add_fusion.place, bf16[16,16,1024]{2,1,0:T(8,128)(2,1)S(1)} %bitcast.81, bf16[16,16,1024]{2,1,0:T(8,128)(2,1)} %collective-permute-done.38.refs_1_, bf16[16,16,1024]{2,1,0:T(8,128)(2,1)} %collective-permute-done.37.refs_2_, ...), custom_call_target="tpu_custom_call", output_to_operand_aliasing={{}: (9, {})} | custom-call | flops 4294967296 | bytes 8388608 | tf_op jit(solution)/shard_map/visibilities/pallas_call | solution.py:269
  481.4 7.5 %visibilities.12.refs_8_ = bf16[128,2,128,1024]{3,2,1,0:T(8,128)(2,1)} custom-call(s32[2]{0:T(128)S(1)} %pad_add_fusion.place, bf16[16,16,1024]{2,1,0:T(8,128)(2,1)S(1)} %bitcast.78, bf16[16,16,1024]{2,1,0:T(8,128)(2,1)S(1)} %copy-done.10, bf16[16,16,1024]{2,1,0:T(8,128)(2,1)S(1)} %copy-done.29, ...), custom_call_target="tpu_custom_call", output_to_operand_aliasing={{}: (9, {})} | custom-call | flops 4294967296 | bytes 8388608 | tf_op jit(solution)/shard_map/visibilities/pallas_call | solution.py:269
  489.0 7.5 %visibilities.13.refs_8_ = bf16[128,2,128,1024]{3,2,1,0:T(8,128)(2,1)} custom-call(s32[2]{0:T(128)S(1)} %pad_add_fusion.place, bf16[16,16,1024]{2,1,0:T(8,128)(2,1)S(1)} %bitcast.74, bf16[16,16,1024]{2,1,0:T(8,128)(2,1)} %collective-permute-done.24.refs_1_, bf16[16,16,1024]{2,1,0:T(8,128)(2,1)} %collective-permute-done.23.refs_2_, ...), custom_call_target="tpu_custom_call", output_to_operand_aliasing={{}: (9, {})} | custom-call | flops 4294967296 | bytes 8388608 | tf_op jit(solution)/shard_map/visibilities/pallas_call | solution.py:269
  508.3 7.1 %visibilities.14.refs_8_ = bf16[128,2,128,1024]{3,2,1,0:T(8,128)(2,1)} custom-call(s32[2]{0:T(128)S(1)} %pad_add_fusion.place, bf16[16,16,1024]{2,1,0:T(8,128)(2,1)S(1)} %bitcast.72, bf16[16,16,1024]{2,1,0:T(8,128)(2,1)S(1)} %collective-permute-done.11.refs_1_, bf16[16,16,1024]{2,1,0:T(8,128)(2,1)S(1)} %copy-done.6, ...), custom_call_target="tpu_custom_call", output_to_operand_aliasing={{}: (9, {})} | custom-call | flops 4294967296 | bytes 8388608 | tf_op jit(solution)/shard_map/visibilities/pallas_call | solution.py:269
  515.4 7.1 %visibilities.15 = bf16[128,2,128,1024]{3,2,1,0:T(8,128)(2,1)} custom-call(s32[2]{0:T(128)S(1)} %pad_add_fusion.place, bf16[16,16,1024]{2,1,0:T(8,128)(2,1)S(1)} %bitcast.69, bf16[16,16,1024]{2,1,0:T(8,128)(2,1)S(1)} %copy-done.62, bf16[16,16,1024]{2,1,0:T(8,128)(2,1)S(1)} %copy-done.56, ...), custom_call_target="tpu_custom_call", output_to_operand_aliasing={{}: (9, {})} | custom-call | flops 4294967296 | bytes 8388608 | tf_op jit(solution)/shard_map/visibilities/pallas_call | solution.py:269
  (316 shorter events, 206.8 us)
Async XLA Ops:
  4.7 83.8 %collective-permute-start = (bf16[8,32,7168]{2,1,0:T(8,128)(2,1)}, bf16[8,32,7168]{2,1,0:T(8,128)(2,1)}, u32[]{:S(2)}, u32[]{:S(2)}) collective-permute-start(bf16[8,32,7168]{2,1,0:T(8,128)(2,1)} %slice.51), channel_id=1, source_target_pairs={{0,1},{1,2},{2,3},{3,4},{4,5},{5,6},{6,7},{8,9},{9,10},{10,11},{11... | collective-permute-start | bytes 11010056 | tf_op jit(solution)/shard_map/ppermute | solution.py:33
  109.8 31.0 %collective-permute-start.1 = (bf16[1536,256]{1,0:T(8,128)(2,1)S(1)}, bf16[1536,256]{1,0:T(8,128)(2,1)S(1)}, u32[]{:S(2)}, u32[]{:S(2)}) collective-permute-start(bf16[1536,256]{1,0:T(8,128)(2,1)S(1)} %get-tuple-element.19), channel_id=1, source_target_pairs={{0,8},{8,16},{16,24},{24,0},{1,9},{9,17},{17,25},{25,1},{2,10},{10... | collective-permute-start | bytes 2359304 | tf_op jit(solution)/shard_map/ppermute | solution.py:414
  109.8 31.0 %collective-permute-start.2 = (bf16[1536,256]{1,0:T(8,128)(2,1)S(1)}, bf16[1536,256]{1,0:T(8,128)(2,1)S(1)}, u32[]{:S(2)}, u32[]{:S(2)}) collective-permute-start(bf16[1536,256]{1,0:T(8,128)(2,1)S(1)} %get-tuple-element.20), channel_id=1, source_target_pairs={{0,16},{8,24},{16,0},{24,8},{1,17},{9,25},{17,1},{25,9},{2,18},{10... | collective-permute-start | bytes 2359304 | tf_op jit(solution)/shard_map/ppermute | solution.py:414
  114.7 39.0 %collective-permute-start.3 = (bf16[1536,256]{1,0:T(8,128)(2,1)S(1)}, bf16[1536,256]{1,0:T(8,128)(2,1)S(1)}, u32[]{:S(2)}, u32[]{:S(2)}) collective-permute-start(bf16[1536,256]{1,0:T(8,128)(2,1)S(1)} %get-tuple-element.21), channel_id=1, source_target_pairs={{0,24},{8,0},{16,8},{24,16},{1,25},{9,1},{17,9},{25,17},{2,26},{10... | collective-permute-start | bytes 2359304 | tf_op jit(solution)/shard_map/ppermute | solution.py:414
  163.5 34.3 %collective-permute-start.32 = (bf16[16,16,1024]{2,1,0:T(8,128)(2,1)S(1)}, bf16[16,16,1024]{2,1,0:T(8,128)(2,1)S(1)}, u32[]{:S(2)}, u32[]{:S(2)}) collective-permute-start(bf16[16,16,1024]{2,1,0:T(8,128)(2,1)S(1)} %bitcast.79), channel_id=1, source_target_pairs={{2,0},{4,2},{6,4},{7,6},{5,7},{3,5},{1,3},{0,1},{10,8},{12,10},{14... | collective-permute-start | bytes 1572872 | tf_op jit(solution)/shard_map/ppermute | solution.py:431
  176.2 30.4 %collective-permute-start.58 = (bf16[16,16,1024]{2,1,0:T(8,128)(2,1)S(1)}, bf16[16,16,1024]{2,1,0:T(8,128)(2,1)S(1)}, u32[]{:S(2)}, u32[]{:S(2)}) collective-permute-start(bf16[16,16,1024]{2,1,0:T(8,128)(2,1)S(1)} %collective-permute-done.57.refs_2_), channel_id=1, source_target_pairs={{0,2},{2,4},{4,6},{6,7},{7,5},{5,3},{3,1},{1,0},{8,10},{10,12},{12... | collective-permute-start | bytes 1572872 | tf_op jit(solution)/shard_map/ppermute | solution.py:431
  187.5 30.4 %collective-permute-start.12 = (bf16[16,16,1024]{2,1,0:T(8,128)(2,1)S(1)}, bf16[16,16,1024]{2,1,0:T(8,128)(2,1)S(1)}, u32[]{:S(2)}, u32[]{:S(2)}) collective-permute-start(bf16[16,16,1024]{2,1,0:T(8,128)(2,1)S(1)} %collective-permute-done.11.refs_1_), channel_id=1, source_target_pairs={{0,2},{2,4},{4,6},{6,7},{7,5},{5,3},{3,1},{1,0},{8,10},{10,12},{12... | collective-permute-start | bytes 1572872 | tf_op jit(solution)/shard_map/ppermute | solution.py:431
  197.9 33.6 %collective-permute-start.19 = (bf16[16,16,1024]{2,1,0:T(8,128)(2,1)S(1)}, bf16[16,16,1024]{2,1,0:T(8,128)(2,1)S(1)}, u32[]{:S(2)}, u32[]{:S(2)}) collective-permute-start(bf16[16,16,1024]{2,1,0:T(8,128)(2,1)S(1)} %collective-permute-done.18.refs_7_), channel_id=1, source_target_pairs={{2,0},{4,2},{6,4},{7,6},{5,7},{3,5},{1,3},{0,1},{10,8},{12,10},{14... | collective-permute-start | bytes 1572872 | tf_op jit(solution)/shard_map/ppermute | solution.py:431
  209.9 32.8 %collective-permute-start.33 = (bf16[16,16,1024]{2,1,0:T(8,128)(2,1)S(1)}, bf16[16,16,1024]{2,1,0:T(8,128)(2,1)S(1)}, u32[]{:S(2)}, u32[]{:S(2)}) collective-permute-start(bf16[16,16,1024]{2,1,0:T(8,128)(2,1)S(1)} %collective-permute-done.32.refs_7_), channel_id=1, source_target_pairs={{2,0},{4,2},{6,4},{7,6},{5,7},{3,5},{1,3},{0,1},{10,8},{12,10},{14... | collective-permute-start | bytes 1572872 | tf_op jit(solution)/shard_map/ppermute | solution.py:431
  221.1 30.4 %collective-permute-start.59 = (bf16[16,16,1024]{2,1,0:T(8,128)(2,1)S(1)}, bf16[16,16,1024]{2,1,0:T(8,128)(2,1)S(1)}, u32[]{:S(2)}, u32[]{:S(2)}) collective-permute-start(bf16[16,16,1024]{2,1,0:T(8,128)(2,1)S(1)} %collective-permute-done.58.refs_3_), channel_id=1, source_target_pairs={{0,2},{2,4},{4,6},{6,7},{7,5},{5,3},{3,1},{1,0},{8,10},{10,12},{12... | collective-permute-start | bytes 1572872 | tf_op jit(solution)/shard_map/ppermute | solution.py:431
  232.4 30.4 %collective-permute-start.13 = (bf16[16,16,1024]{2,1,0:T(8,128)(2,1)S(1)}, bf16[16,16,1024]{2,1,0:T(8,128)(2,1)}, u32[]{:S(2)}, u32[]{:S(2)}) collective-permute-start(bf16[16,16,1024]{2,1,0:T(8,128)(2,1)S(1)} %collective-permute-done.12.refs_2_), channel_id=1, source_target_pairs={{0,2},{2,4},{4,6},{6,7},{7,5},{5,3},{3,1},{1,0},{8,10},{10,12},{12... | collective-permute-start | bytes 1572872 | tf_op jit(solution)/shard_map/ppermute | solution.py:431
  242.8 33.7 %collective-permute-start.20 = (bf16[16,16,1024]{2,1,0:T(8,128)(2,1)S(1)}, bf16[16,16,1024]{2,1,0:T(8,128)(2,1)}, u32[]{:S(2)}, u32[]{:S(2)}) collective-permute-start(bf16[16,16,1024]{2,1,0:T(8,128)(2,1)S(1)} %collective-permute-done.19.refs_6_), channel_id=1, source_target_pairs={{2,0},{4,2},{6,4},{7,6},{5,7},{3,5},{1,3},{0,1},{10,8},{12,10},{14... | collective-permute-start | bytes 1572872 | tf_op jit(solution)/shard_map/ppermute | solution.py:431
  254.9 32.8 %collective-permute-start.34 = (bf16[16,16,1024]{2,1,0:T(8,128)(2,1)S(1)}, bf16[16,16,1024]{2,1,0:T(8,128)(2,1)S(1)}, u32[]{:S(2)}, u32[]{:S(2)}) collective-permute-start(bf16[16,16,1024]{2,1,0:T(8,128)(2,1)S(1)} %collective-permute-done.33.refs_6_), channel_id=1, source_target_pairs={{2,0},{4,2},{6,4},{7,6},{5,7},{3,5},{1,3},{0,1},{10,8},{12,10},{14... | collective-permute-start | bytes 1572872 | tf_op jit(solution)/shard_map/ppermute | solution.py:431
  266.2 30.3 %collective-permute-start.60 = (bf16[16,16,1024]{2,1,0:T(8,128)(2,1)S(1)}, bf16[16,16,1024]{2,1,0:T(8,128)(2,1)S(1)}, u32[]{:S(2)}, u32[]{:S(2)}) collective-permute-start(bf16[16,16,1024]{2,1,0:T(8,128)(2,1)S(1)} %collective-permute-done.59.refs_4_), channel_id=1, source_target_pairs={{0,2},{2,4},{4,6},{6,7},{7,5},{5,3},{3,1},{1,0},{8,10},{10,12},{12... | collective-permute-start | bytes 1572872 | tf_op jit(solution)/shard_map/ppermute | solution.py:431
  276.6 31.2 %collective-permute-start.14 = (bf16[16,16,1024]{2,1,0:T(8,128)(2,1)}, bf16[16,16,1024]{2,1,0:T(8,128)(2,1)}, u32[]{:S(2)}, u32[]{:S(2)}) collective-permute-start(bf16[16,16,1024]{2,1,0:T(8,128)(2,1)} %collective-permute-done.13.refs_3_), channel_id=1, source_target_pairs={{0,2},{2,4},{4,6},{6,7},{7,5},{5,3},{3,1},{1,0},{8,10},{10,12},{12... | collective-permute-start | bytes 1572872 | tf_op jit(solution)/shard_map/ppermute | solution.py:431
  288.5 33.0 %collective-permute-start.21 = (bf16[16,16,1024]{2,1,0:T(8,128)(2,1)}, bf16[16,16,1024]{2,1,0:T(8,128)(2,1)}, u32[]{:S(2)}, u32[]{:S(2)}) collective-permute-start(bf16[16,16,1024]{2,1,0:T(8,128)(2,1)} %collective-permute-done.20.refs_5_), channel_id=1, source_target_pairs={{2,0},{4,2},{6,4},{7,6},{5,7},{3,5},{1,3},{0,1},{10,8},{12,10},{14... | collective-permute-start | bytes 1572872 | tf_op jit(solution)/shard_map/ppermute | solution.py:431
  297.3 29.6 %collective-permute-start.28 = (bf16[16,16,1024]{2,1,0:T(8,128)(2,1)}, bf16[16,16,1024]{2,1,0:T(8,128)(2,1)}, u32[]{:S(2)}, u32[]{:S(2)}) collective-permute-start(bf16[16,16,1024]{2,1,0:T(8,128)(2,1)} %collective-permute-done.27.refs_3_), channel_id=1, source_target_pairs={{0,2},{2,4},{4,6},{6,7},{7,5},{5,3},{3,1},{1,0},{8,10},{10,12},{12... | collective-permute-start | bytes 1572872 | tf_op jit(solution)/shard_map/ppermute | solution.py:431
  301.2 36.9 %collective-permute-start.35 = (bf16[16,16,1024]{2,1,0:T(8,128)(2,1)}, bf16[16,16,1024]{2,1,0:T(8,128)(2,1)}, u32[]{:S(2)}, u32[]{:S(2)}) collective-permute-start(bf16[16,16,1024]{2,1,0:T(8,128)(2,1)} %copy-done.40), channel_id=1, source_target_pairs={{2,0},{4,2},{6,4},{7,6},{5,7},{3,5},{1,3},{0,1},{10,8},{12,10},{14... | collective-permute-start | bytes 1572872 | tf_op jit(solution)/shard_map/ppermute | solution.py:431
  307.9 30.3 %collective-permute-start.42 = (bf16[16,16,1024]{2,1,0:T(8,128)(2,1)}, bf16[16,16,1024]{2,1,0:T(8,128)(2,1)S(1)}, u32[]{:S(2)}, u32[]{:S(2)}) collective-permute-start(bf16[16,16,1024]{2,1,0:T(8,128)(2,1)} %copy-done.44), channel_id=1, source_target_pairs={{0,2},{2,4},{4,6},{6,7},{7,5},{5,3},{3,1},{1,0},{8,10},{10,12},{12... | collective-permute-start | bytes 1572872 | tf_op jit(solution)/shard_map/ppermute | solution.py:431
  310.3 31.2 %collective-permute-start.61 = (bf16[16,16,1024]{2,1,0:T(8,128)(2,1)}, bf16[16,16,1024]{2,1,0:T(8,128)(2,1)}, u32[]{:S(2)}, u32[]{:S(2)}) collective-permute-start(bf16[16,16,1024]{2,1,0:T(8,128)(2,1)} %copy-done.53), channel_id=1, source_target_pairs={{0,2},{2,4},{4,6},{6,7},{7,5},{5,3},{3,1},{1,0},{8,10},{10,12},{12... | collective-permute-start | bytes 1572872 | tf_op jit(solution)/shard_map/ppermute | solution.py:431
  338.2 28.2 %collective-permute-start.22 = (bf16[16,16,1024]{2,1,0:T(8,128)(2,1)}, bf16[16,16,1024]{2,1,0:T(8,128)(2,1)}, u32[]{:S(2)}, u32[]{:S(2)}) collective-permute-start(bf16[16,16,1024]{2,1,0:T(8,128)(2,1)} %collective-permute-done.21.refs_4_), channel_id=1, source_target_pairs={{2,0},{4,2},{6,4},{7,6},{5,7},{3,5},{1,3},{0,1},{10,8},{12,10},{14... | collective-permute-start | bytes 1572872 | tf_op jit(solution)/shard_map/ppermute | solution.py:431
  344.1 33.6 %collective-permute-start.36 = (bf16[16,16,1024]{2,1,0:T(8,128)(2,1)}, bf16[16,16,1024]{2,1,0:T(8,128)(2,1)}, u32[]{:S(2)}, u32[]{:S(2)}) collective-permute-start(bf16[16,16,1024]{2,1,0:T(8,128)(2,1)} %collective-permute-done.35.refs_4_), channel_id=1, source_target_pairs={{2,0},{4,2},{6,4},{7,6},{5,7},{3,5},{1,3},{0,1},{10,8},{12,10},{14... | collective-permute-start | bytes 1572872 | tf_op jit(solution)/shard_map/ppermute | solution.py:431
  358.7 28.5 %collective-permute-start.43 = (bf16[16,16,1024]{2,1,0:T(8,128)(2,1)S(1)}, bf16[16,16,1024]{2,1,0:T(8,128)(2,1)S(1)}, u32[]{:S(2)}, u32[]{:S(2)}) collective-permute-start(bf16[16,16,1024]{2,1,0:T(8,128)(2,1)S(1)} %copy-done.50), channel_id=1, source_target_pairs={{0,2},{2,4},{4,6},{6,7},{7,5},{5,3},{3,1},{1,0},{8,10},{10,12},{12... | collective-permute-start | bytes 1572872 | tf_op jit(solution)/shard_map/ppermute | solution.py:431
  366.5 31.2 %collective-permute-start.16 = (bf16[16,16,1024]{2,1,0:T(8,128)(2,1)}, bf16[16,16,1024]{2,1,0:T(8,128)(2,1)S(1)}, u32[]{:S(2)}, u32[]{:S(2)}) collective-permute-start(bf16[16,16,1024]{2,1,0:T(8,128)(2,1)} %collective-permute-done.15.refs_5_), channel_id=1, source_target_pairs={{0,2},{2,4},{4,6},{6,7},{7,5},{5,3},{3,1},{1,0},{8,10},{10,12},{12... | collective-permute-start | bytes 1572872 | tf_op jit(solution)/shard_map/ppermute | solution.py:431
  379.3 32.0 %collective-permute-start.23 = (bf16[16,16,1024]{2,1,0:T(8,128)(2,1)}, bf16[16,16,1024]{2,1,0:T(8,128)(2,1)}, u32[]{:S(2)}, u32[]{:S(2)}) collective-permute-start(bf16[16,16,1024]{2,1,0:T(8,128)(2,1)} %collective-permute-done.22.refs_3_), channel_id=1, source_target_pairs={{2,0},{4,2},{6,4},{7,6},{5,7},{3,5},{1,3},{0,1},{10,8},{12,10},{14... | collective-permute-start | bytes 1572872 | tf_op jit(solution)/shard_map/ppermute | solution.py:431
  387.3 39.4 %collective-permute-start.30 = (bf16[16,16,1024]{2,1,0:T(8,128)(2,1)}, bf16[16,16,1024]{2,1,0:T(8,128)(2,1)}, u32[]{:S(2)}, u32[]{:S(2)}) collective-permute-start(bf16[16,16,1024]{2,1,0:T(8,128)(2,1)} %collective-permute-done.29.refs_5_), channel_id=1, source_target_pairs={{0,2},{2,4},{4,6},{6,7},{7,5},{5,3},{3,1},{1,0},{8,10},{10,12},{12... | collective-permute-start | bytes 1572872 | tf_op jit(solution)/shard_map/ppermute | solution.py:431
  389.2 37.5 %collective-permute-start.37 = (bf16[16,16,1024]{2,1,0:T(8,128)(2,1)}, bf16[16,16,1024]{2,1,0:T(8,128)(2,1)}, u32[]{:S(2)}, u32[]{:S(2)}) collective-permute-start(bf16[16,16,1024]{2,1,0:T(8,128)(2,1)} %collective-permute-done.36.refs_3_), channel_id=1, source_target_pairs={{2,0},{4,2},{6,4},{7,6},{5,7},{3,5},{1,3},{0,1},{10,8},{12,10},{14... | collective-permute-start | bytes 1572872 | tf_op jit(solution)/shard_map/ppermute | solution.py:431
  400.1 31.2 %collective-permute-start.17 = (bf16[16,16,1024]{2,1,0:T(8,128)(2,1)S(1)}, bf16[16,16,1024]{2,1,0:T(8,128)(2,1)S(1)}, u32[]{:S(2)}, u32[]{:S(2)}) collective-permute-start(bf16[16,16,1024]{2,1,0:T(8,128)(2,1)S(1)} %collective-permute-done.16.refs_6_), channel_id=1, source_target_pairs={{0,2},{2,4},{4,6},{6,7},{7,5},{5,3},{3,1},{1,0},{8,10},{10,12},{12... | collective-permute-start | bytes 1572872 | tf_op jit(solution)/shard_map/ppermute | solution.py:431
  426.7 62.2 %collective-permute-start.24 = (bf16[16,16,1024]{2,1,0:T(8,128)(2,1)}, bf16[16,16,1024]{2,1,0:T(8,128)(2,1)}, u32[]{:S(2)}, u32[]{:S(2)}) collective-permute-start(bf16[16,16,1024]{2,1,0:T(8,128)(2,1)} %collective-permute-done.23.refs_2_), channel_id=1, source_target_pairs={{2,0},{4,2},{6,4},{7,6},{5,7},{3,5},{1,3},{0,1},{10,8},{12,10},{14... | collective-permute-start | bytes 1572872 | tf_op jit(solution)/shard_map/ppermute | solution.py:431
  426.8 50.2 %collective-permute-start.31 = (bf16[16,16,1024]{2,1,0:T(8,128)(2,1)}, bf16[16,16,1024]{2,1,0:T(8,128)(2,1)}, u32[]{:S(2)}, u32[]{:S(2)}) collective-permute-start(bf16[16,16,1024]{2,1,0:T(8,128)(2,1)} %collective-permute-done.30.refs_6_), channel_id=1, source_target_pairs={{0,2},{2,4},{4,6},{6,7},{7,5},{5,3},{3,1},{1,0},{8,10},{10,12},{12... | collective-permute-start | bytes 1572872 | tf_op jit(solution)/shard_map/ppermute | solution.py:431
  431.3 34.0 %collective-permute-start.38 = (bf16[16,16,1024]{2,1,0:T(8,128)(2,1)}, bf16[16,16,1024]{2,1,0:T(8,128)(2,1)}, u32[]{:S(2)}, u32[]{:S(2)}) collective-permute-start(bf16[16,16,1024]{2,1,0:T(8,128)(2,1)} %collective-permute-done.37.refs_2_), channel_id=1, source_target_pairs={{2,0},{4,2},{6,4},{7,6},{5,7},{3,5},{1,3},{0,1},{10,8},{12,10},{14... | collective-permute-start | bytes 1572872 | tf_op jit(solution)/shard_map/ppermute | solution.py:431
  442.0 59.9 %all-to-all-start.1 = ((bf16[4,8,32,128]{3,2,1,0:T(8,128)(2,1)}), bf16[4,8,32,128]{3,2,1,0:T(8,128)(2,1)}, u32[]{:S(2)}, u32[]{:S(2)}) async-start(bf16[4,8,32,128]{3,2,1,0:T(8,128)(2,1)} %bitcast.96), calls=%async_computation.1 | async-start | bytes 524288 | tf_op jit(solution)/shard_map/all_to_all | solution.py:443
  (116 other events, 1300.9 us)

commit v2 on v1

v2 whole, which is shorter than its diff:
```python
import functools
import math

import jax
import jax.numpy as jnp
from jax import lax
from jax.experimental import pallas as pl
from jax.experimental.pallas import tpu as pltpu
from jax.sharding import PartitionSpec as P

A = 1024
FOURIER_LENGTH = 1024
NCH = 512
FILTER_TAPS = 8
BEAMS = 256
LANES = 128
UNITS = 32
CHUNKS = (4, 6, 6, 6, 4, 2, 2, 2)
LONG = 6
BLOCK = 4
HALVES = 2
VMEM = pl.BlockSpec(memory_space=pltpu.VMEM)
HBM = pl.BlockSpec(memory_space=pltpu.HBM)


def params(mib):
    return pltpu.CompilerParams(vmem_limit_bytes=mib * 2**20)


def cost(flops, bytes_accessed):
    return pl.CostEstimate(flops=int(3 * flops), bytes_accessed=int(3 * bytes_accessed), transcendentals=0)


def from_behind(block, axis, distance):
    devices = range(lax.axis_size(axis))
    route = [(i - distance, i) for i in devices if i - distance in devices]
    return lax.ppermute(block, axis, route)


def tap_table():
    position = jnp.arange(FILTER_TAPS * FOURIER_LENGTH, dtype=jnp.int32).astype(jnp.float32) + 0.5
    centred = position / FOURIER_LENGTH - FILTER_TAPS / 2.0
    window = 0.5 - 0.5 * jnp.cos(2.0 * math.pi * position / (FILTER_TAPS * FOURIER_LENGTH))
    return (jnp.sinc(centred) * window).reshape(FILTER_TAPS, FOURIER_LENGTH)


def dft_rows(channel_number):
    chan_ids = jnp.arange(NCH, dtype=jnp.int32).reshape(channel_number, 1, -1, 1)
    sample_ids = jnp.arange(FOURIER_LENGTH, dtype=jnp.int32)
    phase_angle = (chan_ids * sample_ids % FOURIER_LENGTH).astype(jnp.float32) * (
        2.0 * math.pi / FOURIER_LENGTH
    )
    scale = 1.0 / math.sqrt(FOURIER_LENGTH)
    table = jnp.concatenate([jnp.cos(phase_angle) * scale, -jnp.sin(phase_angle) * scale], axis=1)
    return table.astype(jnp.bfloat16).reshape(channel_number, -1, FOURIER_LENGTH)


def synth_table():
    chan_ids = jnp.arange(NCH, dtype=jnp.int32)
    sample_ids = jnp.arange(FOURIER_LENGTH, dtype=jnp.int32)
    phase_angle = (chan_ids[:, None] * sample_ids[None, :] % FOURIER_LENGTH).astype(jnp.float32) * (
        2.0 * math.pi / FOURIER_LENGTH
    )
    scale = 1.0 / math.sqrt(NCH)
    return jnp.stack([jnp.cos(phase_angle) * scale, -jnp.sin(phase_angle) * scale], axis=0).astype(
        jnp.bfloat16
    )


def phasor(delays, chan_ids, scale):
    angle = (delays * chan_ids % FOURIER_LENGTH).astype(jnp.float32) * (
        2.0 * math.pi / FOURIER_LENGTH
    )
    return jnp.cos(angle) * scale, -jnp.sin(angle) * scale


def front_kernel(rows, steps, fold, parcels, place, samples, before, history, taps, table, *refs):
    outs, (filtered, wide) = refs[:-2], refs[-2:]
    step = pl.program_id(0)
    frames = samples.shape[1] // FOURIER_LENGTH
    past = FILTER_TAPS - 1
    group = min(16, rows)
    antennas = filtered.shape[1] // fold

    @pl.when(step < steps)
    def _():
        first = place[1] == 0

        def columns(i, carry):
            at = pl.multiple_of(i * LANES, LANES)
            weights = [
                jnp.broadcast_to(taps[t : t + 1, pl.ds(at, LANES)], (group, LANES))
                for t in range(FILTER_TAPS)
            ]
            for g in range(rows // group):
                here = slice(g * group, (g + 1) * group)
                values = []
                for frame in range(past):
                    lanes = pl.ds(at + frame * FOURIER_LENGTH, LANES)
                    values.append(
                        jnp.where(
                            first,
                            history[here, lanes].astype(jnp.float32),
                            before[here, lanes].astype(jnp.float32),
                        )
                    )
                for frame in range(frames):
                    lanes = pl.ds(at + frame * FOURIER_LENGTH, LANES)
                    values.append(samples[here, lanes].astype(jnp.float32))
                for frame in range(frames):
                    total = values[frame] * weights[0]
                    for t in range(1, FILTER_TAPS):
                        total = total + values[frame + t] * weights[t]
                    to = (frame % fold) * antennas + g * group
                    filtered[frame // fold, pl.ds(step * rows + to, group), pl.ds(at, LANES)] = (
                        total.astype(jnp.bfloat16)
                    )
            return carry

        lax.fori_loop(0, FOURIER_LENGTH // LANES, columns, 0)

    count = table.shape[0] // 2
    for m in range(len(outs) // len(parcels)):

        @pl.when(step == steps + m)
        def _(m=m):
            for several in range(frames // fold):
                got = lax.dot_general(
                    table[...],
                    filtered[several],
                    (((1,), (1,)), ((), ())),
                    preferred_element_type=jnp.float32,
                )
                for part in range(fold):
                    frame = several * fold + part
                    lanes = slice(part * antennas, (part + 1) * antennas)
                    wide[pl.ds(frame, count, stride=2 * frames), :] = got[:count, lanes]
                    wide[pl.ds(frames + frame, count, stride=2 * frames), :] = got[count:, lanes]
            start = 0
            for p, size in enumerate(parcels):
                outs[m * len(parcels) + p][...] = wide[
                    start * 2 * frames : (start + size) * 2 * frames, :
                ].astype(jnp.bfloat16)
                start += size


def front(samples, before, history, place, taps, table, half, parcels):
    antennas = before.shape[0]
    length = samples.shape[1]
    frames = length // FOURIER_LENGTH
    channel_number, channel_total = table.shape[0], table.shape[1] // 2
    rows = min(32, antennas)
    steps = antennas // rows
    fold = math.gcd(frames, max(1, 256 // antennas))
    past = (FILTER_TAPS - 1) * FOURIER_LENGTH
    grid_spec = pltpu.PrefetchScalarGridSpec(
        num_scalar_prefetch=1,
        grid=(steps + channel_number,),
        in_specs=[
            pl.BlockSpec(
                (rows, length), lambda i, s: (half * steps + jnp.minimum(i, steps - 1), 0)
            ),
            pl.BlockSpec((rows, past), lambda i, s: (jnp.minimum(i, steps - 1), 0)),
            pl.BlockSpec(
                (rows, past), lambda i, s: (half * steps + jnp.minimum(i, steps - 1), 0)
            ),
            VMEM,
            pl.BlockSpec(
                (None, 2 * channel_total, FOURIER_LENGTH),
                lambda i, s: (lax.rem(s[0] + jnp.maximum(i - steps, 0), channel_number), 0, 0),
            ),
        ],
        out_specs=[VMEM] * (channel_number * len(parcels)),
        scratch_shapes=[
            pltpu.VMEM((frames // fold, fold * antennas, FOURIER_LENGTH), jnp.bfloat16),
            pltpu.VMEM((channel_total * 2 * frames, antennas), jnp.float32),
        ],
    )
    return pl.pallas_call(
        functools.partial(front_kernel, rows, steps, fold, parcels),
        grid_spec=grid_spec,
        out_shape=[
            jax.ShapeDtypeStruct((size * 2 * frames, antennas), jnp.bfloat16)
            for _ in range(channel_number)
            for size in parcels
        ],
        compiler_params=params(16),
        cost_estimate=cost(2 * antennas * frames * FOURIER_LENGTH * 2 * NCH * 2, 8 * 2**20),
        name="front",
    )(place, samples, before, history, taps, table)


def order_kernel(number, halves, *refs):
    pieces, spread, out = refs[:-2], refs[-2], refs[-1]
    total = None
    for m in range(number):
        left = jnp.concatenate(
            [piece[...] for piece in pieces[m * halves : (m + 1) * halves]], axis=1
        )
        got = jnp.dot(left, spread[m], preferred_element_type=jnp.float32)
        total = got if total is None else total + got
    out[...] = total.astype(jnp.bfloat16)


def into_order(pieces, halves, spread, block, blocks):
    number = len(pieces) // halves
    rows = block * blocks
    width = spread.shape[2]
    return pl.pallas_call(
        functools.partial(order_kernel, number, halves),
        grid=(blocks,),
        in_specs=[
            pl.BlockSpec((block, p.shape[1]), lambda i, at=at: (at // block + i, 0))
            for p, at in pieces
        ]
        + [VMEM],
        out_specs=pl.BlockSpec((block, width), lambda i: (i, 0)),
        out_shape=jax.ShapeDtypeStruct((rows, width), jnp.bfloat16),
        compiler_params=params(10),
        cost_estimate=cost(2 * rows * width * width, rows * width * 4),
        name="into_order",
    )(*[p for p, _ in pieces], spread)


def spread_table(antenna_flags, chan_id, channel_number, block_list):
    per_shard = A // (channel_number * block_list)
    block = (chan_id - jnp.arange(channel_number, dtype=jnp.int32)) % channel_number
    own = jnp.arange(block_list * per_shard, dtype=jnp.int32)
    target = (
        (own // per_shard) * (A // block_list) + block[:, None] * per_shard + own % per_shard
    )
    hit = target[:, :, None] == jnp.arange(A, dtype=jnp.int32)
    return jnp.where(hit, antenna_flags, 0).astype(jnp.bfloat16)


def products_kernel(ends, frames, aliased, seen, formed, place, *refs):
    number = len(ends)
    count = sum(map(len, ends))
    pieces = iter(refs[:count])
    sources = [[next(pieces) for _ in slot] for slot in ends]
    base_re, base_im, step_re, step_im = refs[count : count + 4] if formed else [None] * 4
    outs = refs[count + 4 * formed + aliased :]
    out = outs[0] if seen else None
    beam_out, state_re, state_im = outs[seen:] if formed else [None] * 3
    block, rows = sources[0][0].shape[:2]
    half = rows // 2
    step = pl.program_id(0)

    if formed:

        @pl.when(step == 0)
        def _():
            state_re[...] = base_re[...]
            state_im[...] = base_im[...]

    def slots(i, lanes):
        found = []
        for slot, end in zip(sources, ends):
            value = slot[-1][i, :, lanes]
            for source, last in zip(slot[-2::-1], end[-2::-1]):
                value = jnp.where(step < last, source[i, :, lanes], value)
            found.append(value)
        return jnp.concatenate(found, axis=0)

    def visibilities(i, everything):
        row_count = out.shape[2]
        own_lanes = pl.ds(pl.multiple_of(place[1] * row_count, row_count), row_count)
        wide = slots(i, own_lanes).astype(jnp.float32)
        swapped = jnp.concatenate(
            [
                part
                for s in range(number)
                for part in (
                    wide[(2 * s + 1) * half : (2 * s + 2) * half],
                    -wide[2 * s * half : (2 * s + 1) * half],
                )
            ],
            axis=0,
        )
        left = jnp.concatenate([wide.T, swapped.T], axis=0).astype(jnp.bfloat16)
        got = jnp.dot(left, everything, preferred_element_type=jnp.float32)
        got = (got * (1.0 / frames)).astype(jnp.bfloat16)
        out[i, 0] = got[:row_count]
        out[i, 1] = got[row_count:]

    def beams(i, everything):
        now_re, now_im = state_re[...], state_im[...]
        weights = jnp.concatenate([now_re, now_im], axis=0).astype(jnp.bfloat16)
        state_re[...] = now_re * step_re[...] - now_im * step_im[...]
        state_im[...] = now_re * step_im[...] + now_im * step_re[...]
        got = lax.dot_general(
            weights, everything, (((1,), (1,)), ((), ())), preferred_element_type=jnp.float32
        )
        direct, crossed = jnp.split(got, 2, axis=0)
        width = got.shape[1]
        lane = lax.broadcasted_iota(jnp.int32, crossed.shape, 1)
        real_lane = lax.rem(lane, 2 * half) < half
        crossed = jnp.where(
            real_lane,
            -pltpu.roll(crossed, width - half, 1),
            pltpu.roll(crossed, half, 1),
        )
        beam_out[i] = (direct + crossed).astype(jnp.bfloat16)

    for i in range(block):
        everything = slots(i, slice(None))
        if seen:
            visibilities(i, everything)
        if formed:
            beams(i, everything)


def products_of(
    pieces, place, target, weights, first, count, channel_total, row_count, frames, seen, formed
):
    number = len(pieces)
    rows = pieces[0][0][0].shape[1]
    beams = weights[0].shape[0]
    block = math.gcd(first, BLOCK, *[n for slot in pieces for _, _, n in slot])
    ends = [[sum(n for _, _, n in slot[: c + 1]) // block for c in range(len(slot))] for slot in pieces]
    in_specs = []
    for slot, end in zip(pieces, ends):
        for (_, at, n), last in zip(slot, end):
            begin = last - n // block
            in_specs.append(
                pl.BlockSpec(
                    (block, rows, A),
                    lambda i, s, at=at // block, begin=begin, last=last: (
                        at + jnp.clip(i, begin, last - 1) - begin,
                        0,
                        0,
                    ),
                )
            )
    pieces = [p for slot in pieces for p, _, _ in slot]
    offset = first // block
    aliased = seen and target is not None
    out_specs, out_shape = [], []
    if seen:
        out_specs.append(
            pl.BlockSpec((block, 2, row_count, A), lambda i, s: (i + offset, 0, 0, 0))
        )
        out_shape.append(
            jax.ShapeDtypeStruct((channel_total, 2, row_count, A), jnp.bfloat16)
        )
    if formed:
        out_specs.append(pl.BlockSpec((block, beams, number * rows), lambda i, s: (i, 0, 0)))
        out_shape.append(jax.ShapeDtypeStruct((count, beams, number * rows), jnp.bfloat16))
    others = [*weights] * formed + [target] * aliased
    return pl.pallas_call(
        functools.partial(products_kernel, ends, frames, aliased, seen, formed),
        grid_spec=pltpu.PrefetchScalarGridSpec(
            num_scalar_prefetch=1,
            grid=(count // block,),
            in_specs=in_specs
            + [pl.BlockSpec((beams, A), lambda i, s: (0, 0))] * (4 * formed)
            + [HBM] * aliased,
            out_specs=out_specs,
            scratch_shapes=[pltpu.VMEM((beams, A), jnp.float32)] * (2 * formed),
        ),
        out_shape=out_shape,
        input_output_aliases={1 + len(pieces) + 4 * formed: 0} if aliased else {},
        compiler_params=params(10),
        cost_estimate=cost(12 * count * row_count * A * 256, count * row_count * A * 6),
        name="products",
    )(place, *pieces, *others)


def synthesis_kernel(number, half, owners, spectra, table, out):
    got = [
        lax.dot_general(
            spectra[...], table[e], (((0,), (0,)), ((), ())), preferred_element_type=jnp.float32
        )
        for e in range(2)
    ]
    for s in range(number):
        real, imag = 2 * s * half, (2 * s + 1) * half
        rows = pl.ds(pl.multiple_of(owners[s] * half, half), half)
        out[rows, :] = got[0][real : real + half] + got[1][imag : imag + half]


def synthesis(spectra, table, owners, frames):
    beam_count, channels, width = spectra.shape
    number = owners.shape[0]
    return pl.pallas_call(
        functools.partial(synthesis_kernel, number, frames // number),
        grid_spec=pltpu.PrefetchScalarGridSpec(
            num_scalar_prefetch=1,
            grid=(beam_count,),
            in_specs=[pl.BlockSpec((None, channels, width), lambda i, s: (i, 0, 0)), VMEM],
            out_specs=pl.BlockSpec((None, frames, FOURIER_LENGTH), lambda i, s: (i, 0, 0)),
        ),
        out_shape=jax.ShapeDtypeStruct((beam_count, frames, FOURIER_LENGTH), jnp.float32),
        compiler_params=params(10),
        cost_estimate=cost(4 * beam_count * channels * width * FOURIER_LENGTH, 8 * 2**20),
        name="synthesis",
    )(owners, spectra, table)


def body(samples, history, antenna_flags, beam_delays):
    channel_number = lax.axis_size("chan")
    n_row = lax.axis_size("row")
    chan_id = lax.axis_index("chan")
    row_id = lax.axis_index("row")
    block_list, antennas_per_shard, shard_length = samples.shape
    frames_per_shard = shard_length // FOURIER_LENGTH
    frames = frames_per_shard * n_row
    channel_total = NCH // channel_number
    row_count = A // n_row
    beam_count = BEAMS // (channel_number * n_row)
    antennas = block_list * antennas_per_shard
    unit = channel_total // UNITS
    rows_of = 2 * frames_per_shard
    place = jnp.stack([chan_id, row_id]).astype(jnp.int32)

    cycle = [i for i in range(n_row) if i % 2 == 0] + [i for i in reversed(range(n_row)) if i % 2]
    onward = [(cycle[i], cycle[(i + 1) % n_row]) for i in range(n_row)]
    backward = [(b, a) for a, b in onward]
    position = jnp.array([cycle.index(i) for i in range(n_row)], jnp.int32)[row_id]
    owners = jnp.array(cycle, jnp.int32)[
        (position - jnp.arange(n_row, dtype=jnp.int32)) % n_row
    ]

    past = (FILTER_TAPS - 1) * FOURIER_LENGTH
    blocks = block_list // HALVES
    before = [
        from_behind(samples[h * blocks : (h + 1) * blocks, :, shard_length - past :], "row", 1)
        for h in range(HALVES)
    ]
    delays = lax.dynamic_index_in_dim(
        beam_delays.reshape(channel_number, n_row, beam_count, A), row_id, 1, keepdims=False
    ).reshape(channel_number * beam_count, A)
    sizes = [size * unit for size in CHUNKS]
    firsts = [sum(sizes[:i]) for i in range(len(sizes))]
    calls = []
    for i, (at, size) in enumerate(zip(firsts, sizes)):
        parts = 2 if size >= LONG * unit else 1
        calls += [(i, at + d * (size // 2), size // parts) for d in range(parts)]
    starts = chan_id * channel_total + jnp.array([at for _, at, _ in calls], jnp.int32)
    base_re, base_im = phasor(delays[None], starts[:, None, None], 1.0 / math.sqrt(A))
    step_re, step_im = phasor(delays, 1, 1.0)
    back = synth_table()
    spread = spread_table(antenna_flags, chan_id, channel_number, block_list)

    taps, table = tap_table(), dft_rows(channel_number)
    arrived = []
    for h in range(HALVES):
        if h == HALVES - 1:
            ahead = [p for m in range(1, channel_number) for p, _ in arrived[0][m]]
            before[h], spread, owners, base_re, base_im, step_re, step_im, back, *ahead = (
                lax.optimization_barrier(
                    (before[h], spread, owners, base_re, base_im, step_re, step_im, back, *ahead)
                )
            )
            arrived[0][1:] = [[(p, 0)] for p in ahead]
        parcels = [channel_total]
        if h == HALVES - 1:
            parcels = sizes[:2] + [channel_total - sum(sizes[:2])]
        sent = front(
            samples.reshape(antennas, -1),
            before[h].reshape(antennas // HALVES, -1),
            history.reshape(antennas, -1),
            place,
            taps,
            table,
            h,
            parcels,
        )
        arrived.append([])
        for m in range(channel_number):
            route = [(i, (i + m) % channel_number) for i in range(channel_number)]
            start = 0
            arrived[h].append([])
            for p, size in enumerate(parcels):
                piece = sent[m * len(parcels) + p]
                arrived[h][m].append((lax.ppermute(piece, "chan", route) if m else piece, start))
                start += size
    def chunk_of(i, halves):
        at = firsts[i]
        pieces = []
        for m in range(channel_number):
            for h in halves:
                piece, start = [(p, s) for p, s in arrived[h][m] if s <= at][-1]
                pieces.append((piece, (at - start) * rows_of))
        table = spread if len(halves) > 1 else spread_of_half[halves[0]]
        chunk = into_order(pieces, len(halves), table, unit * rows_of, CHUNKS[i])
        return chunk.reshape(CHUNKS[i] * unit, rows_of, -1)

    whole_steps = (n_row - 1) // 2
    steps = n_row // 2
    everyone = tuple(range(HALVES))
    lanes = [[(i, everyone) for i in range(lane, len(CHUNKS), 2)] for lane in range(2)]
    order = []
    for pair in zip(*lanes):
        for step in range(steps):
            order += [(chunk, step) for chunk in pair]
    passed = {}
    for chunk, _ in order:
        if chunk not in passed:
            start = chunk_of(*chunk)
            passed[chunk] = [[start], [start]]

    def slots_of(i, first, count):
        shift, half = first - firsts[i], sizes[i] // 2
        onwards, backwards = passed[i, everyone]
        held = [[(p, shift, count)] for p in onwards[: whole_steps + 1]]
        if steps > whole_steps:
            far = [(w[-1], 0, half) for w in (onwards, backwards)]
            held.append(far if count > half else far[shift // half :][:1])
        return held + [[(p, shift, count)] for p in backwards[whole_steps:0:-1]]

    visibilities = None
    beams = {}
    waiting = []

    def products(j, seen=True, formed=True):
        nonlocal visibilities
        made = products_of(
            slots_of(*calls[j]),
            place,
            visibilities,
            (base_re[j], base_im[j], step_re, step_im),
            *calls[j][1:],
            channel_total,
            row_count,
            frames,
            seen,
            formed,
        )
        if seen:
            visibilities = made[0]
        if formed:
            beams[j] = made[-1]
        return made

    def to_owners(group):
        value = jnp.concatenate([beams[j] for j in group], axis=0)
        value = value.reshape(-1, channel_number, beam_count, 2 * frames).transpose(1, 2, 0, 3)
        return lax.all_to_all(value, "chan", split_axis=0, concat_axis=0, tiled=True)

    groups = [
        [j for j, (i, _, _) in enumerate(calls) if low <= i < high]
        for low, high in ((0, 4), (4, len(CHUNKS)))
    ]
    arrived_beams = {}

    sent = {}
    for n, (chunk, step) in enumerate(order):
        lane = chunk[0] % 2
        going = [way[-1] for way in passed[chunk]]
        extra = list(sent.get(lane, []))
        if n == 2:
            extra += [arrived[-1][m][-1][0] for m in range(1, channel_number)]
        while waiting and waiting[0][0] <= n:
            j = waiting.pop(0)[1]
            held = lax.optimization_barrier((*going, *products(j), *extra))
            visibilities, beams[j] = held[2:4]
            for g, group in enumerate(groups):
                if j == group[-1]:
                    arrived_beams[g] = to_owners(group)
            going, extra = held[:2], []
        if extra:
            going = lax.optimization_barrier((*going, *extra))[:2]
        if step >= whole_steps:
            half = sizes[chunk[0]] // 2
            going = [going[0][:half], going[1][half:]]
        got = [lax.ppermute(p, "row", r) for p, r in zip(going, (onward, backward))]
        for d in range(2):
            passed[chunk][d].append(got[d])
        sent[lane] = got
        if step == steps - 1 and lane == 1:
            i = chunk[0]
            work = [j for j, call in enumerate(calls) if call[0] in (i - 1, i)]
            for k, j in enumerate(work):
                waiting.append((n + 1 + k * 2 * steps // len(work), j))

    left = [j for _, j in waiting]
    for j in left:
        products(j, seen=False)
    held = lax.optimization_barrier((visibilities, *[beams[j] for j in left]))
    visibilities = held[0]
    for j, value in zip(left, held[1:]):
        beams[j] = value
    for g, group in enumerate(groups):
        if g not in arrived_beams:
            arrived_beams[g] = to_owners(group)
    for j in left:
        products(j, formed=False)
    spectra = jnp.concatenate([arrived_beams[g] for g in range(len(groups))], axis=2)
    spectra = spectra.transpose(1, 0, 2, 3).reshape(beam_count, NCH, 2 * frames)
    beam_series = synthesis(spectra, back, owners, frames)
    return (visibilities, beam_series)


def solution(mesh):
    in_specs = (P(None, "chan", "row"), P(None, "chan", None), P(), P())
    out_specs = (P("chan", None, "row", None), P(("chan", "row"), None, None))
    return jax.shard_map(body, mesh=mesh, in_specs=in_specs, out_specs=out_specs, check_vma=False)
```

time: 532 us -> 484 us (0.910)
  waiting for transfers between devices: 250 us -> 226 us
  local copies, waits for them, and re-layouts: 39.3 us -> 21.8 us
  Pallas kernels: 119 us -> 105 us
  starting transfers between devices: 88.7 us -> 94.2 us
    ppermute x1 -> x2, waiting for transfers between devices: 66.1 us -> 32.5 us  [from_behind(): return lax.ppermute(block, axis, route)]
    unnamed x171 -> x66, local copies, waits for them, and re-layouts: 29 us -> 9.28 us
    pallas_call x19 -> x23, Pallas kernels: 113 us -> 99.3 us  [the longest x13 64.7 us: products_of(): pl.pallas_call(functools.partial(products_kernel, ends, frames, aliased,...]
    ppermute x62 -> x76, waiting for transfers between devices: 184 us -> 193 us  [the longest x64 182 us: body(): got = [lax.ppermute(p, 'row', r) for p, r in zip(going, (onward, backward))]]
    ppermute x62 -> x76, starting transfers between devices: 73.8 us -> 76.3 us  [the longest x64 69.2 us: body(): got = [lax.ppermute(p, 'row', r) for p, r in zip(going, (onward, backward))]]
  transfers between devices with their start and end apart: 65 -> 80, of which waited for: 29 -> 50; matrix products, arithmetic and copies ran while one was open for 7% -> 8% of each run, Pallas kernels for 18% -> 18%
where the time goes in v2:
time: 484 us; the launch traced here: 478 us
  waiting for transfers between devices  226 us (47%)
  Pallas kernels  105 us (22%)
  starting transfers between devices  94.2 us (19%)
  other arithmetic  29 us (6%)
  local copies, waits for them, and re-layouts  21.8 us (5%)
    ppermute x64, waiting for transfers between devices, body(): got = [lax.ppermute(p, 'row', r) for p, r in zip(going, (onward, backward))]  182 us
    ppermute x64, starting transfers between devices, body(): got = [lax.ppermute(p, 'row', r) for p, r in zip(going, (onward, backward))]  69.2 us
    pallas_call x13, Pallas kernels, products_of(): pl.pallas_call(functools.partial(products_kernel, ends, frames, aliased,...  64.7 us
    ppermute x2, waiting for transfers between devices, from_behind(): return lax.ppermute(block, axis, route)  32.5 us
    pallas_call x2, Pallas kernels, front(): pl.pallas_call(functools.partial(front_kernel, rows, steps, fold, parcels...  19 us
    another operation x2, other arithmetic  17.7 us
    pallas_call x8, Pallas kernels, into_order(): pl.pallas_call(functools.partial(order_kernel, number, halves), grid=(blo...  15.6 us
    ppermute x12, waiting for transfers between devices, body(): lax.ppermute(piece, 'chan', route)  11.1 us
  transfers between devices with their start and end apart: 80, of which 50 were waited for; matrix products, arithmetic and copies ran while one was open for 8% of the time, Pallas kernels for 18%

profile of v2, /device:TPU:0, one launch (start us, length us, event | category | flops | bytes accessed | tf_op | source)
XLA Modules:
  0.0 477.5 jit_solution(12053673694127244858)
XLA Ops:
  4.8 6.1 %collective-permute-start = (bf16[4,32,7168]{2,1,0:T(8,128)(2,1)}, bf16[4,32,7168]{2,1,0:T(8,128)(2,1)}, u32[]{:S(2)}, u32[]{:S(2)}) collective-permute-start(bf16[4,32,7168]{2,1,0:T(8,128)(2,1)} %get-tuple-element.257), channel_id=1, source_target_pairs={{0,1},{1,2},{2,3},{3,4},{4,5},{5,6},{6,7},{8,9},{9,10},{10,11},{11... | collective-permute-start | bytes 5505032 | tf_op jit(solution)/shard_map/ppermute | solution.py:37
  18.4 9.1 %multiply_convert_fusion.3 = (bf16[4,1,128,1024]{3,2,1,0:T(8,128)(2,1)S(1)}, bf16[4,1,128,1024]{3,2,1,0:T(8,128)(2,1)S(1)}) fusion(s32[4,128]{1,0:T(4,128)S(1)} %multiply_add_fusion.1), kind=kLoop, calls=%fused_computation.27 | loop fusion | flops 9961472 | bytes 2099200 | tf_op jit(solution)/shard_map/convert.2
  27.7 8.6 %multiply_convert_fusion = (bf16[1,512,1024]{2,1,0:T(8,128)(2,1)S(1)}, bf16[1,512,1024]{2,1,0:T(8,128)(2,1)S(1)}) fusion(), kind=kLoop, calls=%fused_computation.22 | loop fusion | flops 9961472 | bytes 2097152 | tf_op jit(solution)/shard_map/convert.1
  37.6 12.8 %collective-permute-done = bf16[4,32,7168]{2,1,0:T(8,128)(2,1)} collective-permute-done((bf16[4,32,7168]{2,1,0:T(8,128)(2,1)}, bf16[4,32,7168]{2,1,0:T(8,128)(2,1)}, u32[]{:S(2)}, u32[]{:S(2)}) %collective-permute-start) | collective-permute-done | bytes 1835040 | tf_op jit(solution)/shard_map/ppermute | solution.py:37
  50.4 9.5 %front.2 = (bf16[2048,128]{1,0:T(8,128)(2,1)S(1)}, bf16[2048,128]{1,0:T(8,128)(2,1)S(1)}, bf16[2048,128]{1,0:T(8,128)(2,1)S(1)}, bf16[2048,128]{1,0:T(8,128)(2,1)S(1)}) custom-call(s32[2]{0:T(128)S(1)} %pad_add_fusion.place, bf16[256,8192]{1,0:T(8,128)(2,1)S(1)} %bitcast.80, bf16[128,7168]{1,0:T(8,128)(2,1)} %bitcast.3.before, ...), custom_call_target="tpu_custom_call" | custom-call | flops 12884901888 | bytes 25165824 | tf_op jit(solution)/shard_map/front/pallas_call | solution.py:179
  63.0 5.7 %negate_multiply_fusion = (f32[11,32,1024]{2,1,0:T(8,128)S(1)}, f32[11,32,1024]{2,1,0:T(8,128)S(1)}) fusion(s32[11]{0:T(128)S(1)} %broadcast_add_fusion, s32[32,1024]{1,0:T(8,128)S(1)} %copy-done.26), kind=kLoop, calls=%fused_computation.35 | loop fusion | flops 6127616 | bytes 3014700 | tf_op jit(solution)/shard_map/mul | solution.py:74
  68.8 19.8 %collective-permute-done.1 = bf16[4,32,7168]{2,1,0:T(8,128)(2,1)} collective-permute-done((bf16[4,32,7168]{2,1,0:T(8,128)(2,1)}, bf16[4,32,7168]{2,1,0:T(8,128)(2,1)}, u32[]{:S(2)}, u32[]{:S(2)}) %collective-permute-start.1) | collective-permute-done | bytes 1835040 | tf_op jit(solution)/shard_map/ppermute | solution.py:37
  88.6 9.5 %front.3 = (bf16[256,128]{1,0:T(8,128)(2,1)S(1)}, bf16[384,128]{1,0:T(8,128)(2,1)S(1)}, bf16[1408,128]{1,0:T(8,128)(2,1)S(1)}, bf16[256,128]{1,0:T(8,128)(2,1)S(...) custom-call(s32[2]{0:T(128)S(1)} %pad_add_fusion.place, ...), custom_call_target="tpu_custom_call" | custom-call | flops 12884901888 | bytes 25165824 | tf_op jit(solution)/shard_map/front/pallas_call | solution.py:179
  120.8 8.9 %collective-permute-done.11.refs_1_ = bf16[24,16,1024]{2,1,0:T(8,128)(2,1)S(1)} collective-permute-done((bf16[24,16,1024]{2,1,0:T(8,128)(2,1)S(1)}, bf16[24,16,1024]{2,1,0:T(8,128)(2,1)S(1)}, u32[]{:S(2)}, u32[]{:S(2)}) %collective-permute-start.11) | collective-permute-done | bytes 786464 | tf_op jit(solution)/shard_map/ppermute | solution.py:567
  136.2 4.8 collective-permute-done.26.refs_1_
  147.0 21.1 %collective-permute-done.28.refs_2_ = bf16[16,16,1024]{2,1,0:T(8,128)(2,1)S(1)} collective-permute-done((bf16[16,16,1024]{2,1,0:T(8,128)(2,1)S(1)}, bf16[16,16,1024]{2,1,0:T(8,128)(2,1)S(1)}, u32[]{:S(2)}, u32[]{:S(2)}) %collective-permute-start.28) | collective-permute-done | bytes 524320 | tf_op jit(solution)/shard_map/ppermute | solution.py:567
  176.7 8.9 %collective-permute-done.30.refs_3_ = bf16[16,16,1024]{2,1,0:T(8,128)(2,1)S(1)} collective-permute-done((bf16[16,16,1024]{2,1,0:T(8,128)(2,1)S(1)}, bf16[16,16,1024]{2,1,0:T(8,128)(2,1)S(1)}, u32[]{:S(2)}, u32[]{:S(2)}) %collective-permute-start.30) | collective-permute-done | bytes 524320 | tf_op jit(solution)/shard_map/ppermute | solution.py:567
  195.4 7.1 %collective-permute-done.15.refs_3_ = bf16[24,16,1024]{2,1,0:T(8,128)(2,1)S(1)} collective-permute-done((bf16[24,16,1024]{2,1,0:T(8,128)(2,1)S(1)}, bf16[24,16,1024]{2,1,0:T(8,128)(2,1)S(1)}, u32[]{:S(2)}, u32[]{:S(2)}) %collective-permute-start.15) | collective-permute-done | bytes 786464 | tf_op jit(solution)/shard_map/ppermute | solution.py:567
  209.9 6.6 %products.13 = (bf16[128,2,128,1024]{3,2,1,0:T(8,128)(2,1)}, bf16[16,32,128]{2,1,0:T(8,128)(2,1)S(1)}) custom-call(s32[2]{0:T(128)S(1)} %pad_add_fusion.place, bf16[16,16,1024]{2,1,0:T(8,128)(2,1)S(1)} %bitcast.115, bf16[16,16,1024]{2,1,0:T(8,128)(2,1)S(1)} %collective-permute-done.26.refs_1_, bf16[16,16,1024]{2,1,0:T(8,128)(2,1)S(1)} %collective-permute-done.28.refs_2_, ...), custom_call_target="tpu_custom_call" | custom-call | flops 19327352832 | bytes 37748736 | tf_op jit(solution)/shard_map/products/pallas_call | solution.py:350
  220.5 5.4 %products.14 = (bf16[128,2,128,1024]{3,2,1,0:T(8,128)(2,1)}, bf16[12,32,128]{2,1,0:T(8,128)(2,1)S(1)}) custom-call(s32[2]{0:T(128)S(1)} %pad_add_fusion.place, bf16[24,16,1024]{2,1,0:T(8,128)(2,1)S(1)} %bitcast.88, bf16[24,16,1024]{2,1,0:T(8,128)(2,1)S(1)} %collective-permute-done.11.refs_1_, ...), custom_call_target="tpu_custom_call", output_to_operand_aliasing={{0}: (13, {})} | custom-call | flops 14495514624 | bytes 28311552 | tf_op jit(solution)/shard_map/products/pallas_call | solution.py:350
  225.9 11.0 %collective-permute-done.34.refs_1_ = bf16[24,16,1024]{2,1,0:T(8,128)(2,1)S(1)} collective-permute-done((bf16[24,16,1024]{2,1,0:T(8,128)(2,1)S(1)}, bf16[24,16,1024]{2,1,0:T(8,128)(2,1)S(1)}, u32[]{:S(2)}, u32[]{:S(2)}) %collective-permute-start.34) | collective-permute-done | bytes 786464 | tf_op jit(solution)/shard_map/ppermute | solution.py:567
  240.5 13.2 %collective-permute-done.19.refs_1_ = bf16[24,16,1024]{2,1,0:T(8,128)(2,1)S(1)} collective-permute-done((bf16[24,16,1024]{2,1,0:T(8,128)(2,1)S(1)}, bf16[24,16,1024]{2,1,0:T(8,128)(2,1)S(1)}, u32[]{:S(2)}, u32[]{:S(2)}) %collective-permute-start.19) | collective-permute-done | bytes 786464 | tf_op jit(solution)/shard_map/ppermute | solution.py:567
  257.4 13.2 %collective-permute-done.56.refs_2_ = bf16[24,16,1024]{2,1,0:T(8,128)(2,1)S(1)} collective-permute-done((bf16[24,16,1024]{2,1,0:T(8,128)(2,1)S(1)}, bf16[24,16,1024]{2,1,0:T(8,128)(2,1)S(1)}, u32[]{:S(2)}, u32[]{:S(2)}) %collective-permute-start.56) | collective-permute-done | bytes 786464 | tf_op jit(solution)/shard_map/ppermute | solution.py:567
  274.2 5.5 %products.15 = (bf16[128,2,128,1024]{3,2,1,0:T(8,128)(2,1)}, bf16[12,32,128]{2,1,0:T(8,128)(2,1)S(1)}) custom-call(s32[2]{0:T(128)S(1)} %pad_add_fusion.place, bf16[24,16,1024]{2,1,0:T(8,128)(2,1)S(1)} %bitcast.89, bf16[24,16,1024]{2,1,0:T(8,128)(2,1)S(1)} %collective-permute-done.11.refs_1_, ...), custom_call_target="tpu_custom_call", output_to_operand_aliasing={{0}: (13, {})} | custom-call | flops 14495514624 | bytes 28311552 | tf_op jit(solution)/shard_map/products/pallas_call | solution.py:350
  279.7 7.8 %collective-permute-done.21.refs_2_ = bf16[24,16,1024]{2,1,0:T(8,128)(2,1)S(1)} collective-permute-done((bf16[24,16,1024]{2,1,0:T(8,128)(2,1)S(1)}, bf16[24,16,1024]{2,1,0:T(8,128)(2,1)S(1)}, u32[]{:S(2)}, u32[]{:S(2)}) %collective-permute-start.21) | collective-permute-done | bytes 786464 | tf_op jit(solution)/shard_map/ppermute | solution.py:567
  291.1 13.2 %collective-permute-done.58.refs_3_ = bf16[24,16,1024]{2,1,0:T(8,128)(2,1)S(1)} collective-permute-done((bf16[24,16,1024]{2,1,0:T(8,128)(2,1)S(1)}, bf16[24,16,1024]{2,1,0:T(8,128)(2,1)S(1)}, u32[]{:S(2)}, u32[]{:S(2)}) %collective-permute-start.58) | collective-permute-done | bytes 786464 | tf_op jit(solution)/shard_map/ppermute | solution.py:567
  311.1 10.1 %collective-permute-done.36.refs_3_ = bf16[24,16,1024]{2,1,0:T(8,128)(2,1)S(1)} collective-permute-done((bf16[24,16,1024]{2,1,0:T(8,128)(2,1)S(1)}, bf16[24,16,1024]{2,1,0:T(8,128)(2,1)S(1)}, u32[]{:S(2)}, u32[]{:S(2)}) %collective-permute-start.36) | collective-permute-done | bytes 786464 | tf_op jit(solution)/shard_map/ppermute | solution.py:567
  325.0 4.6 collective-permute-done.60.refs_4_
  329.6 5.4 %products.16 = (bf16[128,2,128,1024]{3,2,1,0:T(8,128)(2,1)}, bf16[12,32,128]{2,1,0:T(8,128)(2,1)S(1)}) custom-call(s32[2]{0:T(128)S(1)} %pad_add_fusion.place, bf16[24,16,1024]{2,1,0:T(8,128)(2,1)S(1)} %bitcast.92, bf16[24,16,1024]{2,1,0:T(8,128)(2,1)S(1)} %collective-permute-done.34.refs_1_, ...), custom_call_target="tpu_custom_call", output_to_operand_aliasing={{0}: (13, {})} | custom-call | flops 14495514624 | bytes 28311552 | tf_op jit(solution)/shard_map/products/pallas_call | solution.py:350
  341.6 5.4 %products.17 = (bf16[128,2,128,1024]{3,2,1,0:T(8,128)(2,1)}, bf16[12,32,128]{2,1,0:T(8,128)(2,1)S(1)}) custom-call(s32[2]{0:T(128)S(1)} %pad_add_fusion.place, bf16[24,16,1024]{2,1,0:T(8,128)(2,1)S(1)} %bitcast.93, bf16[24,16,1024]{2,1,0:T(8,128)(2,1)S(1)} %collective-permute-done.34.refs_1_, ...), custom_call_target="tpu_custom_call", output_to_operand_aliasing={{0}: (13, {})} | custom-call | flops 14495514624 | bytes 28311552 | tf_op jit(solution)/shard_map/products/pallas_call | solution.py:350
  359.2 5.4 %products.18 = (bf16[128,2,128,1024]{3,2,1,0:T(8,128)(2,1)}, bf16[12,32,128]{2,1,0:T(8,128)(2,1)S(1)}) custom-call(s32[2]{0:T(128)S(1)} %pad_add_fusion.place, bf16[24,16,1024]{2,1,0:T(8,128)(2,1)S(1)} %bitcast.84, bf16[24,16,1024]{2,1,0:T(8,128)(2,1)S(1)} %collective-permute-done.19.refs_1_, ...), custom_call_target="tpu_custom_call", output_to_operand_aliasing={{0}: (13, {})} | custom-call | flops 14495514624 | bytes 28311552 | tf_op jit(solution)/shard_map/products/pallas_call | solution.py:350
  376.0 5.5 %products.19 = (bf16[128,2,128,1024]{3,2,1,0:T(8,128)(2,1)}, bf16[12,32,128]{2,1,0:T(8,128)(2,1)S(1)}) custom-call(s32[2]{0:T(128)S(1)} %pad_add_fusion.place, bf16[24,16,1024]{2,1,0:T(8,128)(2,1)S(1)} %bitcast.85, bf16[24,16,1024]{2,1,0:T(8,128)(2,1)S(1)} %collective-permute-done.19.refs_1_, ...), custom_call_target="tpu_custom_call", output_to_operand_aliasing={{0}: (13, {})} | custom-call | flops 14495514624 | bytes 28311552 | tf_op jit(solution)/shard_map/products/pallas_call | solution.py:350
  397.5 6.6 %products.20 = (bf16[128,2,128,1024]{3,2,1,0:T(8,128)(2,1)}, bf16[16,32,128]{2,1,0:T(8,128)(2,1)S(1)}) custom-call(s32[2]{0:T(128)S(1)} %pad_add_fusion.place, bf16[16,16,1024]{2,1,0:T(8,128)(2,1)S(1)} %bitcast.96, bf16[16,16,1024]{2,1,0:T(8,128)(2,1)S(1)} %collective-permute-done.62.refs_1_, ...), custom_call_target="tpu_custom_call", output_to_operand_aliasing={{0}: (14, {})} | custom-call | flops 19327352832 | bytes 37748736 | tf_op jit(solution)/shard_map/products/pallas_call | solution.py:350
  433.4 4.2 all-to-all-start
  454.0 4.5 products.24.refs_9_
  465.5 4.4 products.25
  471.3 5.8 %synthesis.1 = f32[8,64,1024]{2,1,0:T(8,128)} custom-call(s32[8]{0:T(128)S(1)} %gather_fusion, bf16[8,512,128]{2,1,0:T(8,128)(2,1)S(1)} %bitcast.110, bf16[2,512,1024]{2,1,0:T(8,128)(2,1)S(1)} %pad_maximum_fusion.1.table), custom_call_target="tpu_custom_call" | custom-call | flops 6442450944 | bytes 25165824 | tf_op jit(solution)/shard_map/synthesis/pallas_call | solution.py:385
  (262 shorter events, 206.0 us)
Async XLA Ops:
  4.8 45.6 %collective-permute-start = (bf16[4,32,7168]{2,1,0:T(8,128)(2,1)}, bf16[4,32,7168]{2,1,0:T(8,128)(2,1)}, u32[]{:S(2)}, u32[]{:S(2)}) collective-permute-start(bf16[4,32,7168]{2,1,0:T(8,128)(2,1)} %get-tuple-element.257), channel_id=1, source_target_pairs={{0,1},{1,2},{2,3},{3,4},{4,5},{5,6},{6,7},{8,9},{9,10},{10,11},{11... | collective-permute-start | bytes 5505032 | tf_op jit(solution)/shard_map/ppermute | solution.py:37
  10.9 77.7 %collective-permute-start.1 = (bf16[4,32,7168]{2,1,0:T(8,128)(2,1)}, bf16[4,32,7168]{2,1,0:T(8,128)(2,1)}, u32[]{:S(2)}, u32[]{:S(2)}) collective-permute-start(bf16[4,32,7168]{2,1,0:T(8,128)(2,1)} %get-tuple-element.256), channel_id=1, source_target_pairs={{0,1},{1,2},{2,3},{3,4},{4,5},{5,6},{6,7},{8,9},{9,10},{10,11},{11... | collective-permute-start | bytes 5505032 | tf_op jit(solution)/shard_map/ppermute | solution.py:37
  59.9 28.7 %collective-permute-start.2 = (bf16[2048,128]{1,0:T(8,128)(2,1)S(1)}, bf16[2048,128]{1,0:T(8,128)(2,1)S(1)}, u32[]{:S(2)}, u32[]{:S(2)}) collective-permute-start(bf16[2048,128]{1,0:T(8,128)(2,1)S(1)} %get-tuple-element.129), channel_id=1, source_target_pairs={{0,8},{8,16},{16,24},{24,0},{1,9},{9,17},{17,25},{25,1},{2,10},{10... | collective-permute-start | bytes 1572872 | tf_op jit(solution)/shard_map/ppermute | solution.py:476
  59.9 28.6 %collective-permute-start.3 = (bf16[2048,128]{1,0:T(8,128)(2,1)S(1)}, bf16[2048,128]{1,0:T(8,128)(2,1)S(1)}, u32[]{:S(2)}, u32[]{:S(2)}) collective-permute-start(bf16[2048,128]{1,0:T(8,128)(2,1)S(1)} %get-tuple-element.130), channel_id=1, source_target_pairs={{0,16},{8,24},{16,0},{24,8},{1,17},{9,25},{17,1},{25,9},{2,18},{10... | collective-permute-start | bytes 1572872 | tf_op jit(solution)/shard_map/ppermute | solution.py:476
  61.5 27.0 %collective-permute-start.4 = (bf16[2048,128]{1,0:T(8,128)(2,1)S(1)}, bf16[2048,128]{1,0:T(8,128)(2,1)S(1)}, u32[]{:S(2)}, u32[]{:S(2)}) collective-permute-start(bf16[2048,128]{1,0:T(8,128)(2,1)S(1)} %get-tuple-element.131), channel_id=1, source_target_pairs={{0,24},{8,0},{16,8},{24,16},{1,25},{9,1},{17,9},{25,17},{2,26},{10... | collective-permute-start | bytes 1572872 | tf_op jit(solution)/shard_map/ppermute | solution.py:476
  108.3 21.4 %collective-permute-start.11 = (bf16[24,16,1024]{2,1,0:T(8,128)(2,1)S(1)}, bf16[24,16,1024]{2,1,0:T(8,128)(2,1)S(1)}, u32[]{:S(2)}, u32[]{:S(2)}) collective-permute-start(bf16[24,16,1024]{2,1,0:T(8,128)(2,1)S(1)} %bitcast.86), channel_id=1, source_target_pairs={{0,2},{2,4},{4,6},{6,7},{7,5},{5,3},{3,1},{1,0},{8,10},{10,12},{12... | collective-permute-start | bytes 2359304 | tf_op jit(solution)/shard_map/ppermute | solution.py:567
  111.8 19.4 %collective-permute-start.12 = (bf16[24,16,1024]{2,1,0:T(8,128)(2,1)S(1)}, bf16[24,16,1024]{2,1,0:T(8,128)(2,1)S(1)}, u32[]{:S(2)}, u32[]{:S(2)}) collective-permute-start(bf16[24,16,1024]{2,1,0:T(8,128)(2,1)S(1)} %bitcast.87), channel_id=1, source_target_pairs={{2,0},{4,2},{6,4},{7,6},{5,7},{3,5},{1,3},{0,1},{10,8},{12,10},{14... | collective-permute-start | bytes 2359304 | tf_op jit(solution)/shard_map/ppermute | solution.py:567
  118.7 22.2 %collective-permute-start.26 = (bf16[16,16,1024]{2,1,0:T(8,128)(2,1)S(1)}, bf16[16,16,1024]{2,1,0:T(8,128)(2,1)S(1)}, u32[]{:S(2)}, u32[]{:S(2)}) collective-permute-start(bf16[16,16,1024]{2,1,0:T(8,128)(2,1)S(1)} %bitcast.113), channel_id=1, source_target_pairs={{0,2},{2,4},{4,6},{6,7},{7,5},{5,3},{3,1},{1,0},{8,10},{10,12},{12... | collective-permute-start | bytes 1572872 | tf_op jit(solution)/shard_map/ppermute | solution.py:567
  131.2 41.6 %collective-permute-start.13 = (bf16[24,16,1024]{2,1,0:T(8,128)(2,1)S(1)}, bf16[24,16,1024]{2,1,0:T(8,128)(2,1)S(1)}, u32[]{:S(2)}, u32[]{:S(2)}) collective-permute-start(bf16[24,16,1024]{2,1,0:T(8,128)(2,1)S(1)} %collective-permute-done.11.refs_1_), channel_id=1, source_target_pairs={{0,2},{2,4},{4,6},{6,7},{7,5},{5,3},{3,1},{1,0},{8,10},{10,12},{12... | collective-permute-start | bytes 2359304 | tf_op jit(solution)/shard_map/ppermute | solution.py:567
  132.6 40.2 %collective-permute-start.14 = (bf16[24,16,1024]{2,1,0:T(8,128)(2,1)S(1)}, bf16[24,16,1024]{2,1,0:T(8,128)(2,1)S(1)}, u32[]{:S(2)}, u32[]{:S(2)}) collective-permute-start(bf16[24,16,1024]{2,1,0:T(8,128)(2,1)S(1)} %collective-permute-done.12.refs_7_), channel_id=1, source_target_pairs={{2,0},{4,2},{6,4},{7,6},{5,7},{3,5},{1,3},{0,1},{10,8},{12,10},{14... | collective-permute-start | bytes 2359304 | tf_op jit(solution)/shard_map/ppermute | solution.py:567
  145.0 23.2 %collective-permute-start.28 = (bf16[16,16,1024]{2,1,0:T(8,128)(2,1)S(1)}, bf16[16,16,1024]{2,1,0:T(8,128)(2,1)S(1)}, u32[]{:S(2)}, u32[]{:S(2)}) collective-permute-start(bf16[16,16,1024]{2,1,0:T(8,128)(2,1)S(1)} %collective-permute-done.26.refs_1_), channel_id=1, source_target_pairs={{0,2},{2,4},{4,6},{6,7},{7,5},{5,3},{3,1},{1,0},{8,10},{10,12},{12... | collective-permute-start | bytes 1572872 | tf_op jit(solution)/shard_map/ppermute | solution.py:567
  147.0 23.8 %collective-permute-start.29 = (bf16[16,16,1024]{2,1,0:T(8,128)(2,1)S(1)}, bf16[16,16,1024]{2,1,0:T(8,128)(2,1)S(1)}, u32[]{:S(2)}, u32[]{:S(2)}) collective-permute-start(bf16[16,16,1024]{2,1,0:T(8,128)(2,1)S(1)} %collective-permute-done.27.refs_8_), channel_id=1, source_target_pairs={{2,0},{4,2},{6,4},{7,6},{5,7},{3,5},{1,3},{0,1},{10,8},{12,10},{14... | collective-permute-start | bytes 1572872 | tf_op jit(solution)/shard_map/ppermute | solution.py:567
  172.8 29.7 %collective-permute-start.15 = (bf16[24,16,1024]{2,1,0:T(8,128)(2,1)S(1)}, bf16[24,16,1024]{2,1,0:T(8,128)(2,1)S(1)}, u32[]{:S(2)}, u32[]{:S(2)}) collective-permute-start(bf16[24,16,1024]{2,1,0:T(8,128)(2,1)S(1)} %collective-permute-done.13.refs_2_), channel_id=1, source_target_pairs={{0,2},{2,4},{4,6},{6,7},{7,5},{5,3},{3,1},{1,0},{8,10},{10,12},{12... | collective-permute-start | bytes 2359304 | tf_op jit(solution)/shard_map/ppermute | solution.py:567
  174.6 29.7 %collective-permute-start.16 = (bf16[24,16,1024]{2,1,0:T(8,128)(2,1)S(1)}, bf16[24,16,1024]{2,1,0:T(8,128)(2,1)S(1)}, u32[]{:S(2)}, u32[]{:S(2)}) collective-permute-start(bf16[24,16,1024]{2,1,0:T(8,128)(2,1)S(1)} %collective-permute-done.14.refs_6_), channel_id=1, source_target_pairs={{2,0},{4,2},{6,4},{7,6},{5,7},{3,5},{1,3},{0,1},{10,8},{12,10},{14... | collective-permute-start | bytes 2359304 | tf_op jit(solution)/shard_map/ppermute | solution.py:567
  187.4 20.7 %collective-permute-start.32 = (bf16[8,16,1024]{2,1,0:T(8,128)(2,1)S(1)}, bf16[8,16,1024]{2,1,0:T(8,128)(2,1)S(1)}, u32[]{:S(2)}, u32[]{:S(2)}) collective-permute-start(bf16[8,16,1024]{2,1,0:T(8,128)(2,1)S(1)} %slice.126), channel_id=1, source_target_pairs={{0,2},{2,4},{4,6},{6,7},{7,5},{5,3},{3,1},{1,0},{8,10},{10,12},{12... | collective-permute-start | bytes 786440 | tf_op jit(solution)/shard_map/ppermute | solution.py:567
  189.1 20.8 %collective-permute-start.33 = (bf16[8,16,1024]{2,1,0:T(8,128)(2,1)S(1)}, bf16[8,16,1024]{2,1,0:T(8,128)(2,1)S(1)}, u32[]{:S(2)}, u32[]{:S(2)}) collective-permute-start(bf16[8,16,1024]{2,1,0:T(8,128)(2,1)S(1)} %slice.127), channel_id=1, source_target_pairs={{2,0},{4,2},{6,4},{7,6},{5,7},{3,5},{1,3},{0,1},{10,8},{12,10},{14... | collective-permute-start | bytes 786440 | tf_op jit(solution)/shard_map/ppermute | solution.py:567
  216.4 20.5 %collective-permute-start.34 = (bf16[24,16,1024]{2,1,0:T(8,128)(2,1)S(1)}, bf16[24,16,1024]{2,1,0:T(8,128)(2,1)S(1)}, u32[]{:S(2)}, u32[]{:S(2)}) collective-permute-start(bf16[24,16,1024]{2,1,0:T(8,128)(2,1)S(1)} %bitcast.90), channel_id=1, source_target_pairs={{0,2},{2,4},{4,6},{6,7},{7,5},{5,3},{3,1},{1,0},{8,10},{10,12},{12... | collective-permute-start | bytes 2359304 | tf_op jit(solution)/shard_map/ppermute | solution.py:567
  218.0 20.5 %collective-permute-start.35 = (bf16[24,16,1024]{2,1,0:T(8,128)(2,1)S(1)}, bf16[24,16,1024]{2,1,0:T(8,128)(2,1)S(1)}, u32[]{:S(2)}, u32[]{:S(2)}) collective-permute-start(bf16[24,16,1024]{2,1,0:T(8,128)(2,1)S(1)} %bitcast.91), channel_id=1, source_target_pairs={{2,0},{4,2},{6,4},{7,6},{5,7},{3,5},{1,3},{0,1},{10,8},{12,10},{14... | collective-permute-start | bytes 2359304 | tf_op jit(solution)/shard_map/ppermute | solution.py:567
  218.5 35.3 %collective-permute-start.19 = (bf16[24,16,1024]{2,1,0:T(8,128)(2,1)S(1)}, bf16[24,16,1024]{2,1,0:T(8,128)(2,1)S(1)}, u32[]{:S(2)}, u32[]{:S(2)}) collective-permute-start(bf16[24,16,1024]{2,1,0:T(8,128)(2,1)S(1)} %bitcast.82), channel_id=1, source_target_pairs={{0,2},{2,4},{4,6},{6,7},{7,5},{5,3},{3,1},{1,0},{8,10},{10,12},{12... | collective-permute-start | bytes 2359304 | tf_op jit(solution)/shard_map/ppermute | solution.py:567
  220.1 35.3 %collective-permute-start.20 = (bf16[24,16,1024]{2,1,0:T(8,128)(2,1)S(1)}, bf16[24,16,1024]{2,1,0:T(8,128)(2,1)S(1)}, u32[]{:S(2)}, u32[]{:S(2)}) collective-permute-start(bf16[24,16,1024]{2,1,0:T(8,128)(2,1)S(1)} %bitcast.83), channel_id=1, source_target_pairs={{2,0},{4,2},{6,4},{7,6},{5,7},{3,5},{1,3},{0,1},{10,8},{12,10},{14... | collective-permute-start | bytes 2359304 | tf_op jit(solution)/shard_map/ppermute | solution.py:567
  238.5 32.1 %collective-permute-start.56 = (bf16[24,16,1024]{2,1,0:T(8,128)(2,1)S(1)}, bf16[24,16,1024]{2,1,0:T(8,128)(2,1)S(1)}, u32[]{:S(2)}, u32[]{:S(2)}) collective-permute-start(bf16[24,16,1024]{2,1,0:T(8,128)(2,1)S(1)} %collective-permute-done.34.refs_1_), channel_id=1, source_target_pairs={{0,2},{2,4},{4,6},{6,7},{7,5},{5,3},{3,1},{1,0},{8,10},{10,12},{12... | collective-permute-start | bytes 2359304 | tf_op jit(solution)/shard_map/ppermute | solution.py:567
  240.1 32.2 %collective-permute-start.57 = (bf16[24,16,1024]{2,1,0:T(8,128)(2,1)S(1)}, bf16[24,16,1024]{2,1,0:T(8,128)(2,1)S(1)}, u32[]{:S(2)}, u32[]{:S(2)}) collective-permute-start(bf16[24,16,1024]{2,1,0:T(8,128)(2,1)S(1)} %collective-permute-done.35.refs_7_), channel_id=1, source_target_pairs={{2,0},{4,2},{6,4},{7,6},{5,7},{3,5},{1,3},{0,1},{10,8},{12,10},{14... | collective-permute-start | bytes 2359304 | tf_op jit(solution)/shard_map/ppermute | solution.py:567
  255.4 32.1 %collective-permute-start.21 = (bf16[24,16,1024]{2,1,0:T(8,128)(2,1)S(1)}, bf16[24,16,1024]{2,1,0:T(8,128)(2,1)S(1)}, u32[]{:S(2)}, u32[]{:S(2)}) collective-permute-start(bf16[24,16,1024]{2,1,0:T(8,128)(2,1)S(1)} %collective-permute-done.19.refs_1_), channel_id=1, source_target_pairs={{0,2},{2,4},{4,6},{6,7},{7,5},{5,3},{3,1},{1,0},{8,10},{10,12},{12... | collective-permute-start | bytes 2359304 | tf_op jit(solution)/shard_map/ppermute | solution.py:567
  256.9 32.2 %collective-permute-start.22 = (bf16[24,16,1024]{2,1,0:T(8,128)(2,1)S(1)}, bf16[24,16,1024]{2,1,0:T(8,128)(2,1)S(1)}, u32[]{:S(2)}, u32[]{:S(2)}) collective-permute-start(bf16[24,16,1024]{2,1,0:T(8,128)(2,1)S(1)} %collective-permute-done.20.refs_7_), channel_id=1, source_target_pairs={{2,0},{4,2},{6,4},{7,6},{5,7},{3,5},{1,3},{0,1},{10,8},{12,10},{14... | collective-permute-start | bytes 2359304 | tf_op jit(solution)/shard_map/ppermute | solution.py:567
  272.2 32.1 %collective-permute-start.58 = (bf16[24,16,1024]{2,1,0:T(8,128)(2,1)S(1)}, bf16[24,16,1024]{2,1,0:T(8,128)(2,1)S(1)}, u32[]{:S(2)}, u32[]{:S(2)}) collective-permute-start(bf16[24,16,1024]{2,1,0:T(8,128)(2,1)S(1)} %collective-permute-done.56.refs_2_), channel_id=1, source_target_pairs={{0,2},{2,4},{4,6},{6,7},{7,5},{5,3},{3,1},{1,0},{8,10},{10,12},{12... | collective-permute-start | bytes 2359304 | tf_op jit(solution)/shard_map/ppermute | solution.py:567
  273.8 32.2 %collective-permute-start.59 = (bf16[24,16,1024]{2,1,0:T(8,128)(2,1)S(1)}, bf16[24,16,1024]{2,1,0:T(8,128)(2,1)S(1)}, u32[]{:S(2)}, u32[]{:S(2)}) collective-permute-start(bf16[24,16,1024]{2,1,0:T(8,128)(2,1)S(1)} %collective-permute-done.57.refs_6_), channel_id=1, source_target_pairs={{2,0},{4,2},{6,4},{7,6},{5,7},{3,5},{1,3},{0,1},{10,8},{12,10},{14... | collective-permute-start | bytes 2359304 | tf_op jit(solution)/shard_map/ppermute | solution.py:567
  289.1 32.1 %collective-permute-start.36 = (bf16[24,16,1024]{2,1,0:T(8,128)(2,1)S(1)}, bf16[24,16,1024]{2,1,0:T(8,128)(2,1)S(1)}, u32[]{:S(2)}, u32[]{:S(2)}) collective-permute-start(bf16[24,16,1024]{2,1,0:T(8,128)(2,1)S(1)} %collective-permute-done.21.refs_2_), channel_id=1, source_target_pairs={{0,2},{2,4},{4,6},{6,7},{7,5},{5,3},{3,1},{1,0},{8,10},{10,12},{12... | collective-permute-start | bytes 2359304 | tf_op jit(solution)/shard_map/ppermute | solution.py:567
  290.6 32.2 %collective-permute-start.37 = (bf16[24,16,1024]{2,1,0:T(8,128)(2,1)S(1)}, bf16[24,16,1024]{2,1,0:T(8,128)(2,1)S(1)}, u32[]{:S(2)}, u32[]{:S(2)}) collective-permute-start(bf16[24,16,1024]{2,1,0:T(8,128)(2,1)S(1)} %collective-permute-done.22.refs_6_), channel_id=1, source_target_pairs={{2,0},{4,2},{6,4},{7,6},{5,7},{3,5},{1,3},{0,1},{10,8},{12,10},{14... | collective-permute-start | bytes 2359304 | tf_op jit(solution)/shard_map/ppermute | solution.py:567
  306.0 23.6 %collective-permute-start.60 = (bf16[12,16,1024]{2,1,0:T(8,128)(2,1)S(1)}, bf16[12,16,1024]{2,1,0:T(8,128)(2,1)S(1)}, u32[]{:S(2)}, u32[]{:S(2)}) collective-permute-start(bf16[12,16,1024]{2,1,0:T(8,128)(2,1)S(1)} %slice.138), channel_id=1, source_target_pairs={{0,2},{2,4},{4,6},{6,7},{7,5},{5,3},{3,1},{1,0},{8,10},{10,12},{12... | collective-permute-start | bytes 1179656 | tf_op jit(solution)/shard_map/ppermute | solution.py:567
  310.6 24.5 %collective-permute-start.61 = (bf16[12,16,1024]{2,1,0:T(8,128)(2,1)S(1)}, bf16[12,16,1024]{2,1,0:T(8,128)(2,1)S(1)}, u32[]{:S(2)}, u32[]{:S(2)}) collective-permute-start(bf16[12,16,1024]{2,1,0:T(8,128)(2,1)S(1)} %slice.141), channel_id=1, source_target_pairs={{2,0},{4,2},{6,4},{7,6},{5,7},{3,5},{1,3},{0,1},{10,8},{12,10},{14... | collective-permute-start | bytes 1179656 | tf_op jit(solution)/shard_map/ppermute | solution.py:567
  340.3 16.8 %collective-permute-start.41 = (bf16[8,16,1024]{2,1,0:T(8,128)(2,1)S(1)}, bf16[8,16,1024]{2,1,0:T(8,128)(2,1)S(1)}, u32[]{:S(2)}, u32[]{:S(2)}) collective-permute-start(bf16[8,16,1024]{2,1,0:T(8,128)(2,1)S(1)} %bitcast.100), channel_id=1, source_target_pairs={{2,0},{4,2},{6,4},{7,6},{5,7},{3,5},{1,3},{0,1},{10,8},{12,10},{14... | collective-permute-start | bytes 786440 | tf_op jit(solution)/shard_map/ppermute | solution.py:567
  433.4 25.1 %all-to-all-start = ((bf16[4,8,88,128]{3,2,1,0:T(8,128)(2,1)}), bf16[4,8,88,128]{3,2,1,0:T(8,128)(2,1)}, u32[]{:S(2)}, u32[]{:S(2)}) async-start(bf16[4,8,88,128]{3,2,1,0:T(8,128)(2,1)} %bitcast.116), calls=%async_computation | async-start | bytes 1441792 | tf_op jit(solution)/shard_map/all_to_all | solution.py:539
  (78 other events, 758.9 us)

commit v3 on v2

--- a/solution.py
+++ b/solution.py
@@ -17,6 +17,7 @@
 UNITS = 32
 CHUNKS = (4, 6, 6, 6, 4, 2, 2, 2)
 LONG = 6
+EARLY = 3
 BLOCK = 4
 HALVES = 2
 VMEM = pl.BlockSpec(memory_space=pltpu.VMEM)
@@ -335,6 +336,7 @@
     pieces = [p for slot in pieces for p, _, _ in slot]
     offset = first // block
     aliased = seen and target is not None
+    room = 10 if seen and formed else 56
     out_specs, out_shape = [], []
     if seen:
         out_specs.append(
@@ -360,41 +362,54 @@
         ),
         out_shape=out_shape,
         input_output_aliases={1 + len(pieces) + 4 * formed: 0} if aliased else {},
-        compiler_params=params(10),
+        compiler_params=params(room),
         cost_estimate=cost(12 * count * row_count * A * 256, count * row_count * A * 6),
         name="products",
     )(place, *pieces, *others)
 
 
-def synthesis_kernel(number, half, owners, spectra, table, out):
-    got = [
-        lax.dot_general(
-            spectra[...], table[e], (((0,), (0,)), ((), ())), preferred_element_type=jnp.float32
-        )
-        for e in range(2)
-    ]
-    for s in range(number):
-        real, imag = 2 * s * half, (2 * s + 1) * half
-        rows = pl.ds(pl.multiple_of(owners[s] * half, half), half)
-        out[rows, :] = got[0][real : real + half] + got[1][imag : imag + half]
-
-
-def synthesis(spectra, table, owners, frames):
-    beam_count, channels, width = spectra.shape
+def synthesis_kernel(number, half, groups, owners, *refs):
+    spectra, tables, out = refs[:groups], refs[groups : 2 * groups], refs[-1]
+    beams, wide = out.shape[0], out.shape[2]
+    got = None
+    for part, table in zip(spectra, tables):
+        value = jnp.concatenate(
+            [
+                jnp.concatenate([part[c, i] for i in range(beams)], axis=1)
+                for c in range(part.shape[0])
+            ],
+            axis=0,
+        )
+        turned = value.T
+        both = [
+            jnp.dot(turned, table[e], preferred_element_type=jnp.float32) for e in range(2)
+        ]
+        got = both if got is None else [a + b for a, b in zip(got, both)]
+    for i in range(beams):
+        for s in range(number):
+            real = (i * number + s) * 2 * half
+            rows = pl.ds(pl.multiple_of(owners[s] * half, half), half)
+            out[i, rows, :] = got[0][real : real + half] + got[1][real + half : real + 2 * half]
+
+
+def synthesis(spectra, tables, owners, frames):
+    beam_count = spectra[0].shape[1]
     number = owners.shape[0]
+    wide = 256
     return pl.pallas_call(
-        functools.partial(synthesis_kernel, number, frames // number),
+        functools.partial(synthesis_kernel, number, frames // number, len(spectra)),
         grid_spec=pltpu.PrefetchScalarGridSpec(
             num_scalar_prefetch=1,
-            grid=(beam_count,),
-            in_specs=[pl.BlockSpec((None, channels, width), lambda i, s: (i, 0, 0)), VMEM],
-            out_specs=pl.BlockSpec((None, frames, FOURIER_LENGTH), lambda i, s: (i, 0, 0)),
+            grid=(FOURIER_LENGTH // wide,),
+            in_specs=[VMEM] * len(spectra)
+            + [pl.BlockSpec(t.shape[:2] + (wide,), lambda i, s: (0, 0, i)) for t in tables],
+            out_specs=pl.BlockSpec((beam_count, frames, wide), lambda i, s: (0, 0, i)),
         ),
         out_shape=jax.ShapeDtypeStruct((beam_count, frames, FOURIER_LENGTH), jnp.float32),
-        compiler_params=params(10),
-        cost_estimate=cost(4 * beam_count * channels * width * FOURIER_LENGTH, 8 * 2**20),
+        compiler_params=params(20),
+        cost_estimate=cost(4 * beam_count * NCH * 2 * frames * FOURIER_LENGTH, 8 * 2**20),
         name="synthesis",
-    )(owners, spectra, table)
+    )(owners, *spectra, *tables)
 
 
 def body(samples, history, antenna_flags, beam_delays):
@@ -423,10 +438,11 @@
 
     past = (FILTER_TAPS - 1) * FOURIER_LENGTH
     blocks = block_list // HALVES
-    before = [
-        from_behind(samples[h * blocks : (h + 1) * blocks, :, shard_length - past :], "row", 1)
-        for h in range(HALVES)
-    ]
+    taps, table = tap_table(), dft_rows(channel_number)
+    tail = samples[:blocks, :, shard_length - past :]
+    before = [from_behind(tail, "row", 1)]
+    later, table = lax.optimization_barrier((samples, table))
+    before.append(from_behind(later[blocks:, :, shard_length - past :], "row", 1))
     delays = lax.dynamic_index_in_dim(
         beam_delays.reshape(channel_number, n_row, beam_count, A), row_id, 1, keepdims=False
     ).reshape(channel_number * beam_count, A)
@@ -435,23 +451,29 @@
     calls = []
     for i, (at, size) in enumerate(zip(firsts, sizes)):
         parts = 2 if size >= LONG * unit else 1
-        calls += [(i, at + d * (size // 2), size // parts) for d in range(parts)]
+        calls += [((i,), at + d * (size // 2), size // parts) for d in range(parts)]
+    calls[-2:] = [(calls[-2][0] + calls[-1][0], calls[-2][1], calls[-2][2] + calls[-1][2])]
     starts = chan_id * channel_total + jnp.array([at for _, at, _ in calls], jnp.int32)
     base_re, base_im = phasor(delays[None], starts[:, None, None], 1.0 / math.sqrt(A))
     step_re, step_im = phasor(delays, 1, 1.0)
-    back = synth_table()
+    cuts = (0, firsts[EARLY], channel_total)
+    back = synth_table().reshape(2, channel_number, channel_total, FOURIER_LENGTH)
+    back = [
+        back[:, :, low:high].reshape(2, -1, FOURIER_LENGTH)
+        for low, high in zip(cuts[:-1], cuts[1:])
+    ]
     spread = spread_table(antenna_flags, chan_id, channel_number, block_list)
 
-    taps, table = tap_table(), dft_rows(channel_number)
     arrived = []
     for h in range(HALVES):
         if h == HALVES - 1:
             ahead = [p for m in range(1, channel_number) for p, _ in arrived[0][m]]
-            before[h], spread, owners, base_re, base_im, step_re, step_im, back, *ahead = (
+            before[h], spread, owners, base_re, base_im, step_re, step_im, *held = (
                 lax.optimization_barrier(
-                    (before[h], spread, owners, base_re, base_im, step_re, step_im, back, *ahead)
+                    (before[h], spread, owners, base_re, base_im, step_re, step_im, *back, *ahead)
                 )
             )
+            back, ahead = held[: len(back)], held[len(back) :]
             arrived[0][1:] = [[(p, 0)] for p in ahead]
         parcels = [channel_total]
         if h == HALVES - 1:
@@ -500,14 +522,19 @@
             start = chunk_of(*chunk)
             passed[chunk] = [[start], [start]]
 
-    def slots_of(i, first, count):
-        shift, half = first - firsts[i], sizes[i] // 2
-        onwards, backwards = passed[i, everyone]
-        held = [[(p, shift, count)] for p in onwards[: whole_steps + 1]]
-        if steps > whole_steps:
-            far = [(w[-1], 0, half) for w in (onwards, backwards)]
-            held.append(far if count > half else far[shift // half :][:1])
-        return held + [[(p, shift, count)] for p in backwards[whole_steps:0:-1]]
+    def slots_of(chunks, first, count):
+        found = []
+        for i in chunks:
+            shift, half = max(first - firsts[i], 0), sizes[i] // 2
+            size = min(count, sizes[i])
+            onwards, backwards = passed[i, everyone]
+            held = [[(p, shift, size)] for p in onwards[: whole_steps + 1]]
+            if steps > whole_steps:
+                far = [(w[-1], 0, half) for w in (onwards, backwards)]
+                held.append(far if size > half else far[shift // half :][:1])
+            held += [[(p, shift, size)] for p in backwards[whole_steps:0:-1]]
+            found = [a + b for a, b in zip(found, held)] if found else held
+        return found
 
     visibilities = None
     beams = {}
@@ -539,8 +566,8 @@
         return lax.all_to_all(value, "chan", split_axis=0, concat_axis=0, tiled=True)
 
     groups = [
-        [j for j, (i, _, _) in enumerate(calls) if low <= i < high]
-        for low, high in ((0, 4), (4, len(CHUNKS)))
+        [j for j, (i, _, _) in enumerate(calls) if low <= i[0] < high]
+        for low, high in ((0, EARLY), (EARLY, len(CHUNKS)))
     ]
     arrived_beams = {}
 
@@ -559,6 +586,8 @@
                 if j == group[-1]:
                     arrived_beams[g] = to_owners(group)
             going, extra = held[:2], []
+        if n == len(order) - 1:
+            extra.append(arrived_beams[0])
         if extra:
             going = lax.optimization_barrier((*going, *extra))[:2]
         if step >= whole_steps:
@@ -570,7 +599,7 @@
         sent[lane] = got
         if step == steps - 1 and lane == 1:
             i = chunk[0]
-            work = [j for j, call in enumerate(calls) if call[0] in (i - 1, i)]
+            work = [j for j, call in enumerate(calls) if call[0][-1] in (i - 1, i)]
             for k, j in enumerate(work):
                 waiting.append((n + 1 + k * 2 * steps // len(work), j))
 
@@ -586,9 +615,9 @@
             arrived_beams[g] = to_owners(group)
     for j in left:
         products(j, formed=False)
-    spectra = jnp.concatenate([arrived_beams[g] for g in range(len(groups))], axis=2)
-    spectra = spectra.transpose(1, 0, 2, 3).reshape(beam_count, NCH, 2 * frames)
-    beam_series = synthesis(spectra, back, owners, frames)
+    beam_series = synthesis(
+        [arrived_beams[g] for g in range(len(groups))], back, owners, frames
+    )
     return (visibilities, beam_series)
 
 

time: 484 us -> 480 us (level)
    pallas_call x13 -> x11, Pallas kernels: 64.7 us -> 64.8 us  [products_of(): pl.pallas_call(functools.partial(products_kernel, ends, frames, aliased,...]
  transfers between devices with their start and end apart: 80 -> 80, of which waited for: 50 -> 56; matrix products, arithmetic and copies ran while one was open for 8% -> 8% of each run, Pallas kernels for 18% -> 17%
where the time goes in v3:
time: 480 us; the launch traced here: 473 us
  waiting for transfers between devices  223 us (46%)
  Pallas kernels  104 us (22%)
  starting transfers between devices  96.7 us (20%)
  other arithmetic  28.1 us (6%)
  local copies, waits for them, and re-layouts  19.7 us (4%)
    ppermute x64, waiting for transfers between devices, body(): got = [lax.ppermute(p, 'row', r) for p, r in zip(going, (onward, backward))]  184 us
    ppermute x64, starting transfers between devices, body(): got = [lax.ppermute(p, 'row', r) for p, r in zip(going, (onward, backward))]  69 us
    pallas_call x11, Pallas kernels, products_of(): pl.pallas_call(functools.partial(products_kernel, ends, frames, aliased,...  64.8 us
    ppermute x2, waiting for transfers between devices, from_behind(): return lax.ppermute(block, axis, route)  29.4 us
    pallas_call x2, Pallas kernels, front(): pl.pallas_call(functools.partial(front_kernel, rows, steps, fold, parcels...  18.7 us
    another operation x2, other arithmetic  18.2 us
    pallas_call x8, Pallas kernels, into_order(): pl.pallas_call(functools.partial(order_kernel, number, halves), grid=(blo...  15.6 us
    ppermute x12, starting transfers between devices, body(): lax.ppermute(piece, 'chan', route)  11.1 us
  transfers between devices with their start and end apart: 80, of which 56 were waited for; matrix products, arithmetic and copies ran while one was open for 8% of the time, Pallas kernels for 17%

profile of v3, /device:TPU:0, one launch (start us, length us, event | category | flops | bytes accessed | tf_op | source)
XLA Modules:
  0.0 473.2 jit_solution(5377719516742610533)
XLA Ops:
  3.5 6.1 %collective-permute-start = (bf16[4,32,7168]{2,1,0:T(8,128)(2,1)}, bf16[4,32,7168]{2,1,0:T(8,128)(2,1)}, u32[]{:S(2)}, u32[]{:S(2)}) collective-permute-start(bf16[4,32,7168]{2,1,0:T(8,128)(2,1)} %slice.120), channel_id=1, source_target_pairs={{0,1},{1,2},{2,3},{3,4},{4,5},{5,6},{6,7},{8,9},{9,10},{10,11},{11... | collective-permute-start | bytes 5505032 | tf_op jit(solution)/shard_map/ppermute | solution.py:38
  9.6 9.1 %multiply_convert_fusion.3 = (bf16[4,1,128,1024]{3,2,1,0:T(8,128)(2,1)S(1)}, bf16[4,1,128,1024]{3,2,1,0:T(8,128)(2,1)S(1)}) fusion(s32[4,128]{1,0:T(4,128)S(1)} %multiply_add_fusion.1), kind=kLoop, calls=%fused_computation.26 | loop fusion | flops 9961472 | bytes 2099200 | tf_op jit(solution)/shard_map/convert.2
  28.7 9.1 %multiply_convert_fusion = (bf16[1,4,128,1024]{3,2,1,0:T(8,128)(2,1)S(1)}, bf16[1,4,128,1024]{3,2,1,0:T(8,128)(2,1)S(1)}) fusion(s32[4,128]{1,0:T(4,128)S(1)} %multiply_add_fusion.1), kind=kLoop, calls=%fused_computation.21 | loop fusion | flops 9961472 | bytes 2099200 | tf_op jit(solution)/shard_map/convert.1
  39.6 9.4 %collective-permute-done = bf16[4,32,7168]{2,1,0:T(8,128)(2,1)} collective-permute-done((bf16[4,32,7168]{2,1,0:T(8,128)(2,1)}, bf16[4,32,7168]{2,1,0:T(8,128)(2,1)}, u32[]{:S(2)}, u32[]{:S(2)}) %collective-permute-start) | collective-permute-done | bytes 1835040 | tf_op jit(solution)/shard_map/ppermute | solution.py:38
  49.1 9.3 %front.2 = (bf16[2048,128]{1,0:T(8,128)(2,1)S(1)}, bf16[2048,128]{1,0:T(8,128)(2,1)S(1)}, bf16[2048,128]{1,0:T(8,128)(2,1)S(1)}, bf16[2048,128]{1,0:T(8,128)(2,1)S(1)}) custom-call(s32[2]{0:T(128)S(1)} %pad_add_fusion.place, bf16[256,8192]{1,0:T(8,128)(2,1)S(1)} %bitcast.72, bf16[128,7168]{1,0:T(8,128)(2,1)} %bitcast.3.before, ...), custom_call_target="tpu_custom_call" | custom-call | flops 12884901888 | bytes 25165824 | tf_op jit(solution)/shard_map/front/pallas_call | solution.py:180
  62.1 5.2 %negate_multiply_fusion = (f32[10,32,1024]{2,1,0:T(8,128)S(1)}, f32[10,32,1024]{2,1,0:T(8,128)S(1)}) fusion(s32[10]{0:T(128)S(1)} %broadcast_add_fusion, s32[32,1024]{1,0:T(8,128)S(1)} %get-tuple-element.259), kind=kLoop, calls=%fused_computation.36 | loop fusion | flops 5570560 | bytes 2752552 | tf_op jit(solution)/shard_map/mul | solution.py:75
  67.3 20.0 %collective-permute-done.1 = bf16[4,32,7168]{2,1,0:T(8,128)(2,1)} collective-permute-done((bf16[4,32,7168]{2,1,0:T(8,128)(2,1)}, bf16[4,32,7168]{2,1,0:T(8,128)(2,1)}, u32[]{:S(2)}, u32[]{:S(2)}) %collective-permute-start.1) | collective-permute-done | bytes 1835040 | tf_op jit(solution)/shard_map/ppermute | solution.py:38
  87.3 9.3 %front.3 = (bf16[256,128]{1,0:T(8,128)(2,1)S(1)}, bf16[384,128]{1,0:T(8,128)(2,1)S(1)}, bf16[1408,128]{1,0:T(8,128)(2,1)S(1)}, bf16[256,128]{1,0:T(8,128)(2,1)S(...) custom-call(s32[2]{0:T(128)S(1)} %pad_add_fusion.place, ...), custom_call_target="tpu_custom_call" | custom-call | flops 12884901888 | bytes 25165824 | tf_op jit(solution)/shard_map/front/pallas_call | solution.py:180
  119.7 7.5 %collective-permute-done.24.refs_1_ = bf16[24,16,1024]{2,1,0:T(8,128)(2,1)S(1)} collective-permute-done((bf16[24,16,1024]{2,1,0:T(8,128)(2,1)S(1)}, bf16[24,16,1024]{2,1,0:T(8,128)(2,1)S(1)}, u32[]{:S(2)}, u32[]{:S(2)}) %collective-permute-start.24) | collective-permute-done | bytes 786464 | tf_op jit(solution)/shard_map/ppermute | solution.py:596
  144.5 21.9 %collective-permute-done.13.refs_2_ = bf16[16,16,1024]{2,1,0:T(8,128)(2,1)S(1)} collective-permute-done((bf16[16,16,1024]{2,1,0:T(8,128)(2,1)S(1)}, bf16[16,16,1024]{2,1,0:T(8,128)(2,1)S(1)}, u32[]{:S(2)}, u32[]{:S(2)}) %collective-permute-start.13) | collective-permute-done | bytes 524320 | tf_op jit(solution)/shard_map/ppermute | solution.py:596
  175.5 9.0 %collective-permute-done.15.refs_3_ = bf16[16,16,1024]{2,1,0:T(8,128)(2,1)S(1)} collective-permute-done((bf16[16,16,1024]{2,1,0:T(8,128)(2,1)S(1)}, bf16[16,16,1024]{2,1,0:T(8,128)(2,1)S(1)}, u32[]{:S(2)}, u32[]{:S(2)}) %collective-permute-start.15) | collective-permute-done | bytes 524320 | tf_op jit(solution)/shard_map/ppermute | solution.py:596
  194.3 7.1 %collective-permute-done.28.refs_3_ = bf16[24,16,1024]{2,1,0:T(8,128)(2,1)S(1)} collective-permute-done((bf16[24,16,1024]{2,1,0:T(8,128)(2,1)S(1)}, bf16[24,16,1024]{2,1,0:T(8,128)(2,1)S(1)}, u32[]{:S(2)}, u32[]{:S(2)}) %collective-permute-start.28) | collective-permute-done | bytes 786464 | tf_op jit(solution)/shard_map/ppermute | solution.py:596
  208.7 6.6 %products.11 = (bf16[128,2,128,1024]{3,2,1,0:T(8,128)(2,1)}, bf16[16,32,128]{2,1,0:T(8,128)(2,1)S(1)}) custom-call(s32[2]{0:T(128)S(1)} %pad_add_fusion.place, bf16[16,16,1024]{2,1,0:T(8,128)(2,1)S(1)} %bitcast.108, bf16[16,16,1024]{2,1,0:T(8,128)(2,1)S(1)} %collective-permute-done.11.refs_1_, bf16[16,16,1024]{2,1,0:T(8,128)(2,1)S(1)} %collective-permute-done.13.refs_2_, ...), custom_call_target="tpu_custom_call" | custom-call | flops 19327352832 | bytes 37748736 | tf_op jit(solution)/shard_map/products/pallas_call | solution.py:352
  219.4 5.4 %products.12 = (bf16[128,2,128,1024]{3,2,1,0:T(8,128)(2,1)}, bf16[12,32,128]{2,1,0:T(8,128)(2,1)S(1)}) custom-call(s32[2]{0:T(128)S(1)} %pad_add_fusion.place, bf16[24,16,1024]{2,1,0:T(8,128)(2,1)S(1)} %bitcast.80, bf16[24,16,1024]{2,1,0:T(8,128)(2,1)S(1)} %collective-permute-done.24.refs_1_, ...), custom_call_target="tpu_custom_call", output_to_operand_aliasing={{0}: (13, {})} | custom-call | flops 14495514624 | bytes 28311552 | tf_op jit(solution)/shard_map/products/pallas_call | solution.py:352
  224.8 11.0 %collective-permute-done.19.refs_1_ = bf16[24,16,1024]{2,1,0:T(8,128)(2,1)S(1)} collective-permute-done((bf16[24,16,1024]{2,1,0:T(8,128)(2,1)S(1)}, bf16[24,16,1024]{2,1,0:T(8,128)(2,1)S(1)}, u32[]{:S(2)}, u32[]{:S(2)}) %collective-permute-start.19) | collective-permute-done | bytes 786464 | tf_op jit(solution)/shard_map/ppermute | solution.py:596
  239.4 13.2 %collective-permute-done.37.refs_1_ = bf16[24,16,1024]{2,1,0:T(8,128)(2,1)S(1)} collective-permute-done((bf16[24,16,1024]{2,1,0:T(8,128)(2,1)S(1)}, bf16[24,16,1024]{2,1,0:T(8,128)(2,1)S(1)}, u32[]{:S(2)}, u32[]{:S(2)}) %collective-permute-start.37) | collective-permute-done | bytes 786464 | tf_op jit(solution)/shard_map/ppermute | solution.py:596
  256.3 13.2 %collective-permute-done.31.refs_2_ = bf16[24,16,1024]{2,1,0:T(8,128)(2,1)S(1)} collective-permute-done((bf16[24,16,1024]{2,1,0:T(8,128)(2,1)S(1)}, bf16[24,16,1024]{2,1,0:T(8,128)(2,1)S(1)}, u32[]{:S(2)}, u32[]{:S(2)}) %collective-permute-start.31) | collective-permute-done | bytes 786464 | tf_op jit(solution)/shard_map/ppermute | solution.py:596
  273.1 5.4 %products.13 = (bf16[128,2,128,1024]{3,2,1,0:T(8,128)(2,1)}, bf16[12,32,128]{2,1,0:T(8,128)(2,1)S(1)}) custom-call(s32[2]{0:T(128)S(1)} %pad_add_fusion.place, bf16[24,16,1024]{2,1,0:T(8,128)(2,1)S(1)} %bitcast.81, bf16[24,16,1024]{2,1,0:T(8,128)(2,1)S(1)} %collective-permute-done.24.refs_1_, ...), custom_call_target="tpu_custom_call", output_to_operand_aliasing={{0}: (13, {})} | custom-call | flops 14495514624 | bytes 28311552 | tf_op jit(solution)/shard_map/products/pallas_call | solution.py:352
  278.6 7.8 %collective-permute-done.39.refs_2_ = bf16[24,16,1024]{2,1,0:T(8,128)(2,1)S(1)} collective-permute-done((bf16[24,16,1024]{2,1,0:T(8,128)(2,1)S(1)}, bf16[24,16,1024]{2,1,0:T(8,128)(2,1)S(1)}, u32[]{:S(2)}, u32[]{:S(2)}) %collective-permute-start.39) | collective-permute-done | bytes 786464 | tf_op jit(solution)/shard_map/ppermute | solution.py:596
  290.0 13.2 %collective-permute-done.33.refs_3_ = bf16[24,16,1024]{2,1,0:T(8,128)(2,1)S(1)} collective-permute-done((bf16[24,16,1024]{2,1,0:T(8,128)(2,1)S(1)}, bf16[24,16,1024]{2,1,0:T(8,128)(2,1)S(1)}, u32[]{:S(2)}, u32[]{:S(2)}) %collective-permute-start.33) | collective-permute-done | bytes 786464 | tf_op jit(solution)/shard_map/ppermute | solution.py:596
  311.0 9.1 %collective-permute-done.46.refs_3_ = bf16[24,16,1024]{2,1,0:T(8,128)(2,1)S(1)} collective-permute-done((bf16[24,16,1024]{2,1,0:T(8,128)(2,1)S(1)}, bf16[24,16,1024]{2,1,0:T(8,128)(2,1)S(1)}, u32[]{:S(2)}, u32[]{:S(2)}) %collective-permute-start.46) | collective-permute-done | bytes 786464 | tf_op jit(solution)/shard_map/ppermute | solution.py:596
  323.9 4.7 collective-permute-done.35.refs_4_
  328.5 5.4 %products.14 = (bf16[128,2,128,1024]{3,2,1,0:T(8,128)(2,1)}, bf16[12,32,128]{2,1,0:T(8,128)(2,1)S(1)}) custom-call(s32[2]{0:T(128)S(1)} %pad_add_fusion.place, bf16[24,16,1024]{2,1,0:T(8,128)(2,1)S(1)} %bitcast.84, bf16[24,16,1024]{2,1,0:T(8,128)(2,1)S(1)} %collective-permute-done.19.refs_1_, ...), custom_call_target="tpu_custom_call", output_to_operand_aliasing={{0}: (13, {})} | custom-call | flops 14495514624 | bytes 28311552 | tf_op jit(solution)/shard_map/products/pallas_call | solution.py:352
  340.4 5.5 %products.15 = (bf16[128,2,128,1024]{3,2,1,0:T(8,128)(2,1)}, bf16[12,32,128]{2,1,0:T(8,128)(2,1)S(1)}) custom-call(s32[2]{0:T(128)S(1)} %pad_add_fusion.place, bf16[24,16,1024]{2,1,0:T(8,128)(2,1)S(1)} %bitcast.85, bf16[24,16,1024]{2,1,0:T(8,128)(2,1)S(1)} %collective-permute-done.19.refs_1_, ...), custom_call_target="tpu_custom_call", output_to_operand_aliasing={{0}: (13, {})} | custom-call | flops 14495514624 | bytes 28311552 | tf_op jit(solution)/shard_map/products/pallas_call | solution.py:352
  358.1 5.5 %products.16 = (bf16[128,2,128,1024]{3,2,1,0:T(8,128)(2,1)}, bf16[12,32,128]{2,1,0:T(8,128)(2,1)S(1)}) custom-call(s32[2]{0:T(128)S(1)} %pad_add_fusion.place, bf16[24,16,1024]{2,1,0:T(8,128)(2,1)S(1)} %bitcast.76, bf16[24,16,1024]{2,1,0:T(8,128)(2,1)S(1)} %collective-permute-done.37.refs_1_, ...), custom_call_target="tpu_custom_call", output_to_operand_aliasing={{0}: (13, {})} | custom-call | flops 14495514624 | bytes 28311552 | tf_op jit(solution)/shard_map/products/pallas_call | solution.py:352
  375.2 5.5 %products.17 = (bf16[128,2,128,1024]{3,2,1,0:T(8,128)(2,1)}, bf16[12,32,128]{2,1,0:T(8,128)(2,1)S(1)}) custom-call(s32[2]{0:T(128)S(1)} %pad_add_fusion.place, bf16[24,16,1024]{2,1,0:T(8,128)(2,1)S(1)} %bitcast.77, bf16[24,16,1024]{2,1,0:T(8,128)(2,1)S(1)} %collective-permute-done.37.refs_1_, ...), custom_call_target="tpu_custom_call", output_to_operand_aliasing={{0}: (13, {})} | custom-call | flops 14495514624 | bytes 28311552 | tf_op jit(solution)/shard_map/products/pallas_call | solution.py:352
  389.7 5.1 %collective-permute-done.61.refs_4_ = bf16[4,16,1024]{2,1,0:T(8,128)(2,1)S(1)} collective-permute-done((bf16[4,16,1024]{2,1,0:T(8,128)(2,1)S(1)}, bf16[4,16,1024]{2,1,0:T(8,128)(2,1)S(1)}, u32[]{:S(2)}, u32[]{:S(2)}) %collective-permute-start.61) | collective-permute-done | bytes 131104 | tf_op jit(solution)/shard_map/ppermute | solution.py:596
  399.1 6.6 %products.18 = (bf16[128,2,128,1024]{3,2,1,0:T(8,128)(2,1)}, bf16[16,32,128]{2,1,0:T(8,128)(2,1)S(1)}) custom-call(s32[2]{0:T(128)S(1)} %pad_add_fusion.place, bf16[16,16,1024]{2,1,0:T(8,128)(2,1)S(1)} %bitcast.88, bf16[16,16,1024]{2,1,0:T(8,128)(2,1)S(1)} %collective-permute-done.42.refs_1_, ...), custom_call_target="tpu_custom_call", output_to_operand_aliasing={{0}: (14, {})} | custom-call | flops 19327352832 | bytes 37748736 | tf_op jit(solution)/shard_map/products/pallas_call | solution.py:352
  429.7 5.2 %collective-permute-done.71.refs_7_ = bf16[8,16,1024]{2,1,0:T(8,128)(2,1)S(1)} collective-permute-done((bf16[8,16,1024]{2,1,0:T(8,128)(2,1)}, bf16[8,16,1024]{2,1,0:T(8,128)(2,1)S(1)}, u32[]{:S(2)}, u32[]{:S(2)}) %collective-permute-start.71) | collective-permute-done | bytes 262176 | tf_op jit(solution)/shard_map/ppermute | solution.py:596
  447.4 6.5 %products.20 = bf16[16,32,128]{2,1,0:T(8,128)(2,1)} custom-call(s32[2]{0:T(128)} %copy-done.22, bf16[8,16,1024]{2,1,0:T(8,128)(2,1)} %bitcast.93, bf16[8,16,1024]{2,1,0:T(8,128)(2,1)} %bitcast.100, bf16[8,16,1024]{2,1,0:T(8,128)(2,1)} %collective-permute-done.54.refs_2_, bf16[8,16,1024]{2,1,0:T(8,128)(2,1)} %collective-permute-done.63.refs_3_, ...), custom_call_target="tpu_custom_call" | custom-call | flops 19327352832 | bytes 37748736 | tf_op jit(solution)/shard_map/products/pallas_call | solution.py:352
  459.3 8.2 %products.21 = bf16[128,2,128,1024]{3,2,1,0:T(8,128)(2,1)} custom-call(s32[2]{0:T(128)} %copy-done.22, bf16[8,16,1024]{2,1,0:T(8,128)(2,1)} %bitcast.94, bf16[8,16,1024]{2,1,0:T(8,128)(2,1)} %bitcast.101, bf16[8,16,1024]{2,1,0:T(8,128)(2,1)} %collective-permute-done.54.refs_2_, ...), custom_call_target="tpu_custom_call", output_to_operand_aliasing={{}: (19, {})} | custom-call | flops 19327352832 | bytes 37748736 | tf_op jit(solution)/shard_map/products/pallas_call | solution.py:352
  468.1 4.6 synthesis.1
  (273 shorter events, 200.6 us)
Async XLA Ops:
  3.5 45.6 %collective-permute-start = (bf16[4,32,7168]{2,1,0:T(8,128)(2,1)}, bf16[4,32,7168]{2,1,0:T(8,128)(2,1)}, u32[]{:S(2)}, u32[]{:S(2)}) collective-permute-start(bf16[4,32,7168]{2,1,0:T(8,128)(2,1)} %slice.120), channel_id=1, source_target_pairs={{0,1},{1,2},{2,3},{3,4},{4,5},{5,6},{6,7},{8,9},{9,10},{10,11},{11... | collective-permute-start | bytes 5505032 | tf_op jit(solution)/shard_map/ppermute | solution.py:38
  21.8 65.4 %collective-permute-start.1 = (bf16[4,32,7168]{2,1,0:T(8,128)(2,1)}, bf16[4,32,7168]{2,1,0:T(8,128)(2,1)}, u32[]{:S(2)}, u32[]{:S(2)}) collective-permute-start(bf16[4,32,7168]{2,1,0:T(8,128)(2,1)} %slice.121), channel_id=1, source_target_pairs={{0,1},{1,2},{2,3},{3,4},{4,5},{5,6},{6,7},{8,9},{9,10},{10,11},{11... | collective-permute-start | bytes 5505032 | tf_op jit(solution)/shard_map/ppermute | solution.py:38
  58.4 28.8 %collective-permute-start.2 = (bf16[2048,128]{1,0:T(8,128)(2,1)S(1)}, bf16[2048,128]{1,0:T(8,128)(2,1)S(1)}, u32[]{:S(2)}, u32[]{:S(2)}) collective-permute-start(bf16[2048,128]{1,0:T(8,128)(2,1)S(1)} %get-tuple-element.133), channel_id=1, source_target_pairs={{0,8},{8,16},{16,24},{24,0},{1,9},{9,17},{17,25},{25,1},{2,10},{10... | collective-permute-start | bytes 1572872 | tf_op jit(solution)/shard_map/ppermute | solution.py:498
  58.5 28.8 %collective-permute-start.3 = (bf16[2048,128]{1,0:T(8,128)(2,1)S(1)}, bf16[2048,128]{1,0:T(8,128)(2,1)S(1)}, u32[]{:S(2)}, u32[]{:S(2)}) collective-permute-start(bf16[2048,128]{1,0:T(8,128)(2,1)S(1)} %get-tuple-element.134), channel_id=1, source_target_pairs={{0,16},{8,24},{16,0},{24,8},{1,17},{9,25},{17,1},{25,9},{2,18},{10... | collective-permute-start | bytes 1572872 | tf_op jit(solution)/shard_map/ppermute | solution.py:498
  60.0 27.2 %collective-permute-start.4 = (bf16[2048,128]{1,0:T(8,128)(2,1)S(1)}, bf16[2048,128]{1,0:T(8,128)(2,1)S(1)}, u32[]{:S(2)}, u32[]{:S(2)}) collective-permute-start(bf16[2048,128]{1,0:T(8,128)(2,1)S(1)} %get-tuple-element.135), channel_id=1, source_target_pairs={{0,24},{8,0},{16,8},{24,16},{1,25},{9,1},{17,9},{25,17},{2,26},{10... | collective-permute-start | bytes 1572872 | tf_op jit(solution)/shard_map/ppermute | solution.py:498
  105.8 21.4 %collective-permute-start.24 = (bf16[24,16,1024]{2,1,0:T(8,128)(2,1)S(1)}, bf16[24,16,1024]{2,1,0:T(8,128)(2,1)S(1)}, u32[]{:S(2)}, u32[]{:S(2)}) collective-permute-start(bf16[24,16,1024]{2,1,0:T(8,128)(2,1)S(1)} %bitcast.78), channel_id=1, source_target_pairs={{0,2},{2,4},{4,6},{6,7},{7,5},{5,3},{3,1},{1,0},{8,10},{10,12},{12... | collective-permute-start | bytes 2359304 | tf_op jit(solution)/shard_map/ppermute | solution.py:596
  109.3 20.0 %collective-permute-start.25 = (bf16[24,16,1024]{2,1,0:T(8,128)(2,1)S(1)}, bf16[24,16,1024]{2,1,0:T(8,128)(2,1)S(1)}, u32[]{:S(2)}, u32[]{:S(2)}) collective-permute-start(bf16[24,16,1024]{2,1,0:T(8,128)(2,1)S(1)} %bitcast.79), channel_id=1, source_target_pairs={{2,0},{4,2},{6,4},{7,6},{5,7},{3,5},{1,3},{0,1},{10,8},{12,10},{14... | collective-permute-start | bytes 2359304 | tf_op jit(solution)/shard_map/ppermute | solution.py:596
  114.7 17.2 %collective-permute-start.6 = (bf16[1408,128]{1,0:T(8,128)(2,1)S(1)}, bf16[1408,128]{1,0:T(8,128)(2,1)S(1)}, u32[]{:S(2)}, u32[]{:S(2)}) collective-permute-start(bf16[1408,128]{1,0:T(8,128)(2,1)S(1)} %get-tuple-element.141), channel_id=1, source_target_pairs={{0,16},{8,24},{16,0},{24,8},{1,17},{9,25},{17,1},{25,9},{2,18},{10... | collective-permute-start | bytes 1081352 | tf_op jit(solution)/shard_map/ppermute | solution.py:498
  117.9 20.5 %collective-permute-start.11 = (bf16[16,16,1024]{2,1,0:T(8,128)(2,1)S(1)}, bf16[16,16,1024]{2,1,0:T(8,128)(2,1)S(1)}, u32[]{:S(2)}, u32[]{:S(2)}) collective-permute-start(bf16[16,16,1024]{2,1,0:T(8,128)(2,1)S(1)} %bitcast.106), channel_id=1, source_target_pairs={{0,2},{2,4},{4,6},{6,7},{7,5},{5,3},{3,1},{1,0},{8,10},{10,12},{12... | collective-permute-start | bytes 1572872 | tf_op jit(solution)/shard_map/ppermute | solution.py:596
  130.4 41.3 %collective-permute-start.26 = (bf16[24,16,1024]{2,1,0:T(8,128)(2,1)S(1)}, bf16[24,16,1024]{2,1,0:T(8,128)(2,1)S(1)}, u32[]{:S(2)}, u32[]{:S(2)}) collective-permute-start(bf16[24,16,1024]{2,1,0:T(8,128)(2,1)S(1)} %collective-permute-done.24.refs_1_), channel_id=1, source_target_pairs={{0,2},{2,4},{4,6},{6,7},{7,5},{5,3},{3,1},{1,0},{8,10},{10,12},{12... | collective-permute-start | bytes 2359304 | tf_op jit(solution)/shard_map/ppermute | solution.py:596
  132.0 39.7 %collective-permute-start.27 = (bf16[24,16,1024]{2,1,0:T(8,128)(2,1)S(1)}, bf16[24,16,1024]{2,1,0:T(8,128)(2,1)S(1)}, u32[]{:S(2)}, u32[]{:S(2)}) collective-permute-start(bf16[24,16,1024]{2,1,0:T(8,128)(2,1)S(1)} %collective-permute-done.25.refs_7_), channel_id=1, source_target_pairs={{2,0},{4,2},{6,4},{7,6},{5,7},{3,5},{1,3},{0,1},{10,8},{12,10},{14... | collective-permute-start | bytes 2359304 | tf_op jit(solution)/shard_map/ppermute | solution.py:596
  142.4 23.9 %collective-permute-start.13 = (bf16[16,16,1024]{2,1,0:T(8,128)(2,1)S(1)}, bf16[16,16,1024]{2,1,0:T(8,128)(2,1)S(1)}, u32[]{:S(2)}, u32[]{:S(2)}) collective-permute-start(bf16[16,16,1024]{2,1,0:T(8,128)(2,1)S(1)} %collective-permute-done.11.refs_1_), channel_id=1, source_target_pairs={{0,2},{2,4},{4,6},{6,7},{7,5},{5,3},{3,1},{1,0},{8,10},{10,12},{12... | collective-permute-start | bytes 1572872 | tf_op jit(solution)/shard_map/ppermute | solution.py:596
  144.5 25.2 %collective-permute-start.14 = (bf16[16,16,1024]{2,1,0:T(8,128)(2,1)S(1)}, bf16[16,16,1024]{2,1,0:T(8,128)(2,1)S(1)}, u32[]{:S(2)}, u32[]{:S(2)}) collective-permute-start(bf16[16,16,1024]{2,1,0:T(8,128)(2,1)S(1)} %collective-permute-done.12.refs_8_), channel_id=1, source_target_pairs={{2,0},{4,2},{6,4},{7,6},{5,7},{3,5},{1,3},{0,1},{10,8},{12,10},{14... | collective-permute-start | bytes 1572872 | tf_op jit(solution)/shard_map/ppermute | solution.py:596
  171.7 29.7 %collective-permute-start.28 = (bf16[24,16,1024]{2,1,0:T(8,128)(2,1)S(1)}, bf16[24,16,1024]{2,1,0:T(8,128)(2,1)S(1)}, u32[]{:S(2)}, u32[]{:S(2)}) collective-permute-start(bf16[24,16,1024]{2,1,0:T(8,128)(2,1)S(1)} %collective-permute-done.26.refs_2_), channel_id=1, source_target_pairs={{0,2},{2,4},{4,6},{6,7},{7,5},{5,3},{3,1},{1,0},{8,10},{10,12},{12... | collective-permute-start | bytes 2359304 | tf_op jit(solution)/shard_map/ppermute | solution.py:596
  173.4 29.7 %collective-permute-start.29 = (bf16[24,16,1024]{2,1,0:T(8,128)(2,1)S(1)}, bf16[24,16,1024]{2,1,0:T(8,128)(2,1)S(1)}, u32[]{:S(2)}, u32[]{:S(2)}) collective-permute-start(bf16[24,16,1024]{2,1,0:T(8,128)(2,1)S(1)} %collective-permute-done.27.refs_6_), channel_id=1, source_target_pairs={{2,0},{4,2},{6,4},{7,6},{5,7},{3,5},{1,3},{0,1},{10,8},{12,10},{14... | collective-permute-start | bytes 2359304 | tf_op jit(solution)/shard_map/ppermute | solution.py:596
  186.3 20.7 %collective-permute-start.17 = (bf16[8,16,1024]{2,1,0:T(8,128)(2,1)S(1)}, bf16[8,16,1024]{2,1,0:T(8,128)(2,1)S(1)}, u32[]{:S(2)}, u32[]{:S(2)}) collective-permute-start(bf16[8,16,1024]{2,1,0:T(8,128)(2,1)S(1)} %slice.124), channel_id=1, source_target_pairs={{0,2},{2,4},{4,6},{6,7},{7,5},{5,3},{3,1},{1,0},{8,10},{10,12},{12... | collective-permute-start | bytes 786440 | tf_op jit(solution)/shard_map/ppermute | solution.py:596
  187.9 20.8 %collective-permute-start.18 = (bf16[8,16,1024]{2,1,0:T(8,128)(2,1)S(1)}, bf16[8,16,1024]{2,1,0:T(8,128)(2,1)S(1)}, u32[]{:S(2)}, u32[]{:S(2)}) collective-permute-start(bf16[8,16,1024]{2,1,0:T(8,128)(2,1)S(1)} %slice.125), channel_id=1, source_target_pairs={{2,0},{4,2},{6,4},{7,6},{5,7},{3,5},{1,3},{0,1},{10,8},{12,10},{14... | collective-permute-start | bytes 786440 | tf_op jit(solution)/shard_map/ppermute | solution.py:596
  215.3 20.5 %collective-permute-start.19 = (bf16[24,16,1024]{2,1,0:T(8,128)(2,1)S(1)}, bf16[24,16,1024]{2,1,0:T(8,128)(2,1)S(1)}, u32[]{:S(2)}, u32[]{:S(2)}) collective-permute-start(bf16[24,16,1024]{2,1,0:T(8,128)(2,1)S(1)} %bitcast.82), channel_id=1, source_target_pairs={{0,2},{2,4},{4,6},{6,7},{7,5},{5,3},{3,1},{1,0},{8,10},{10,12},{12... | collective-permute-start | bytes 2359304 | tf_op jit(solution)/shard_map/ppermute | solution.py:596
  216.9 20.5 %collective-permute-start.20 = (bf16[24,16,1024]{2,1,0:T(8,128)(2,1)S(1)}, bf16[24,16,1024]{2,1,0:T(8,128)(2,1)S(1)}, u32[]{:S(2)}, u32[]{:S(2)}) collective-permute-start(bf16[24,16,1024]{2,1,0:T(8,128)(2,1)S(1)} %bitcast.83), channel_id=1, source_target_pairs={{2,0},{4,2},{6,4},{7,6},{5,7},{3,5},{1,3},{0,1},{10,8},{12,10},{14... | collective-permute-start | bytes 2359304 | tf_op jit(solution)/shard_map/ppermute | solution.py:596
  217.4 35.3 %collective-permute-start.37 = (bf16[24,16,1024]{2,1,0:T(8,128)(2,1)S(1)}, bf16[24,16,1024]{2,1,0:T(8,128)(2,1)S(1)}, u32[]{:S(2)}, u32[]{:S(2)}) collective-permute-start(bf16[24,16,1024]{2,1,0:T(8,128)(2,1)S(1)} %bitcast.74), channel_id=1, source_target_pairs={{0,2},{2,4},{4,6},{6,7},{7,5},{5,3},{3,1},{1,0},{8,10},{10,12},{12... | collective-permute-start | bytes 2359304 | tf_op jit(solution)/shard_map/ppermute | solution.py:596
  218.9 35.3 %collective-permute-start.38 = (bf16[24,16,1024]{2,1,0:T(8,128)(2,1)S(1)}, bf16[24,16,1024]{2,1,0:T(8,128)(2,1)S(1)}, u32[]{:S(2)}, u32[]{:S(2)}) collective-permute-start(bf16[24,16,1024]{2,1,0:T(8,128)(2,1)S(1)} %bitcast.75), channel_id=1, source_target_pairs={{2,0},{4,2},{6,4},{7,6},{5,7},{3,5},{1,3},{0,1},{10,8},{12,10},{14... | collective-permute-start | bytes 2359304 | tf_op jit(solution)/shard_map/ppermute | solution.py:596
  237.4 32.1 %collective-permute-start.31 = (bf16[24,16,1024]{2,1,0:T(8,128)(2,1)S(1)}, bf16[24,16,1024]{2,1,0:T(8,128)(2,1)S(1)}, u32[]{:S(2)}, u32[]{:S(2)}) collective-permute-start(bf16[24,16,1024]{2,1,0:T(8,128)(2,1)S(1)} %collective-permute-done.19.refs_1_), channel_id=1, source_target_pairs={{0,2},{2,4},{4,6},{6,7},{7,5},{5,3},{3,1},{1,0},{8,10},{10,12},{12... | collective-permute-start | bytes 2359304 | tf_op jit(solution)/shard_map/ppermute | solution.py:596
  238.9 32.2 %collective-permute-start.32 = (bf16[24,16,1024]{2,1,0:T(8,128)(2,1)S(1)}, bf16[24,16,1024]{2,1,0:T(8,128)(2,1)S(1)}, u32[]{:S(2)}, u32[]{:S(2)}) collective-permute-start(bf16[24,16,1024]{2,1,0:T(8,128)(2,1)S(1)} %collective-permute-done.20.refs_7_), channel_id=1, source_target_pairs={{2,0},{4,2},{6,4},{7,6},{5,7},{3,5},{1,3},{0,1},{10,8},{12,10},{14... | collective-permute-start | bytes 2359304 | tf_op jit(solution)/shard_map/ppermute | solution.py:596
  254.2 32.1 %collective-permute-start.39 = (bf16[24,16,1024]{2,1,0:T(8,128)(2,1)S(1)}, bf16[24,16,1024]{2,1,0:T(8,128)(2,1)S(1)}, u32[]{:S(2)}, u32[]{:S(2)}) collective-permute-start(bf16[24,16,1024]{2,1,0:T(8,128)(2,1)S(1)} %collective-permute-done.37.refs_1_), channel_id=1, source_target_pairs={{0,2},{2,4},{4,6},{6,7},{7,5},{5,3},{3,1},{1,0},{8,10},{10,12},{12... | collective-permute-start | bytes 2359304 | tf_op jit(solution)/shard_map/ppermute | solution.py:596
  255.8 32.2 %collective-permute-start.40 = (bf16[24,16,1024]{2,1,0:T(8,128)(2,1)S(1)}, bf16[24,16,1024]{2,1,0:T(8,128)(2,1)S(1)}, u32[]{:S(2)}, u32[]{:S(2)}) collective-permute-start(bf16[24,16,1024]{2,1,0:T(8,128)(2,1)S(1)} %collective-permute-done.38.refs_7_), channel_id=1, source_target_pairs={{2,0},{4,2},{6,4},{7,6},{5,7},{3,5},{1,3},{0,1},{10,8},{12,10},{14... | collective-permute-start | bytes 2359304 | tf_op jit(solution)/shard_map/ppermute | solution.py:596
  271.1 32.1 %collective-permute-start.33 = (bf16[24,16,1024]{2,1,0:T(8,128)(2,1)S(1)}, bf16[24,16,1024]{2,1,0:T(8,128)(2,1)S(1)}, u32[]{:S(2)}, u32[]{:S(2)}) collective-permute-start(bf16[24,16,1024]{2,1,0:T(8,128)(2,1)S(1)} %collective-permute-done.31.refs_2_), channel_id=1, source_target_pairs={{0,2},{2,4},{4,6},{6,7},{7,5},{5,3},{3,1},{1,0},{8,10},{10,12},{12... | collective-permute-start | bytes 2359304 | tf_op jit(solution)/shard_map/ppermute | solution.py:596
  272.7 32.2 %collective-permute-start.34 = (bf16[24,16,1024]{2,1,0:T(8,128)(2,1)S(1)}, bf16[24,16,1024]{2,1,0:T(8,128)(2,1)S(1)}, u32[]{:S(2)}, u32[]{:S(2)}) collective-permute-start(bf16[24,16,1024]{2,1,0:T(8,128)(2,1)S(1)} %collective-permute-done.32.refs_6_), channel_id=1, source_target_pairs={{2,0},{4,2},{6,4},{7,6},{5,7},{3,5},{1,3},{0,1},{10,8},{12,10},{14... | collective-permute-start | bytes 2359304 | tf_op jit(solution)/shard_map/ppermute | solution.py:596
  288.0 32.1 %collective-permute-start.46 = (bf16[24,16,1024]{2,1,0:T(8,128)(2,1)S(1)}, bf16[24,16,1024]{2,1,0:T(8,128)(2,1)S(1)}, u32[]{:S(2)}, u32[]{:S(2)}) collective-permute-start(bf16[24,16,1024]{2,1,0:T(8,128)(2,1)S(1)} %collective-permute-done.39.refs_2_), channel_id=1, source_target_pairs={{0,2},{2,4},{4,6},{6,7},{7,5},{5,3},{3,1},{1,0},{8,10},{10,12},{12... | collective-permute-start | bytes 2359304 | tf_op jit(solution)/shard_map/ppermute | solution.py:596
  289.5 32.2 %collective-permute-start.47 = (bf16[24,16,1024]{2,1,0:T(8,128)(2,1)S(1)}, bf16[24,16,1024]{2,1,0:T(8,128)(2,1)S(1)}, u32[]{:S(2)}, u32[]{:S(2)}) collective-permute-start(bf16[24,16,1024]{2,1,0:T(8,128)(2,1)S(1)} %collective-permute-done.40.refs_6_), channel_id=1, source_target_pairs={{2,0},{4,2},{6,4},{7,6},{5,7},{3,5},{1,3},{0,1},{10,8},{12,10},{14... | collective-permute-start | bytes 2359304 | tf_op jit(solution)/shard_map/ppermute | solution.py:596
  304.8 23.7 %collective-permute-start.35 = (bf16[12,16,1024]{2,1,0:T(8,128)(2,1)S(1)}, bf16[12,16,1024]{2,1,0:T(8,128)(2,1)S(1)}, u32[]{:S(2)}, u32[]{:S(2)}) collective-permute-start(bf16[12,16,1024]{2,1,0:T(8,128)(2,1)S(1)} %slice.131), channel_id=1, source_target_pairs={{0,2},{2,4},{4,6},{6,7},{7,5},{5,3},{3,1},{1,0},{8,10},{10,12},{12... | collective-permute-start | bytes 1179656 | tf_op jit(solution)/shard_map/ppermute | solution.py:596
  310.5 23.5 %collective-permute-start.41 = (bf16[12,16,1024]{2,1,0:T(8,128)(2,1)S(1)}, bf16[12,16,1024]{2,1,0:T(8,128)(2,1)S(1)}, u32[]{:S(2)}, u32[]{:S(2)}) collective-permute-start(bf16[12,16,1024]{2,1,0:T(8,128)(2,1)S(1)} %slice.137), channel_id=1, source_target_pairs={{2,0},{4,2},{6,4},{7,6},{5,7},{3,5},{1,3},{0,1},{10,8},{12,10},{14... | collective-permute-start | bytes 1179656 | tf_op jit(solution)/shard_map/ppermute | solution.py:596
  408.8 20.9 %all-to-all-start = ((bf16[4,8,64,128]{3,2,1,0:T(8,128)(2,1)}), bf16[4,8,64,128]{3,2,1,0:T(8,128)(2,1)S(1)}, u32[]{:S(2)}, u32[]{:S(2)}) async-start(bf16[4,8,64,128]{3,2,1,0:T(8,128)(2,1)} %bitcast.109), calls=%async_computation | async-start | bytes 1048576 | tf_op jit(solution)/shard_map/all_to_all | solution.py:566
  (84 other events, 1994.9 us)

commit v4 on v3

--- a/solution.py
+++ b/solution.py
@@ -205,6 +205,8 @@
 
 def into_order(pieces, halves, spread, block, blocks):
     number = len(pieces) // halves
+    together = math.gcd(blocks, *[at // block for _, at in pieces])
+    block, blocks = block * together, blocks // together
     rows = block * blocks
     width = spread.shape[2]
     return pl.pallas_call(

time: 480 us -> 478 us (level)
  Pallas kernels: 104 us -> 95.2 us
  waiting for transfers between devices: 223 us -> 230 us
    pallas_call x8, Pallas kernels: 15.6 us -> 7.05 us  [into_order(): pl.pallas_call(functools.partial(order_kernel, number, halves), grid=(blo...]
    ppermute x64, waiting for transfers between devices: 184 us -> 191 us  [body(): got = [lax.ppermute(p, 'row', r) for p, r in zip(going, (onward, backward))]]
  transfers between devices with their start and end apart: 80 -> 80, of which waited for: 56 -> 55; matrix products, arithmetic and copies ran while one was open for 8% -> 8% of each run, Pallas kernels for 17% -> 16%
where the time goes in v4:
time: 478 us; the launch traced here: 472 us
  waiting for transfers between devices  230 us (48%)
  starting transfers between devices  97.1 us (20%)
  Pallas kernels  95.2 us (20%)
  other arithmetic  28.1 us (6%)
  local copies, waits for them, and re-layouts  19.7 us (4%)
    ppermute x64, waiting for transfers between devices, body(): got = [lax.ppermute(p, 'row', r) for p, r in zip(going, (onward, backward))]  191 us
    ppermute x64, starting transfers between devices, body(): got = [lax.ppermute(p, 'row', r) for p, r in zip(going, (onward, backward))]  69 us
    pallas_call x11, Pallas kernels, products_of(): pl.pallas_call(functools.partial(products_kernel, ends, frames, aliased,...  64.8 us
    ppermute x2, waiting for transfers between devices, from_behind(): return lax.ppermute(block, axis, route)  29.4 us
    pallas_call x2, Pallas kernels, front(): pl.pallas_call(functools.partial(front_kernel, rows, steps, fold, parcels...  18.7 us
    another operation x2, other arithmetic  18.2 us
    ppermute x12, starting transfers between devices, body(): lax.ppermute(piece, 'chan', route)  11.1 us
  transfers between devices with their start and end apart: 80, of which 55 were waited for; matrix products, arithmetic and copies ran while one was open for 8% of the time, Pallas kernels for 16%

profile of v4, /device:TPU:0, one launch (start us, length us, event | category | flops | bytes accessed | tf_op | source)
XLA Modules:
  0.0 471.7 jit_solution(17913896847498784806)
XLA Ops:
  3.5 6.1 %collective-permute-start = (bf16[4,32,7168]{2,1,0:T(8,128)(2,1)}, bf16[4,32,7168]{2,1,0:T(8,128)(2,1)}, u32[]{:S(2)}, u32[]{:S(2)}) collective-permute-start(bf16[4,32,7168]{2,1,0:T(8,128)(2,1)} %slice.120), channel_id=1, source_target_pairs={{0,1},{1,2},{2,3},{3,4},{4,5},{5,6},{6,7},{8,9},{9,10},{10,11},{11... | collective-permute-start | bytes 5505032 | tf_op jit(solution)/shard_map/ppermute | solution.py:38
  9.6 9.1 %multiply_convert_fusion.3 = (bf16[4,1,128,1024]{3,2,1,0:T(8,128)(2,1)S(1)}, bf16[4,1,128,1024]{3,2,1,0:T(8,128)(2,1)S(1)}) fusion(s32[4,128]{1,0:T(4,128)S(1)} %multiply_add_fusion.1), kind=kLoop, calls=%fused_computation.26 | loop fusion | flops 9961472 | bytes 2099200 | tf_op jit(solution)/shard_map/convert.2
  28.7 9.1 %multiply_convert_fusion = (bf16[1,4,128,1024]{3,2,1,0:T(8,128)(2,1)S(1)}, bf16[1,4,128,1024]{3,2,1,0:T(8,128)(2,1)S(1)}) fusion(s32[4,128]{1,0:T(4,128)S(1)} %multiply_add_fusion.1), kind=kLoop, calls=%fused_computation.21 | loop fusion | flops 9961472 | bytes 2099200 | tf_op jit(solution)/shard_map/convert.1
  39.6 9.4 %collective-permute-done = bf16[4,32,7168]{2,1,0:T(8,128)(2,1)} collective-permute-done((bf16[4,32,7168]{2,1,0:T(8,128)(2,1)}, bf16[4,32,7168]{2,1,0:T(8,128)(2,1)}, u32[]{:S(2)}, u32[]{:S(2)}) %collective-permute-start) | collective-permute-done | bytes 1835040 | tf_op jit(solution)/shard_map/ppermute | solution.py:38
  49.1 9.3 %front.2 = (bf16[2048,128]{1,0:T(8,128)(2,1)S(1)}, bf16[2048,128]{1,0:T(8,128)(2,1)S(1)}, bf16[2048,128]{1,0:T(8,128)(2,1)S(1)}, bf16[2048,128]{1,0:T(8,128)(2,1)S(1)}) custom-call(s32[2]{0:T(128)S(1)} %pad_add_fusion.place, bf16[256,8192]{1,0:T(8,128)(2,1)S(1)} %bitcast.72, bf16[128,7168]{1,0:T(8,128)(2,1)} %bitcast.3.before, ...), custom_call_target="tpu_custom_call" | custom-call | flops 12884901888 | bytes 25165824 | tf_op jit(solution)/shard_map/front/pallas_call | solution.py:180
  62.1 5.2 %negate_multiply_fusion = (f32[10,32,1024]{2,1,0:T(8,128)S(1)}, f32[10,32,1024]{2,1,0:T(8,128)S(1)}) fusion(s32[10]{0:T(128)S(1)} %broadcast_add_fusion, s32[32,1024]{1,0:T(8,128)S(1)} %get-tuple-element.259), kind=kLoop, calls=%fused_computation.36 | loop fusion | flops 5570560 | bytes 2752552 | tf_op jit(solution)/shard_map/mul | solution.py:75
  67.3 20.0 %collective-permute-done.1 = bf16[4,32,7168]{2,1,0:T(8,128)(2,1)} collective-permute-done((bf16[4,32,7168]{2,1,0:T(8,128)(2,1)}, bf16[4,32,7168]{2,1,0:T(8,128)(2,1)}, u32[]{:S(2)}, u32[]{:S(2)}) %collective-permute-start.1) | collective-permute-done | bytes 1835040 | tf_op jit(solution)/shard_map/ppermute | solution.py:38
  87.3 9.3 %front.3 = (bf16[256,128]{1,0:T(8,128)(2,1)S(1)}, bf16[384,128]{1,0:T(8,128)(2,1)S(1)}, bf16[1408,128]{1,0:T(8,128)(2,1)S(1)}, bf16[256,128]{1,0:T(8,128)(2,1)S(...) custom-call(s32[2]{0:T(128)S(1)} %pad_add_fusion.place, ...), custom_call_target="tpu_custom_call" | custom-call | flops 12884901888 | bytes 25165824 | tf_op jit(solution)/shard_map/front/pallas_call | solution.py:180
  116.9 8.7 %collective-permute-done.24.refs_1_ = bf16[24,16,1024]{2,1,0:T(8,128)(2,1)S(1)} collective-permute-done((bf16[24,16,1024]{2,1,0:T(8,128)(2,1)S(1)}, bf16[24,16,1024]{2,1,0:T(8,128)(2,1)S(1)}, u32[]{:S(2)}, u32[]{:S(2)}) %collective-permute-start.24) | collective-permute-done | bytes 786464 | tf_op jit(solution)/shard_map/ppermute | solution.py:598
  143.0 21.9 %collective-permute-done.13.refs_2_ = bf16[16,16,1024]{2,1,0:T(8,128)(2,1)S(1)} collective-permute-done((bf16[16,16,1024]{2,1,0:T(8,128)(2,1)S(1)}, bf16[16,16,1024]{2,1,0:T(8,128)(2,1)S(1)}, u32[]{:S(2)}, u32[]{:S(2)}) %collective-permute-start.13) | collective-permute-done | bytes 524320 | tf_op jit(solution)/shard_map/ppermute | solution.py:598
  173.9 9.0 %collective-permute-done.15.refs_3_ = bf16[16,16,1024]{2,1,0:T(8,128)(2,1)S(1)} collective-permute-done((bf16[16,16,1024]{2,1,0:T(8,128)(2,1)S(1)}, bf16[16,16,1024]{2,1,0:T(8,128)(2,1)S(1)}, u32[]{:S(2)}, u32[]{:S(2)}) %collective-permute-start.15) | collective-permute-done | bytes 524320 | tf_op jit(solution)/shard_map/ppermute | solution.py:598
  189.6 10.2 %collective-permute-done.28.refs_3_ = bf16[24,16,1024]{2,1,0:T(8,128)(2,1)S(1)} collective-permute-done((bf16[24,16,1024]{2,1,0:T(8,128)(2,1)S(1)}, bf16[24,16,1024]{2,1,0:T(8,128)(2,1)S(1)}, u32[]{:S(2)}, u32[]{:S(2)}) %collective-permute-start.28) | collective-permute-done | bytes 786464 | tf_op jit(solution)/shard_map/ppermute | solution.py:598
  207.2 6.6 %products.11 = (bf16[128,2,128,1024]{3,2,1,0:T(8,128)(2,1)}, bf16[16,32,128]{2,1,0:T(8,128)(2,1)S(1)}) custom-call(s32[2]{0:T(128)S(1)} %pad_add_fusion.place, bf16[16,16,1024]{2,1,0:T(8,128)(2,1)S(1)} %bitcast.108, bf16[16,16,1024]{2,1,0:T(8,128)(2,1)S(1)} %collective-permute-done.11.refs_1_, bf16[16,16,1024]{2,1,0:T(8,128)(2,1)S(1)} %collective-permute-done.13.refs_2_, ...), custom_call_target="tpu_custom_call" | custom-call | flops 19327352832 | bytes 37748736 | tf_op jit(solution)/shard_map/products/pallas_call | solution.py:354
  217.9 5.4 %products.12 = (bf16[128,2,128,1024]{3,2,1,0:T(8,128)(2,1)}, bf16[12,32,128]{2,1,0:T(8,128)(2,1)S(1)}) custom-call(s32[2]{0:T(128)S(1)} %pad_add_fusion.place, bf16[24,16,1024]{2,1,0:T(8,128)(2,1)S(1)} %bitcast.80, bf16[24,16,1024]{2,1,0:T(8,128)(2,1)S(1)} %collective-permute-done.24.refs_1_, ...), custom_call_target="tpu_custom_call", output_to_operand_aliasing={{0}: (13, {})} | custom-call | flops 14495514624 | bytes 28311552 | tf_op jit(solution)/shard_map/products/pallas_call | solution.py:354
  223.3 11.0 %collective-permute-done.19.refs_1_ = bf16[24,16,1024]{2,1,0:T(8,128)(2,1)S(1)} collective-permute-done((bf16[24,16,1024]{2,1,0:T(8,128)(2,1)S(1)}, bf16[24,16,1024]{2,1,0:T(8,128)(2,1)S(1)}, u32[]{:S(2)}, u32[]{:S(2)}) %collective-permute-start.19) | collective-permute-done | bytes 786464 | tf_op jit(solution)/shard_map/ppermute | solution.py:598
  237.9 13.3 %collective-permute-done.37.refs_1_ = bf16[24,16,1024]{2,1,0:T(8,128)(2,1)S(1)} collective-permute-done((bf16[24,16,1024]{2,1,0:T(8,128)(2,1)S(1)}, bf16[24,16,1024]{2,1,0:T(8,128)(2,1)S(1)}, u32[]{:S(2)}, u32[]{:S(2)}) %collective-permute-start.37) | collective-permute-done | bytes 786464 | tf_op jit(solution)/shard_map/ppermute | solution.py:598
  254.7 13.3 %collective-permute-done.31.refs_2_ = bf16[24,16,1024]{2,1,0:T(8,128)(2,1)S(1)} collective-permute-done((bf16[24,16,1024]{2,1,0:T(8,128)(2,1)S(1)}, bf16[24,16,1024]{2,1,0:T(8,128)(2,1)S(1)}, u32[]{:S(2)}, u32[]{:S(2)}) %collective-permute-start.31) | collective-permute-done | bytes 786464 | tf_op jit(solution)/shard_map/ppermute | solution.py:598
  271.6 5.4 %products.13 = (bf16[128,2,128,1024]{3,2,1,0:T(8,128)(2,1)}, bf16[12,32,128]{2,1,0:T(8,128)(2,1)S(1)}) custom-call(s32[2]{0:T(128)S(1)} %pad_add_fusion.place, bf16[24,16,1024]{2,1,0:T(8,128)(2,1)S(1)} %bitcast.81, bf16[24,16,1024]{2,1,0:T(8,128)(2,1)S(1)} %collective-permute-done.24.refs_1_, ...), custom_call_target="tpu_custom_call", output_to_operand_aliasing={{0}: (13, {})} | custom-call | flops 14495514624 | bytes 28311552 | tf_op jit(solution)/shard_map/products/pallas_call | solution.py:354
  277.0 7.8 %collective-permute-done.39.refs_2_ = bf16[24,16,1024]{2,1,0:T(8,128)(2,1)S(1)} collective-permute-done((bf16[24,16,1024]{2,1,0:T(8,128)(2,1)S(1)}, bf16[24,16,1024]{2,1,0:T(8,128)(2,1)S(1)}, u32[]{:S(2)}, u32[]{:S(2)}) %collective-permute-start.39) | collective-permute-done | bytes 786464 | tf_op jit(solution)/shard_map/ppermute | solution.py:598
  288.4 13.3 %collective-permute-done.33.refs_3_ = bf16[24,16,1024]{2,1,0:T(8,128)(2,1)S(1)} collective-permute-done((bf16[24,16,1024]{2,1,0:T(8,128)(2,1)S(1)}, bf16[24,16,1024]{2,1,0:T(8,128)(2,1)S(1)}, u32[]{:S(2)}, u32[]{:S(2)}) %collective-permute-start.33) | collective-permute-done | bytes 786464 | tf_op jit(solution)/shard_map/ppermute | solution.py:598
  307.3 11.2 %collective-permute-done.46.refs_3_ = bf16[24,16,1024]{2,1,0:T(8,128)(2,1)S(1)} collective-permute-done((bf16[24,16,1024]{2,1,0:T(8,128)(2,1)S(1)}, bf16[24,16,1024]{2,1,0:T(8,128)(2,1)S(1)}, u32[]{:S(2)}, u32[]{:S(2)}) %collective-permute-start.46) | collective-permute-done | bytes 786464 | tf_op jit(solution)/shard_map/ppermute | solution.py:598
  322.3 4.7 collective-permute-done.35.refs_4_
  327.0 5.5 %products.14 = (bf16[128,2,128,1024]{3,2,1,0:T(8,128)(2,1)}, bf16[12,32,128]{2,1,0:T(8,128)(2,1)S(1)}) custom-call(s32[2]{0:T(128)S(1)} %pad_add_fusion.place, bf16[24,16,1024]{2,1,0:T(8,128)(2,1)S(1)} %bitcast.84, bf16[24,16,1024]{2,1,0:T(8,128)(2,1)S(1)} %collective-permute-done.19.refs_1_, ...), custom_call_target="tpu_custom_call", output_to_operand_aliasing={{0}: (13, {})} | custom-call | flops 14495514624 | bytes 28311552 | tf_op jit(solution)/shard_map/products/pallas_call | solution.py:354
  338.9 5.4 %products.15 = (bf16[128,2,128,1024]{3,2,1,0:T(8,128)(2,1)}, bf16[12,32,128]{2,1,0:T(8,128)(2,1)S(1)}) custom-call(s32[2]{0:T(128)S(1)} %pad_add_fusion.place, bf16[24,16,1024]{2,1,0:T(8,128)(2,1)S(1)} %bitcast.85, bf16[24,16,1024]{2,1,0:T(8,128)(2,1)S(1)} %collective-permute-done.19.refs_1_, ...), custom_call_target="tpu_custom_call", output_to_operand_aliasing={{0}: (13, {})} | custom-call | flops 14495514624 | bytes 28311552 | tf_op jit(solution)/shard_map/products/pallas_call | solution.py:354
  356.5 5.5 %products.16 = (bf16[128,2,128,1024]{3,2,1,0:T(8,128)(2,1)}, bf16[12,32,128]{2,1,0:T(8,128)(2,1)S(1)}) custom-call(s32[2]{0:T(128)S(1)} %pad_add_fusion.place, bf16[24,16,1024]{2,1,0:T(8,128)(2,1)S(1)} %bitcast.76, bf16[24,16,1024]{2,1,0:T(8,128)(2,1)S(1)} %collective-permute-done.37.refs_1_, ...), custom_call_target="tpu_custom_call", output_to_operand_aliasing={{0}: (13, {})} | custom-call | flops 14495514624 | bytes 28311552 | tf_op jit(solution)/shard_map/products/pallas_call | solution.py:354
  373.6 5.5 %products.17 = (bf16[128,2,128,1024]{3,2,1,0:T(8,128)(2,1)}, bf16[12,32,128]{2,1,0:T(8,128)(2,1)S(1)}) custom-call(s32[2]{0:T(128)S(1)} %pad_add_fusion.place, bf16[24,16,1024]{2,1,0:T(8,128)(2,1)S(1)} %bitcast.77, bf16[24,16,1024]{2,1,0:T(8,128)(2,1)S(1)} %collective-permute-done.37.refs_1_, ...), custom_call_target="tpu_custom_call", output_to_operand_aliasing={{0}: (13, {})} | custom-call | flops 14495514624 | bytes 28311552 | tf_op jit(solution)/shard_map/products/pallas_call | solution.py:354
  388.2 5.1 %collective-permute-done.61.refs_4_ = bf16[4,16,1024]{2,1,0:T(8,128)(2,1)S(1)} collective-permute-done((bf16[4,16,1024]{2,1,0:T(8,128)(2,1)S(1)}, bf16[4,16,1024]{2,1,0:T(8,128)(2,1)S(1)}, u32[]{:S(2)}, u32[]{:S(2)}) %collective-permute-start.61) | collective-permute-done | bytes 131104 | tf_op jit(solution)/shard_map/ppermute | solution.py:598
  397.6 6.6 %products.18 = (bf16[128,2,128,1024]{3,2,1,0:T(8,128)(2,1)}, bf16[16,32,128]{2,1,0:T(8,128)(2,1)S(1)}) custom-call(s32[2]{0:T(128)S(1)} %pad_add_fusion.place, bf16[16,16,1024]{2,1,0:T(8,128)(2,1)S(1)} %bitcast.88, bf16[16,16,1024]{2,1,0:T(8,128)(2,1)S(1)} %collective-permute-done.42.refs_1_, ...), custom_call_target="tpu_custom_call", output_to_operand_aliasing={{0}: (14, {})} | custom-call | flops 19327352832 | bytes 37748736 | tf_op jit(solution)/shard_map/products/pallas_call | solution.py:354
  428.4 5.3 %collective-permute-done.71.refs_7_ = bf16[8,16,1024]{2,1,0:T(8,128)(2,1)S(1)} collective-permute-done((bf16[8,16,1024]{2,1,0:T(8,128)(2,1)}, bf16[8,16,1024]{2,1,0:T(8,128)(2,1)S(1)}, u32[]{:S(2)}, u32[]{:S(2)}) %collective-permute-start.71) | collective-permute-done | bytes 262176 | tf_op jit(solution)/shard_map/ppermute | solution.py:598
  445.9 6.5 %products.20 = bf16[16,32,128]{2,1,0:T(8,128)(2,1)} custom-call(s32[2]{0:T(128)} %copy-done.22, bf16[8,16,1024]{2,1,0:T(8,128)(2,1)} %bitcast.93, bf16[8,16,1024]{2,1,0:T(8,128)(2,1)} %bitcast.100, bf16[8,16,1024]{2,1,0:T(8,128)(2,1)} %collective-permute-done.54.refs_2_, bf16[8,16,1024]{2,1,0:T(8,128)(2,1)} %collective-permute-done.63.refs_3_, ...), custom_call_target="tpu_custom_call" | custom-call | flops 19327352832 | bytes 37748736 | tf_op jit(solution)/shard_map/products/pallas_call | solution.py:354
  457.8 8.2 %products.21 = bf16[128,2,128,1024]{3,2,1,0:T(8,128)(2,1)} custom-call(s32[2]{0:T(128)} %copy-done.22, bf16[8,16,1024]{2,1,0:T(8,128)(2,1)} %bitcast.94, bf16[8,16,1024]{2,1,0:T(8,128)(2,1)} %bitcast.101, bf16[8,16,1024]{2,1,0:T(8,128)(2,1)} %collective-permute-done.54.refs_2_, ...), custom_call_target="tpu_custom_call", output_to_operand_aliasing={{}: (19, {})} | custom-call | flops 19327352832 | bytes 37748736 | tf_op jit(solution)/shard_map/products/pallas_call | solution.py:354
  466.6 4.6 synthesis.1
  (273 shorter events, 192.4 us)
Async XLA Ops:
  3.5 45.6 %collective-permute-start = (bf16[4,32,7168]{2,1,0:T(8,128)(2,1)}, bf16[4,32,7168]{2,1,0:T(8,128)(2,1)}, u32[]{:S(2)}, u32[]{:S(2)}) collective-permute-start(bf16[4,32,7168]{2,1,0:T(8,128)(2,1)} %slice.120), channel_id=1, source_target_pairs={{0,1},{1,2},{2,3},{3,4},{4,5},{5,6},{6,7},{8,9},{9,10},{10,11},{11... | collective-permute-start | bytes 5505032 | tf_op jit(solution)/shard_map/ppermute | solution.py:38
  21.8 65.4 %collective-permute-start.1 = (bf16[4,32,7168]{2,1,0:T(8,128)(2,1)}, bf16[4,32,7168]{2,1,0:T(8,128)(2,1)}, u32[]{:S(2)}, u32[]{:S(2)}) collective-permute-start(bf16[4,32,7168]{2,1,0:T(8,128)(2,1)} %slice.121), channel_id=1, source_target_pairs={{0,1},{1,2},{2,3},{3,4},{4,5},{5,6},{6,7},{8,9},{9,10},{10,11},{11... | collective-permute-start | bytes 5505032 | tf_op jit(solution)/shard_map/ppermute | solution.py:38
  58.4 28.8 %collective-permute-start.2 = (bf16[2048,128]{1,0:T(8,128)(2,1)S(1)}, bf16[2048,128]{1,0:T(8,128)(2,1)S(1)}, u32[]{:S(2)}, u32[]{:S(2)}) collective-permute-start(bf16[2048,128]{1,0:T(8,128)(2,1)S(1)} %get-tuple-element.133), channel_id=1, source_target_pairs={{0,8},{8,16},{16,24},{24,0},{1,9},{9,17},{17,25},{25,1},{2,10},{10... | collective-permute-start | bytes 1572872 | tf_op jit(solution)/shard_map/ppermute | solution.py:500
  58.5 28.8 %collective-permute-start.3 = (bf16[2048,128]{1,0:T(8,128)(2,1)S(1)}, bf16[2048,128]{1,0:T(8,128)(2,1)S(1)}, u32[]{:S(2)}, u32[]{:S(2)}) collective-permute-start(bf16[2048,128]{1,0:T(8,128)(2,1)S(1)} %get-tuple-element.134), channel_id=1, source_target_pairs={{0,16},{8,24},{16,0},{24,8},{1,17},{9,25},{17,1},{25,9},{2,18},{10... | collective-permute-start | bytes 1572872 | tf_op jit(solution)/shard_map/ppermute | solution.py:500
  60.0 27.2 %collective-permute-start.4 = (bf16[2048,128]{1,0:T(8,128)(2,1)S(1)}, bf16[2048,128]{1,0:T(8,128)(2,1)S(1)}, u32[]{:S(2)}, u32[]{:S(2)}) collective-permute-start(bf16[2048,128]{1,0:T(8,128)(2,1)S(1)} %get-tuple-element.135), channel_id=1, source_target_pairs={{0,24},{8,0},{16,8},{24,16},{1,25},{9,1},{17,9},{25,17},{2,26},{10... | collective-permute-start | bytes 1572872 | tf_op jit(solution)/shard_map/ppermute | solution.py:500
  104.2 21.4 %collective-permute-start.24 = (bf16[24,16,1024]{2,1,0:T(8,128)(2,1)S(1)}, bf16[24,16,1024]{2,1,0:T(8,128)(2,1)S(1)}, u32[]{:S(2)}, u32[]{:S(2)}) collective-permute-start(bf16[24,16,1024]{2,1,0:T(8,128)(2,1)S(1)} %bitcast.78), channel_id=1, source_target_pairs={{0,2},{2,4},{4,6},{6,7},{7,5},{5,3},{3,1},{1,0},{8,10},{10,12},{12... | collective-permute-start | bytes 2359304 | tf_op jit(solution)/shard_map/ppermute | solution.py:598
  107.7 20.0 %collective-permute-start.25 = (bf16[24,16,1024]{2,1,0:T(8,128)(2,1)S(1)}, bf16[24,16,1024]{2,1,0:T(8,128)(2,1)S(1)}, u32[]{:S(2)}, u32[]{:S(2)}) collective-permute-start(bf16[24,16,1024]{2,1,0:T(8,128)(2,1)S(1)} %bitcast.79), channel_id=1, source_target_pairs={{2,0},{4,2},{6,4},{7,6},{5,7},{3,5},{1,3},{0,1},{10,8},{12,10},{14... | collective-permute-start | bytes 2359304 | tf_op jit(solution)/shard_map/ppermute | solution.py:598
  113.2 17.2 %collective-permute-start.6 = (bf16[1408,128]{1,0:T(8,128)(2,1)S(1)}, bf16[1408,128]{1,0:T(8,128)(2,1)S(1)}, u32[]{:S(2)}, u32[]{:S(2)}) collective-permute-start(bf16[1408,128]{1,0:T(8,128)(2,1)S(1)} %get-tuple-element.141), channel_id=1, source_target_pairs={{0,16},{8,24},{16,0},{24,8},{1,17},{9,25},{17,1},{25,9},{2,18},{10... | collective-permute-start | bytes 1081352 | tf_op jit(solution)/shard_map/ppermute | solution.py:500
  115.1 21.7 %collective-permute-start.11 = (bf16[16,16,1024]{2,1,0:T(8,128)(2,1)S(1)}, bf16[16,16,1024]{2,1,0:T(8,128)(2,1)S(1)}, u32[]{:S(2)}, u32[]{:S(2)}) collective-permute-start(bf16[16,16,1024]{2,1,0:T(8,128)(2,1)S(1)} %bitcast.106), channel_id=1, source_target_pairs={{0,2},{2,4},{4,6},{6,7},{7,5},{5,3},{3,1},{1,0},{8,10},{10,12},{12... | collective-permute-start | bytes 1572872 | tf_op jit(solution)/shard_map/ppermute | solution.py:598
  128.8 41.3 %collective-permute-start.26 = (bf16[24,16,1024]{2,1,0:T(8,128)(2,1)S(1)}, bf16[24,16,1024]{2,1,0:T(8,128)(2,1)S(1)}, u32[]{:S(2)}, u32[]{:S(2)}) collective-permute-start(bf16[24,16,1024]{2,1,0:T(8,128)(2,1)S(1)} %collective-permute-done.24.refs_1_), channel_id=1, source_target_pairs={{0,2},{2,4},{4,6},{6,7},{7,5},{5,3},{3,1},{1,0},{8,10},{10,12},{12... | collective-permute-start | bytes 2359304 | tf_op jit(solution)/shard_map/ppermute | solution.py:598
  130.4 39.7 %collective-permute-start.27 = (bf16[24,16,1024]{2,1,0:T(8,128)(2,1)S(1)}, bf16[24,16,1024]{2,1,0:T(8,128)(2,1)S(1)}, u32[]{:S(2)}, u32[]{:S(2)}) collective-permute-start(bf16[24,16,1024]{2,1,0:T(8,128)(2,1)S(1)} %collective-permute-done.25.refs_7_), channel_id=1, source_target_pairs={{2,0},{4,2},{6,4},{7,6},{5,7},{3,5},{1,3},{0,1},{10,8},{12,10},{14... | collective-permute-start | bytes 2359304 | tf_op jit(solution)/shard_map/ppermute | solution.py:598
  140.9 23.9 %collective-permute-start.13 = (bf16[16,16,1024]{2,1,0:T(8,128)(2,1)S(1)}, bf16[16,16,1024]{2,1,0:T(8,128)(2,1)S(1)}, u32[]{:S(2)}, u32[]{:S(2)}) collective-permute-start(bf16[16,16,1024]{2,1,0:T(8,128)(2,1)S(1)} %collective-permute-done.11.refs_1_), channel_id=1, source_target_pairs={{0,2},{2,4},{4,6},{6,7},{7,5},{5,3},{3,1},{1,0},{8,10},{10,12},{12... | collective-permute-start | bytes 1572872 | tf_op jit(solution)/shard_map/ppermute | solution.py:598
  142.9 25.2 %collective-permute-start.14 = (bf16[16,16,1024]{2,1,0:T(8,128)(2,1)S(1)}, bf16[16,16,1024]{2,1,0:T(8,128)(2,1)S(1)}, u32[]{:S(2)}, u32[]{:S(2)}) collective-permute-start(bf16[16,16,1024]{2,1,0:T(8,128)(2,1)S(1)} %collective-permute-done.12.refs_8_), channel_id=1, source_target_pairs={{2,0},{4,2},{6,4},{7,6},{5,7},{3,5},{1,3},{0,1},{10,8},{12,10},{14... | collective-permute-start | bytes 1572872 | tf_op jit(solution)/shard_map/ppermute | solution.py:598
  170.1 29.7 %collective-permute-start.28 = (bf16[24,16,1024]{2,1,0:T(8,128)(2,1)S(1)}, bf16[24,16,1024]{2,1,0:T(8,128)(2,1)S(1)}, u32[]{:S(2)}, u32[]{:S(2)}) collective-permute-start(bf16[24,16,1024]{2,1,0:T(8,128)(2,1)S(1)} %collective-permute-done.26.refs_2_), channel_id=1, source_target_pairs={{0,2},{2,4},{4,6},{6,7},{7,5},{5,3},{3,1},{1,0},{8,10},{10,12},{12... | collective-permute-start | bytes 2359304 | tf_op jit(solution)/shard_map/ppermute | solution.py:598
  171.9 29.7 %collective-permute-start.29 = (bf16[24,16,1024]{2,1,0:T(8,128)(2,1)S(1)}, bf16[24,16,1024]{2,1,0:T(8,128)(2,1)S(1)}, u32[]{:S(2)}, u32[]{:S(2)}) collective-permute-start(bf16[24,16,1024]{2,1,0:T(8,128)(2,1)S(1)} %collective-permute-done.27.refs_6_), channel_id=1, source_target_pairs={{2,0},{4,2},{6,4},{7,6},{5,7},{3,5},{1,3},{0,1},{10,8},{12,10},{14... | collective-permute-start | bytes 2359304 | tf_op jit(solution)/shard_map/ppermute | solution.py:598
  184.7 20.7 %collective-permute-start.17 = (bf16[8,16,1024]{2,1,0:T(8,128)(2,1)S(1)}, bf16[8,16,1024]{2,1,0:T(8,128)(2,1)S(1)}, u32[]{:S(2)}, u32[]{:S(2)}) collective-permute-start(bf16[8,16,1024]{2,1,0:T(8,128)(2,1)S(1)} %slice.124), channel_id=1, source_target_pairs={{0,2},{2,4},{4,6},{6,7},{7,5},{5,3},{3,1},{1,0},{8,10},{10,12},{12... | collective-permute-start | bytes 786440 | tf_op jit(solution)/shard_map/ppermute | solution.py:598
  186.4 20.8 %collective-permute-start.18 = (bf16[8,16,1024]{2,1,0:T(8,128)(2,1)S(1)}, bf16[8,16,1024]{2,1,0:T(8,128)(2,1)S(1)}, u32[]{:S(2)}, u32[]{:S(2)}) collective-permute-start(bf16[8,16,1024]{2,1,0:T(8,128)(2,1)S(1)} %slice.125), channel_id=1, source_target_pairs={{2,0},{4,2},{6,4},{7,6},{5,7},{3,5},{1,3},{0,1},{10,8},{12,10},{14... | collective-permute-start | bytes 786440 | tf_op jit(solution)/shard_map/ppermute | solution.py:598
  213.8 20.5 %collective-permute-start.19 = (bf16[24,16,1024]{2,1,0:T(8,128)(2,1)S(1)}, bf16[24,16,1024]{2,1,0:T(8,128)(2,1)S(1)}, u32[]{:S(2)}, u32[]{:S(2)}) collective-permute-start(bf16[24,16,1024]{2,1,0:T(8,128)(2,1)S(1)} %bitcast.82), channel_id=1, source_target_pairs={{0,2},{2,4},{4,6},{6,7},{7,5},{5,3},{3,1},{1,0},{8,10},{10,12},{12... | collective-permute-start | bytes 2359304 | tf_op jit(solution)/shard_map/ppermute | solution.py:598
  215.4 20.5 %collective-permute-start.20 = (bf16[24,16,1024]{2,1,0:T(8,128)(2,1)S(1)}, bf16[24,16,1024]{2,1,0:T(8,128)(2,1)S(1)}, u32[]{:S(2)}, u32[]{:S(2)}) collective-permute-start(bf16[24,16,1024]{2,1,0:T(8,128)(2,1)S(1)} %bitcast.83), channel_id=1, source_target_pairs={{2,0},{4,2},{6,4},{7,6},{5,7},{3,5},{1,3},{0,1},{10,8},{12,10},{14... | collective-permute-start | bytes 2359304 | tf_op jit(solution)/shard_map/ppermute | solution.py:598
  215.8 35.3 %collective-permute-start.37 = (bf16[24,16,1024]{2,1,0:T(8,128)(2,1)S(1)}, bf16[24,16,1024]{2,1,0:T(8,128)(2,1)S(1)}, u32[]{:S(2)}, u32[]{:S(2)}) collective-permute-start(bf16[24,16,1024]{2,1,0:T(8,128)(2,1)S(1)} %bitcast.74), channel_id=1, source_target_pairs={{0,2},{2,4},{4,6},{6,7},{7,5},{5,3},{3,1},{1,0},{8,10},{10,12},{12... | collective-permute-start | bytes 2359304 | tf_op jit(solution)/shard_map/ppermute | solution.py:598
  217.4 35.3 %collective-permute-start.38 = (bf16[24,16,1024]{2,1,0:T(8,128)(2,1)S(1)}, bf16[24,16,1024]{2,1,0:T(8,128)(2,1)S(1)}, u32[]{:S(2)}, u32[]{:S(2)}) collective-permute-start(bf16[24,16,1024]{2,1,0:T(8,128)(2,1)S(1)} %bitcast.75), channel_id=1, source_target_pairs={{2,0},{4,2},{6,4},{7,6},{5,7},{3,5},{1,3},{0,1},{10,8},{12,10},{14... | collective-permute-start | bytes 2359304 | tf_op jit(solution)/shard_map/ppermute | solution.py:598
  235.8 32.1 %collective-permute-start.31 = (bf16[24,16,1024]{2,1,0:T(8,128)(2,1)S(1)}, bf16[24,16,1024]{2,1,0:T(8,128)(2,1)S(1)}, u32[]{:S(2)}, u32[]{:S(2)}) collective-permute-start(bf16[24,16,1024]{2,1,0:T(8,128)(2,1)S(1)} %collective-permute-done.19.refs_1_), channel_id=1, source_target_pairs={{0,2},{2,4},{4,6},{6,7},{7,5},{5,3},{3,1},{1,0},{8,10},{10,12},{12... | collective-permute-start | bytes 2359304 | tf_op jit(solution)/shard_map/ppermute | solution.py:598
  237.4 32.1 %collective-permute-start.32 = (bf16[24,16,1024]{2,1,0:T(8,128)(2,1)S(1)}, bf16[24,16,1024]{2,1,0:T(8,128)(2,1)S(1)}, u32[]{:S(2)}, u32[]{:S(2)}) collective-permute-start(bf16[24,16,1024]{2,1,0:T(8,128)(2,1)S(1)} %collective-permute-done.20.refs_7_), channel_id=1, source_target_pairs={{2,0},{4,2},{6,4},{7,6},{5,7},{3,5},{1,3},{0,1},{10,8},{12,10},{14... | collective-permute-start | bytes 2359304 | tf_op jit(solution)/shard_map/ppermute | solution.py:598
  252.7 32.1 %collective-permute-start.39 = (bf16[24,16,1024]{2,1,0:T(8,128)(2,1)S(1)}, bf16[24,16,1024]{2,1,0:T(8,128)(2,1)S(1)}, u32[]{:S(2)}, u32[]{:S(2)}) collective-permute-start(bf16[24,16,1024]{2,1,0:T(8,128)(2,1)S(1)} %collective-permute-done.37.refs_1_), channel_id=1, source_target_pairs={{0,2},{2,4},{4,6},{6,7},{7,5},{5,3},{3,1},{1,0},{8,10},{10,12},{12... | collective-permute-start | bytes 2359304 | tf_op jit(solution)/shard_map/ppermute | solution.py:598
  254.3 32.1 %collective-permute-start.40 = (bf16[24,16,1024]{2,1,0:T(8,128)(2,1)S(1)}, bf16[24,16,1024]{2,1,0:T(8,128)(2,1)S(1)}, u32[]{:S(2)}, u32[]{:S(2)}) collective-permute-start(bf16[24,16,1024]{2,1,0:T(8,128)(2,1)S(1)} %collective-permute-done.38.refs_7_), channel_id=1, source_target_pairs={{2,0},{4,2},{6,4},{7,6},{5,7},{3,5},{1,3},{0,1},{10,8},{12,10},{14... | collective-permute-start | bytes 2359304 | tf_op jit(solution)/shard_map/ppermute | solution.py:598
  269.5 32.1 %collective-permute-start.33 = (bf16[24,16,1024]{2,1,0:T(8,128)(2,1)S(1)}, bf16[24,16,1024]{2,1,0:T(8,128)(2,1)S(1)}, u32[]{:S(2)}, u32[]{:S(2)}) collective-permute-start(bf16[24,16,1024]{2,1,0:T(8,128)(2,1)S(1)} %collective-permute-done.31.refs_2_), channel_id=1, source_target_pairs={{0,2},{2,4},{4,6},{6,7},{7,5},{5,3},{3,1},{1,0},{8,10},{10,12},{12... | collective-permute-start | bytes 2359304 | tf_op jit(solution)/shard_map/ppermute | solution.py:598
  271.1 32.1 %collective-permute-start.34 = (bf16[24,16,1024]{2,1,0:T(8,128)(2,1)S(1)}, bf16[24,16,1024]{2,1,0:T(8,128)(2,1)S(1)}, u32[]{:S(2)}, u32[]{:S(2)}) collective-permute-start(bf16[24,16,1024]{2,1,0:T(8,128)(2,1)S(1)} %collective-permute-done.32.refs_6_), channel_id=1, source_target_pairs={{2,0},{4,2},{6,4},{7,6},{5,7},{3,5},{1,3},{0,1},{10,8},{12,10},{14... | collective-permute-start | bytes 2359304 | tf_op jit(solution)/shard_map/ppermute | solution.py:598
  286.4 32.1 %collective-permute-start.46 = (bf16[24,16,1024]{2,1,0:T(8,128)(2,1)S(1)}, bf16[24,16,1024]{2,1,0:T(8,128)(2,1)S(1)}, u32[]{:S(2)}, u32[]{:S(2)}) collective-permute-start(bf16[24,16,1024]{2,1,0:T(8,128)(2,1)S(1)} %collective-permute-done.39.refs_2_), channel_id=1, source_target_pairs={{0,2},{2,4},{4,6},{6,7},{7,5},{5,3},{3,1},{1,0},{8,10},{10,12},{12... | collective-permute-start | bytes 2359304 | tf_op jit(solution)/shard_map/ppermute | solution.py:598
  288.0 32.1 %collective-permute-start.47 = (bf16[24,16,1024]{2,1,0:T(8,128)(2,1)S(1)}, bf16[24,16,1024]{2,1,0:T(8,128)(2,1)S(1)}, u32[]{:S(2)}, u32[]{:S(2)}) collective-permute-start(bf16[24,16,1024]{2,1,0:T(8,128)(2,1)S(1)} %collective-permute-done.40.refs_6_), channel_id=1, source_target_pairs={{2,0},{4,2},{6,4},{7,6},{5,7},{3,5},{1,3},{0,1},{10,8},{12,10},{14... | collective-permute-start | bytes 2359304 | tf_op jit(solution)/shard_map/ppermute | solution.py:598
  303.3 23.7 %collective-permute-start.35 = (bf16[12,16,1024]{2,1,0:T(8,128)(2,1)S(1)}, bf16[12,16,1024]{2,1,0:T(8,128)(2,1)S(1)}, u32[]{:S(2)}, u32[]{:S(2)}) collective-permute-start(bf16[12,16,1024]{2,1,0:T(8,128)(2,1)S(1)} %slice.131), channel_id=1, source_target_pairs={{0,2},{2,4},{4,6},{6,7},{7,5},{5,3},{3,1},{1,0},{8,10},{10,12},{12... | collective-permute-start | bytes 1179656 | tf_op jit(solution)/shard_map/ppermute | solution.py:598
  306.8 25.6 %collective-permute-start.41 = (bf16[12,16,1024]{2,1,0:T(8,128)(2,1)S(1)}, bf16[12,16,1024]{2,1,0:T(8,128)(2,1)S(1)}, u32[]{:S(2)}, u32[]{:S(2)}) collective-permute-start(bf16[12,16,1024]{2,1,0:T(8,128)(2,1)S(1)} %slice.137), channel_id=1, source_target_pairs={{2,0},{4,2},{6,4},{7,6},{5,7},{3,5},{1,3},{0,1},{10,8},{12,10},{14... | collective-permute-start | bytes 1179656 | tf_op jit(solution)/shard_map/ppermute | solution.py:598
  407.3 21.2 %all-to-all-start = ((bf16[4,8,64,128]{3,2,1,0:T(8,128)(2,1)}), bf16[4,8,64,128]{3,2,1,0:T(8,128)(2,1)S(1)}, u32[]{:S(2)}, u32[]{:S(2)}) async-start(bf16[4,8,64,128]{3,2,1,0:T(8,128)(2,1)} %bitcast.109), calls=%async_computation | async-start | bytes 1048576 | tf_op jit(solution)/shard_map/all_to_all | solution.py:568
  (84 other events, 1992.3 us)
